TPU v7x, 128 devices: a whole 4x4x4 slice. The times are simulated.
128 devices in a mesh: seq: 32 (over y, x, core), ffn: 4 (over z).
Axes of the slice: x: 4, y: 4, z: 4, core: 2. Of those that a mesh axis runs over, the one named last changes fastest.
Arguments:
- stream_one: bfloat16 [4, 8192, 1024], P('ffn', 'seq'), may hold values from -6 to 6
- stream_two: bfloat16 [4, 8192, 1024], P('ffn', 'seq'), may hold values from -6 to 6
- doc_lengths: int32 [4, 9], P('ffn'), may hold values from 0 to 8192, as said below
- bucket_ids: int32 [4, 32, 8192], P('ffn', 'seq'), may hold values from 0 to 127
- norm1_gain: float32 [1024], replicated, may hold values from 0.5 to 1.5
- norm1_bias: float32 [1024], replicated, may hold values from -1.8 to 1.8
- w_qk: bfloat16 [1024, 1024], replicated, may hold values from -4 to 4
- w_value: bfloat16 [1024, 1024], replicated, may hold values from -0.1875 to 0.1875
- w_out: bfloat16 [1024, 1024], replicated, may hold values from -1.5 to 1.5
- norm2_gain: float32 [1024], replicated, may hold values from 0.5 to 1.5
- norm2_bias: float32 [1024], replicated, may hold values from -1.8 to 1.8
- w_up: bfloat16 [1024, 4096], P(None, 'ffn'), may hold values from -0.1875 to 0.1875
- w_down: bfloat16 [1024, 4096], P(None, 'ffn'), may hold values from -0.09375 to 0.09375
- grad_out_one: bfloat16 [4, 8192, 1024], P('ffn', 'seq'), may hold values from -6 to 6
- grad_out_two: bfloat16 [4, 8192, 1024], P('ffn', 'seq'), may hold values from -6 to 6
Outputs:
- output_one: bfloat16 [4, 8192, 1024], P('ffn', 'seq')
- output_two: bfloat16 [4, 8192, 1024], P('ffn', 'seq')
- grad_stream_one: float32 [4, 8192, 1024], P('ffn', 'seq')
- grad_stream_two: float32 [4, 8192, 1024], P('ffn', 'seq')
- grad_norm1_gain: float32 [1024], P(('seq', 'ffn'))
- grad_norm1_bias: float32 [1024], P(('seq', 'ffn'))
- grad_w_qk: float32 [1024, 1024], P(('seq', 'ffn'))
- grad_w_value: float32 [1024, 1024], P(('seq', 'ffn'))
- grad_w_out: float32 [1024, 1024], P(('seq', 'ffn'))
- grad_norm2_gain: float32 [1024], P(('seq', 'ffn'))
- grad_norm2_bias: float32 [1024], P(('seq', 'ffn'))
- grad_w_up: float32 [1024, 4096], P('seq', 'ffn')
- grad_w_down: float32 [1024, 4096], P('seq', 'ffn')
Inputs may be any that keep to these rules, and one draw needn't show every extreme that they name: `doc_lengths`: each sequence's lengths sum to 8192; its fifth document starts before position 256 and ends after position 7936; the others may be empty.
All inputs are finite; a program needn't handle non-finite values.
Results may differ from a plain program's by a relative error of at most 0.017.
Values may be sent and summed in bfloat16 or wider, within the bound.
No kernel may reach another device: no remote copies, remote signals or barrier semaphores. Data moves between devices by JAX's collectives and lax.ppermute only.
A program may use at most 192 MiB of HBM per device.

v0:
```python
import jax
import jax.numpy as jnp
from jax import lax
from jax.sharding import PartitionSpec as P

HEADS = 8
DH = 128
ROUNDS = 4
SPAN = 64


EPS_NORM = 1e-05
EPS_KEY = 1e-06
SELF_PENALTY = 1000.0
MASKED = -1000000000.0


def cut_along(array, dim, peers):
    dims = array.shape
    tiles = array.reshape(*dims[:dim], peers, dims[dim] // peers, *dims[dim + 1 :])
    return jnp.moveaxis(tiles, dim, 0)


def sent_and_summed(array, axis, dim):
    tiles = cut_along(array, dim, lax.axis_size(axis))
    arrived = lax.all_to_all(tiles, axis, split_axis=0, concat_axis=0, tiled=True)
    return arrived.astype(jnp.float32).sum(axis=0)


def piece_ends(length, count):
    unit = 8 if length >= 8 * count else 1
    return [length // unit * k // count * unit for k in range(1, count)]


def in_order(tiles, dim):
    tiles = jnp.moveaxis(tiles, 0, dim)
    dims = tiles.shape
    return tiles.reshape(*dims[:dim], dims[dim] * dims[dim + 1], *dims[dim + 2 :])


def exchange_in_pieces(array, axis, pieces, split_dim, concat_dim):
    tiles = cut_along(array, split_dim, lax.axis_size(axis))
    split_at = max(range(1, max(2, tiles.ndim - 1)), key=lambda d: tiles.shape[d])
    done = []
    for section in jnp.split(tiles, piece_ends(tiles.shape[split_at], pieces), axis=split_at):
        if section.size:
            done.append(lax.all_to_all(section, axis, split_axis=0, concat_axis=0, tiled=True))
    return in_order(jnp.concatenate(done, axis=split_at), concat_dim)


def one_scatter(arrays, axis, dims):
    peers = lax.axis_size(axis)
    tiles = [cut_along(a, dim, peers) for a, dim in zip(arrays, dims)]
    lines = jnp.concatenate([b.reshape(peers, -1) for b in tiles], axis=1)
    extent = max(16, -(-lines.shape[1] // 1024) * 8)
    lines = jnp.pad(lines, ((0, 0), (0, extent * 128 - lines.shape[1]))).reshape(-1, 128)
    flat, at, done = (lax.psum_scatter(lines, axis, tiled=True).reshape(-1), 0, [])
    for b in tiles:
        part = b[0]
        done.append(flat[at : at + part.size].reshape(part.shape))
        at += part.size
    return tuple(done)


def layer_norm(values, gain, offset):
    centre = jnp.mean(values, axis=-1, keepdims=True)
    centred = values - centre
    spread = jnp.mean(centred * centred, axis=-1, keepdims=True)
    return centred * lax.rsqrt(spread + EPS_NORM) * gain + offset


def gelu_exact(values):
    return jax.nn.gelu(values, approximate=False)


def unit_rows(queries_full):
    return queries_full * lax.rsqrt(
        jnp.sum(queries_full * queries_full, axis=-1, keepdims=True) + EPS_KEY
    )


def combine(per_round, round_logs):
    round_weight = jax.nn.softmax(round_logs, axis=1)
    return jnp.sum(round_weight[..., None] * per_round, axis=1)


def segment_ids(lengths_row, length):
    ends = jnp.cumsum(lengths_row, dtype=jnp.int32)
    places = jnp.arange(length, dtype=jnp.int32)
    return jnp.sum((places[:, None] >= ends[None, :]).astype(jnp.int32), axis=1, dtype=jnp.int32)


def span_view(array, blocks_per):
    spanned = array.reshape((-1, SPAN) + array.shape[1:])
    return spanned.reshape((-1, blocks_per) + spanned.shape[1:])


def key_view(array, blocks_per):
    spanned = array.reshape((-1, SPAN) + array.shape[1:])
    window = jnp.concatenate([jnp.roll(spanned, 1, 0), spanned], axis=1)
    return window.reshape((-1, blocks_per) + window.shape[1:])


def block_scores(queries, keys, query_pos, key_pos, query_seg, key_seg):
    raw_dots = jnp.einsum("cqd,ckd->cqk", queries, keys, preferred_element_type=jnp.float32)
    scores = raw_dots * DH ** (-0.5)
    self_mask = (query_pos[:, :, None] == key_pos[:, None, :]).astype(jnp.float32)
    scores = scores - SELF_PENALTY * self_mask
    allowed = (query_seg[:, :, None] == key_seg[:, None, :]) & (
        key_pos[:, None, :] <= query_pos[:, :, None]
    )
    return jnp.where(allowed, scores, MASKED)


def attend(packed, bucket_row, segment):
    length = packed.shape[0]
    span_count = length // SPAN
    blocks_per = min(span_count, max(1, 512 // SPAN))
    places = jnp.arange(length, dtype=jnp.int32)
    order = jnp.argsort(bucket_row * length + places)
    backward_index = jnp.zeros((length,), jnp.int32).at[order].set(places)
    sorted_rows = packed[order]
    queries = sorted_rows[:, :DH]
    key_values = sorted_rows[:, DH:]
    unit_keys = unit_rows(queries.astype(jnp.float32)).astype(jnp.bfloat16)
    sorted_seg = segment[order]
    pieces = (
        span_view(queries, blocks_per),
        key_view(unit_keys, blocks_per),
        key_view(key_values, blocks_per),
        span_view(order, blocks_per),
        key_view(order, blocks_per),
        span_view(sorted_seg, blocks_per),
        key_view(sorted_seg, blocks_per),
    )

    def block_forward(block_in):
        scores = block_scores(
            block_in[0], block_in[1], block_in[3], block_in[4], block_in[5], block_in[6]
        )
        row_max = jnp.max(scores, axis=-1, keepdims=True)
        totals = jnp.log(jnp.sum(jnp.exp(scores - row_max), axis=-1, keepdims=True)) + row_max
        probabilities = jnp.exp(scores - totals).astype(jnp.bfloat16)
        outcome = jnp.einsum(
            "cqk,ckd->cqd", probabilities, block_in[2], preferred_element_type=jnp.float32
        )
        return (outcome, totals[..., 0])

    outcome, key_totals = lax.map(block_forward, pieces)
    outcome = outcome.reshape(length, DH)
    key_totals = key_totals.reshape(length)
    return (
        outcome[backward_index].astype(jnp.bfloat16),
        key_totals[backward_index],
        sorted_rows,
        order,
        backward_index,
        unit_keys,
        key_totals,
    )


def attend_back(
    sorted_rows, order, backward_index, unit_keys, key_totals, segment, grad_outcome, grad_totals
):
    length = sorted_rows.shape[0]
    span_count = length // SPAN
    blocks_per = min(span_count, max(1, 512 // SPAN))
    queries = sorted_rows[:, :DH]
    key_values = sorted_rows[:, DH:]
    sorted_seg = segment[order]
    pieces = (
        span_view(queries, blocks_per),
        key_view(unit_keys, blocks_per),
        key_view(key_values, blocks_per),
        span_view(order, blocks_per),
        key_view(order, blocks_per),
        span_view(sorted_seg, blocks_per),
        key_view(sorted_seg, blocks_per),
        span_view(key_totals, blocks_per),
        span_view(grad_outcome[order], blocks_per),
        span_view(grad_totals[order], blocks_per),
    )

    def block_backward(block_in):
        scores = block_scores(
            block_in[0], block_in[1], block_in[3], block_in[4], block_in[5], block_in[6]
        )
        probabilities = jnp.exp(scores - block_in[7][..., None])
        low_probs = probabilities.astype(jnp.bfloat16)
        grad_probs = jnp.einsum(
            "cqd,ckd->cqk", block_in[8], block_in[2], preferred_element_type=jnp.float32
        )
        inner_sum = jnp.sum(probabilities * grad_probs, axis=-1, keepdims=True)
        grad_scores = probabilities * (grad_probs - inner_sum + block_in[9][..., None])
        grad_dots = (grad_scores * DH ** (-0.5)).astype(jnp.bfloat16)
        grad_queries = jnp.einsum(
            "cqk,ckd->cqd", grad_dots, block_in[1], preferred_element_type=jnp.float32
        )
        grad_keys = jnp.einsum(
            "cqk,cqd->ckd", grad_dots, block_in[0], preferred_element_type=jnp.float32
        )
        grad_values = jnp.einsum(
            "cqk,cqd->ckd", low_probs, block_in[8], preferred_element_type=jnp.float32
        )
        return (grad_queries, grad_keys, grad_values)

    grad_queries, grad_keys, grad_values = lax.map(block_backward, pieces)

    def fold_window(window):
        window = window.reshape(span_count, 2 * SPAN, DH)
        return (window[:, SPAN:] + jnp.roll(window[:, :SPAN], -1, 0)).reshape(length, DH)

    grad_unit = fold_window(grad_keys)
    grad_values = fold_window(grad_values)
    pullback = jax.vjp(unit_rows, queries.astype(jnp.float32))[1]
    grad_queries = grad_queries.reshape(length, DH) + pullback(grad_unit)[0]
    both_grads = jnp.concatenate([grad_queries, grad_values], axis=1)
    return both_grads[backward_index].astype(jnp.bfloat16)


def shards(
    stream_one,
    stream_two,
    doc_lengths,
    bucket_ids,
    norm1_gain,
    norm1_bias,
    w_qk,
    w_value,
    w_out,
    norm2_gain,
    norm2_bias,
    w_up,
    w_down,
    grad_out_one,
    grad_out_two,
):
    shard_rows = stream_one.shape[1]
    model_width = stream_one.shape[2]
    groups = HEADS * ROUNDS
    length = shard_rows * lax.axis_size("seq")
    input_one = stream_one[0].astype(jnp.float32)
    input_two = stream_two[0].astype(jnp.float32)
    segment = segment_ids(doc_lengths[0], length)
    normed_one = layer_norm(input_two, norm1_gain, norm1_bias).astype(jnp.bfloat16)
    shared_qk = jnp.dot(normed_one, w_qk, preferred_element_type=jnp.float32).astype(jnp.bfloat16)
    value_rows = jnp.dot(normed_one, w_value, preferred_element_type=jnp.float32).astype(
        jnp.bfloat16
    )
    joined = jnp.concatenate(
        [shared_qk.reshape(shard_rows, HEADS, DH), value_rows.reshape(shard_rows, HEADS, DH)],
        axis=2,
    )
    copies = jnp.broadcast_to(
        joined.transpose(1, 0, 2)[:, None], (HEADS, ROUNDS, shard_rows, 2 * DH)
    )
    copies = copies.reshape(groups, shard_rows, 2 * DH)
    received = lax.all_to_all(copies, "seq", split_axis=0, concat_axis=1, tiled=True)

    def attend_item(pieces):
        return attend(pieces[0], pieces[1], segment)

    attended, totals, sorted_rows, orders, backward_index, unit_keys, key_totals = lax.map(
        attend_item, (received, bucket_ids[0])
    )
    round_values = lax.all_to_all(attended, "seq", split_axis=1, concat_axis=0, tiled=True)
    round_totals = lax.all_to_all(totals, "seq", split_axis=1, concat_axis=0, tiled=True)
    per_round = round_values.reshape(HEADS, ROUNDS, shard_rows, DH).astype(jnp.float32)
    round_logs = round_totals.reshape(HEADS, ROUNDS, shard_rows)
    mixture = combine(per_round, round_logs)
    mixture_rows = mixture.transpose(1, 0, 2).reshape(shard_rows, model_width).astype(jnp.bfloat16)
    sum_one = input_one + jnp.dot(mixture_rows, w_out, preferred_element_type=jnp.float32)
    normed_two = layer_norm(sum_one, norm2_gain, norm2_bias).astype(jnp.bfloat16)
    gathered = lax.all_gather(normed_two, "ffn", axis=0, tiled=True)
    pre_act = jnp.dot(gathered, w_up, preferred_element_type=jnp.float32)
    hidden = gelu_exact(pre_act).astype(jnp.bfloat16)
    piece = hidden
    sum_two = input_two + sent_and_summed(
        lax.dot_general(
            piece, w_down, (((1,), (1,)), ((), ())), preferred_element_type=jnp.float32
        ).astype(jnp.bfloat16),
        "ffn",
        0,
    )
    grad_one_in = grad_out_one[0].astype(jnp.float32)
    grad_two_in = grad_out_two[0].astype(jnp.float32)
    grad_branch_two = grad_two_in.astype(jnp.bfloat16)
    grad_rows = lax.all_gather(grad_branch_two, "ffn", axis=0, tiled=True)
    rows_again, pre_again, hidden_again = (gathered, pre_act, hidden)
    grad_hidden = jnp.dot(grad_rows, w_down, preferred_element_type=jnp.float32)
    grad_pre = jax.vjp(gelu_exact, pre_again)[1](grad_hidden)[0].astype(jnp.bfloat16)
    grad_down_part = lax.dot_general(
        grad_rows, hidden_again, (((0,), (0,)), ((), ())), preferred_element_type=jnp.float32
    )
    grad_up_part = lax.dot_general(
        rows_again, grad_pre, (((0,), (0,)), ((), ())), preferred_element_type=jnp.float32
    )
    piece = grad_pre
    grad_normed_two = sent_and_summed(
        lax.dot_general(
            piece, w_up, (((1,), (1,)), ((), ())), preferred_element_type=jnp.float32
        ).astype(jnp.bfloat16),
        "ffn",
        0,
    )
    pullback_two = jax.vjp(layer_norm, sum_one, norm2_gain, norm2_bias)[1]
    grad_from_ffn, grad_gain_two, grad_bias_two = pullback_two(grad_normed_two)
    grad_first = grad_one_in + grad_from_ffn
    grad_branch_one = grad_first.astype(jnp.bfloat16)
    grad_proj_out = lax.dot_general(
        mixture_rows, grad_branch_one, (((0,), (0,)), ((), ())), preferred_element_type=jnp.float32
    )
    grad_mixture = lax.dot_general(
        grad_branch_one, w_out, (((1,), (1,)), ((), ())), preferred_element_type=jnp.float32
    )
    grad_mixture = grad_mixture.reshape(shard_rows, HEADS, DH).transpose(1, 0, 2)
    grad_round, grad_logs = jax.vjp(combine, per_round, round_logs)[1](grad_mixture)
    grad_round = grad_round.astype(jnp.bfloat16).reshape(groups, shard_rows, DH)
    grad_logs = grad_logs.reshape(groups, shard_rows)
    far_grads = lax.all_to_all(grad_round, "seq", split_axis=0, concat_axis=1, tiled=True)
    far_totals = lax.all_to_all(
        grad_logs.astype(jnp.bfloat16), "seq", split_axis=0, concat_axis=1, tiled=True
    ).astype(grad_logs.dtype)

    def back_item(pieces):
        return attend_back(
            pieces[0], pieces[1], pieces[2], pieces[3], pieces[4], segment, pieces[5], pieces[6]
        )

    item_grads = lax.map(
        back_item,
        (sorted_rows, orders, backward_index, unit_keys, key_totals, far_grads, far_totals),
    )
    owner_grads = exchange_in_pieces(item_grads, "seq", 2, 1, 0)
    round_sums = jnp.sum(
        owner_grads.reshape(HEADS, ROUNDS, shard_rows, 2 * DH).astype(jnp.float32), axis=1
    )
    grad_qk = (
        round_sums[:, :, :DH]
        .transpose(1, 0, 2)
        .reshape(shard_rows, model_width)
        .astype(jnp.bfloat16)
    )
    grad_values = (
        round_sums[:, :, DH:]
        .transpose(1, 0, 2)
        .reshape(shard_rows, model_width)
        .astype(jnp.bfloat16)
    )
    grad_proj_qk = lax.dot_general(
        normed_one, grad_qk, (((0,), (0,)), ((), ())), preferred_element_type=jnp.float32
    )
    grad_proj_value = lax.dot_general(
        normed_one, grad_values, (((0,), (0,)), ((), ())), preferred_element_type=jnp.float32
    )
    grad_normed_one = lax.dot_general(
        grad_qk, w_qk, (((1,), (1,)), ((), ())), preferred_element_type=jnp.float32
    )
    grad_normed_one = grad_normed_one + lax.dot_general(
        grad_values, w_value, (((1,), (1,)), ((), ())), preferred_element_type=jnp.float32
    )
    pullback_one = jax.vjp(layer_norm, input_two, norm1_gain, norm1_bias)[1]
    grad_from_attn, grad_gain_one, grad_bias_one = pullback_one(grad_normed_one)
    grad_second = grad_two_in + grad_from_attn
    shared = one_scatter(
        (
            grad_gain_one,
            grad_bias_one,
            grad_proj_qk,
            grad_proj_value,
            grad_proj_out,
            grad_gain_two,
            grad_bias_two,
        ),
        ("seq", "ffn"),
        (0, 0, 0, 0, 0, 0, 0),
    )
    ffn_sums = (
        lax.psum_scatter(
            grad_up_part.astype(jnp.bfloat16), "seq", scatter_dimension=0, tiled=True
        ).astype(jnp.float32),
        lax.psum_scatter(
            grad_down_part.astype(jnp.bfloat16), "seq", scatter_dimension=0, tiled=True
        ).astype(jnp.float32),
    )
    return (
        sum_one.astype(jnp.bfloat16)[None],
        sum_two.astype(jnp.bfloat16)[None],
        grad_first[None],
        grad_second[None],
        shared[0],
        shared[1],
        shared[2],
        shared[3],
        shared[4],
        shared[5],
        shared[6],
        ffn_sums[0],
        ffn_sums[1],
    )


def solution(mesh):
    return jax.shard_map(
        shards,
        mesh=mesh,
        in_specs=(
            P("ffn", "seq", None),
            P("ffn", "seq", None),
            P("ffn", None),
            P("ffn", "seq", None),
            P(),
            P(),
            P(),
            P(),
            P(),
            P(),
            P(),
            P(None, "ffn"),
            P(None, "ffn"),
            P("ffn", "seq", None),
            P("ffn", "seq", None),
        ),
        out_specs=(
            P("ffn", "seq", None),
            P("ffn", "seq", None),
            P("ffn", "seq", None),
            P("ffn", "seq", None),
            P(("seq", "ffn")),
            P(("seq", "ffn")),
            P(("seq", "ffn"), None),
            P(("seq", "ffn"), None),
            P(("seq", "ffn"), None),
            P(("seq", "ffn")),
            P(("seq", "ffn")),
            P("seq", "ffn"),
            P("seq", "ffn"),
        ),
        check_vma=False,
    )
```

profile of v0, /device:TPU:1, one launch (start us, length us, event | category | flops | bytes accessed | tf_op | source)
XLA Modules:
  0.0 1817.8 jit_solution(9560343211753411256)
XLA Ops:
  16.9 8.8 all-to-all-start
  26.0 6.8 sort.19
  33.1 45.5 %gather_fusion = s32[8192]{0:T(1024)S(1)} fusion(s32[8192]{0:T(1024)S(1)} %convert_reduce_fusion.5, s32[8192]{0:T(1024)S(1)} %get-tuple-element.353), kind=kCustom, calls=%fused_computation | custom fusion | bytes 98304 | tf_op jit(solution)/shard_map/while/body/eval_jaxpr/gather | solution.py:126
  78.8 30.7 %scatter_custom_fusion = s32[8192]{0:T(1024)S(1)} fusion(s32[8192]{0:T(1024)S(1)} %get-tuple-element.352, s32[8192]{0:T(1024)S(1)} %iota.17, s32[]{:T(128)} %copy.89), kind=kCustom, calls=%fused_computation.210 | custom fusion | bytes 32772 | tf_op jit(solution)/shard_map/while/body/eval_jaxpr/scatter | solution.py:121
  111.7 33.6 %gather_fusion.1 = bf16[8192,256]{1,0:T(8,128)(2,1)} fusion(bf16[8192,256]{1,0:T(8,128)(2,1)} %bitcast.33, s32[8192]{0:T(1024)S(1)} %get-tuple-element.353), kind=kCustom, calls=%fused_computation.1 | custom fusion | bytes 8421376 | tf_op jit(solution)/shard_map/while/body/eval_jaxpr/gather | solution.py:122
  146.1 2.9 fusion.60
  150.8 3.5 fusion.61
  158.8 3.6 pad_maximum_fusion.1
  162.4 57.4 %while.51 = (s32[]{:T(128)}, bf16[16,8,64,128]{3,2,1,0:T(8,128)(2,1)}, f32[16,8,64]{2,1,0:T(8,128)S(1)}, s32[16,8,64]{2,1,0:T(8,128)S(1)}, s32[16,8,128]{2,1,0:T...) while((s32[]{:T(128)}, ...), condition=%wide.region_9.10_spmd.clone, body=%wide.region_6.9_spmd.sunk.clone | while | flops 34405888 | bytes 1767545 | solution.py:149
  220.5 80.6 %gather_fusion.2 = f32[8192]{0:T(1024)} fusion(f32[8192]{0:T(1024)S(1)} %reshape.645, s32[8192]{0:T(1024)S(1)} %fusion.102), kind=kCustom, calls=%fused_computation.2 | custom fusion | bytes 98304 | tf_op jit(solution)/shard_map/while/body/eval_jaxpr/gather | solution.py:154
  301.1 7.7 all-to-all-start.1
  308.8 29.8 %gather_fusion.3 = bf16[8192,128]{1,0:T(8,128)(2,1)} fusion(bf16[8192,128]{1,0:T(8,128)(2,1)} %bitcast.328, s32[8192]{0:T(1024)S(1)} %fusion.102), kind=kCustom, calls=%fused_computation.3 | custom fusion | bytes 4227072 | tf_op jit(solution)/shard_map/while/body/eval_jaxpr/gather | solution.py:153
  338.6 7.5 copy.61
  346.6 46.5 %reduce.6 = bf16[8192,128]{1,0:T(8,128)(2,1)} reduce(bf16[8192,1,128]{2,1,0:T(2,128)(2,1)} %bitcast.332, bf16[]{:T(256)} %broadcast.491), dimensions={1}, to_apply=%bitcast.262.reduce_sub_computation | reduce | bytes 4194306
  393.1 4.0 reshape.753
  397.1 7.4 all-to-all-start.2
  404.8 27.6 %all-to-all-done.2 = bf16[32,2,16384]{2,1,0:T(2,128)(2,1)} async-done(((bf16[32,2,16384]{2,1,0:T(2,128)(2,1)}), bf16[32,2,16384]{2,1,0:T(2,128)(2,1)}, u32[]{:S(2)}, u32[]{:S(2)}) %all-to-all-start.2) | async-done | bytes 2097184 | tf_op jit(solution)/shard_map/all_to_all | solution.py:267
  432.4 10.5 reshape.754
  442.9 7.0 bitcast_convert_fusion
  459.2 30.3 %all-gather.4.cloned.1.call-done = bf16[1024,1024]{1,0:T(8,128)(2,1)} async-done(((bf16[256,1024]{1,0:T(8,128)(2,1)}), bf16[1024,1024]{1,0:T(8,128)(2,1)}) %all-gather.4.cloned.1.call-update) | async-done | bytes 2097168 | tf_op jit(solution)/shard_map/all_gather | solution.py:275
  489.5 14.1 multiply_convert_fusion
  503.6 18.5 %all-gather.6.cloned.1.call-done = bf16[1,1024,1024]{2,1,0:T(8,128)(2,1)} async-done(((bf16[1,256,1024]{2,1,0:T(8,128)(2,1)}), bf16[1,1024,1024]{2,1,0:T(8,128)(2,1)}) %all-gather.6.cloned.1.call-update) | async-done | bytes 2097168 | tf_op jit(solution)/shard_map/all_gather | solution.py:289
  522.1 8.0 add_convert_fusion
  530.1 3.7 convolution_convert_fusion.1
  533.8 5.1 all-to-all-start.4
  542.1 22.6 %all-to-all-done.4 = bf16[4,256,1024]{2,1,0:T(8,128)(2,1)} async-done(((bf16[4,256,1024]{2,1,0:T(8,128)(2,1)}), bf16[4,256,1024]{2,1,0:T(8,128)(2,1)}, u32[]{:S(2)}, u32[]{:S(2)}) %all-to-all-start.4) | async-done | bytes 2097184 | tf_op jit(solution)/shard_map/all_to_all | solution.py:26
  574.3 61.0 %multiply_reduce_fusion.1 = f32[8192]{0:T(1024)S(1)} fusion(f32[1,8192,128]{2,0,1:T(1,128)S(1)} %bitcast.334, bf16[8192,1,128]{2,1,0:T(2,128)(2,1)S(1)} %copy-done.4), kind=kLoop, calls=%fused_computation.108 | loop fusion | flops 3137536 | bytes 6324224 | tf_op jit(solution)/shard_map/transpose(jvp())/reduce_sum | solution.py:84
  636.9 8.4 all-to-all-start.6
  647.6 4.6 all-to-all-done.6
  652.2 5.4 all-to-all-start.5
  657.7 45.5 %gather_fusion.5 = f32[8192]{0:T(1024)S(1)} fusion(f32[8192]{0:T(1024)S(1)} %bitcast.327, s32[8192]{0:T(1024)S(1)} %get-tuple-element.353), kind=kCustom, calls=%fused_computation.5 | custom fusion | bytes 98304 | tf_op jit(solution)/shard_map/while/body/eval_jaxpr/gather | solution.py:182
  703.3 29.8 %gather_fusion.4 = bf16[8192,128]{1,0:T(8,128)(2,1)} fusion(bf16[8192,128]{1,0:T(8,128)(2,1)} %bitcast.59, s32[8192]{0:T(1024)S(1)} %get-tuple-element.353), kind=kCustom, calls=%fused_computation.4 | custom fusion | bytes 4227072 | tf_op jit(solution)/shard_map/while/body/eval_jaxpr/gather | solution.py:181
  733.1 183.6 %while.52 = (s32[]{:T(128)}, f32[16,8,64,128]{3,2,1,0:T(8,128)}, f32[16,8,128,128]{3,2,1,0:T(8,128)}, f32[16,8,128,128]{3,2,1,0:T(8,128)}, s32[16,8,64]{2,1,0:T(...) while((s32[]{:T(128)}, f32[16,8,64,128]{3,2,1,0:T(8,128)}, ...), condition=%wide.region_24.25_spmd.clone, body=%wide.region_22.24_spmd.sunk.clone | while | flops 85329152 | bytes 5565593 | solution.py:208
  751.2 2.8 fusion.208
  762.8 2.8 fusion.208
  774.3 2.8 fusion.208
  797.2 2.8 fusion.208
  820.1 2.8 fusion.208
  843.1 2.8 fusion.208
  866.0 2.8 fusion.208
  877.5 2.8 fusion.208
  889.0 2.8 fusion.208
  911.9 2.8 fusion.208
  925.3 3.3 slice_add_fusion
  928.8 4.4 fusion.59
  935.6 33.6 %gather_fusion.6 = bf16[8192,256]{1,0:T(8,128)(2,1)} fusion(bf16[8192,256]{1,0:T(8,128)(2,1)} %pad_maximum_fusion, s32[8192]{0:T(1024)S(1)} %fusion.102), kind=kCustom, calls=%fused_computation.6 | custom fusion | bytes 8421376 | tf_op jit(solution)/shard_map/while/body/eval_jaxpr/gather | solution.py:219
  969.2 4.8 fusion.125
  974.0 7.5 all-to-all-start.7
  981.6 6.0 convert_bitcast_fusion
  987.5 4.0 copy.52
  991.5 17.9 all-to-all-done.7
  1009.4 6.9 all-to-all-start.8
  1016.4 6.0 convolution_convert_fusion
  1025.3 5.0 reshape_reshape.12
  1030.3 14.7 all-to-all-done.8
  1056.9 4.9 reshape_reshape.11
  1064.6 5.0 reshape_reshape.10
  1069.6 16.4 concatenate.111
  1086.0 10.9 pad.4
  1096.9 12.3 reshape.664
  1110.8 4.0 convolution_convert_fusion.2
  1114.8 26.9 %all_to_all.70 = bf16[4,256,1024]{2,1,0:T(8,128)(2,1)S(1)} all-to-all(bf16[4,256,1024]{2,1,0:T(8,128)(2,1)S(1)} %bitcast.360), channel_id=1, replica_groups=mesh['seq'=32,'ffn'=4] {'ffn'}, dimensions={0} | all-to-all | bytes 4194304 | tf_op jit(solution)/shard_map/all_to_all | solution.py:26
  1144.8 5.7 reduce-scatter.9.cloned.1.call-done
  1154.7 652.2 %reduce-scatter.13.cloned.1.call-done = f32[200,128]{1,0:T(8,128)} async-done(((f32[25600,128]{1,0:T(8,128)}), f32[200,128]{1,0:T(8,128)}) %reduce-scatter.13.cloned.1.call-update) | async-done | bytes 102416
  (440 shorter events, 300.5 us)
Async XLA Ops:
  7.2 482.3 %copy-start = (bf16[1024,1024]{1,0:T(8,128)(2,1)S(1)}, bf16[1024,1024]{1,0:T(8,128)(2,1)}, u32[]{:S(2)}) copy-start(bf16[1024,1024]{1,0:T(8,128)(2,1)} %param.30) | copy-start | bytes 6291460
  7.2 6.0 copy-start.5
  7.2 6.0 copy-start.23
  7.2 6.0 copy-start.34
  7.2 6.0 copy-start.14
  8.6 5.4 copy-start.25
  10.0 0.5 copy-start.38
  10.5 3.5 copy-start.30
  16.9 8.8 copy-start.43
  16.9 9.0 copy-start.28
  16.9 94.7 %all-to-all-start = ((bf16[32,256,256]{2,1,0:T(8,128)(2,1)}), bf16[32,256,256]{2,1,0:T(8,128)(2,1)}, u32[]{:S(2)}, u32[]{:S(2)}) async-start(bf16[32,256,256]{2,1,0:T(8,128)(2,1)} %bitcast.331), calls=%async_computation | async-start | bytes 8388608 | tf_op jit(solution)/shard_map/all_to_all | solution.py:259
  145.3 5.6 copy-start.2
  154.3 2.1 copy-start.7
  156.4 2.2 slice-start
  156.4 2.4 copy-start.8
  219.8 0.6 copy-start.17
  220.4 80.6 %copy-start.22 = (f32[16,8,64]{2,1,0:T(8,128)}, f32[16,8,64]{2,1,0:T(8,128)S(1)}, u32[]{:S(2)}) copy-start(f32[16,8,64]{2,1,0:T(8,128)S(1)} %get-tuple-element.642) | copy-start | bytes 98308
  301.1 96.0 %all-to-all-start.1 = ((f32[1,32,256]{2,0,1:T(1,128)}), f32[1,32,256]{2,0,1:T(1,128)S(1)}, u32[]{:S(2)}, u32[]{:S(2)}) async-start(f32[1,32,256]{2,0,1:T(1,128)} %bitcast.43), calls=%async_computation.1 | async-start | bytes 65536 | tf_op jit(solution)/shard_map/all_to_all | solution.py:268
  397.1 35.3 %all-to-all-start.2 = ((bf16[32,2,16384]{2,1,0:T(2,128)(2,1)}), bf16[32,2,16384]{2,1,0:T(2,128)(2,1)}, u32[]{:S(2)}, u32[]{:S(2)}) async-start(bf16[32,2,16384]{2,1,0:T(2,128)(2,1)} %reshape.753), calls=%async_computation.2 | async-start | bytes 4194304 | tf_op jit(solution)/shard_map/all_to_all | solution.py:267
  404.5 85.0 %all-gather.4.cloned.1.call-start = ((), (), s32[]{:S(2)}) async-start(), calls=%async_computation.12 | async-start | bytes 2621440 | tf_op jit(solution)/shard_map/all_gather | solution.py:275
  455.3 0.8 copy-start.32
  455.5 0.6 copy-start.40
  456.1 0.6 copy-start.36
  458.4 63.7 %all-gather.6.cloned.1.call-start = ((), (), s32[]{:S(2)}) async-start(), calls=%async_computation.14 | async-start | bytes 2621440 | tf_op jit(solution)/shard_map/all_gather | solution.py:289
  530.1 3.7 copy-start.44
  533.8 33.6 %copy-start.27 = (f32[1024]{0:T(1024)S(1)}, f32[1024]{0:T(1024)}, u32[]{:S(2)}) copy-start(f32[1024]{0:T(1024)} %param.28) | copy-start | bytes 12292
  533.8 33.6 %copy-start.33 = (f32[256]{0:T(256)S(1)}, f32[256]{0:T(256)}, u32[]{:S(2)}) copy-start(f32[256]{0:T(256)} %copy-done.32) | copy-start | bytes 3076
  533.8 33.6 %copy-start.37 = (f32[256]{0:T(256)S(1)}, f32[256]{0:T(256)}, u32[]{:S(2)}) copy-start(f32[256]{0:T(256)} %copy-done.36) | copy-start | bytes 3076
  533.8 34.0 %copy-start.41 = (f32[256]{0:T(256)S(1)}, f32[256]{0:T(256)}, u32[]{:S(2)}) copy-start(f32[256]{0:T(256)} %copy-done.40) | copy-start | bytes 3076
  533.8 30.9 %all-to-all-start.4 = ((bf16[4,256,1024]{2,1,0:T(8,128)(2,1)}), bf16[4,256,1024]{2,1,0:T(8,128)(2,1)}, u32[]{:S(2)}, u32[]{:S(2)}) async-start(bf16[4,256,1024]{2,1,0:T(8,128)(2,1)} %bitcast.359), calls=%async_computation.4 | async-start | bytes 4194304 | tf_op jit(solution)/shard_map/all_to_all | solution.py:26
  564.7 5.2 copy-start.16
  567.5 3.6 copy-start.11
  572.1 2.2 copy-start.4
  574.3 61.0 %copy-start.29 = (f32[8,256]{1,0:T(8,128)S(1)}, f32[8,256]{1,0:T(8,128)}, u32[]{:S(2)}) copy-start(f32[8,256]{1,0:T(8,128)} %multiply_divide_fusion) | copy-start | bytes 24580
  574.3 61.1 %copy-start.20 = (f32[32,1,256]{2,1,0:T(1,128)S(1)}, f32[32,1,256]{2,1,0:T(1,128)}, u32[]{:S(2)}) copy-start(f32[32,1,256]{2,1,0:T(1,128)} %sub.115) | copy-start | bytes 98308
  574.3 61.1 %copy-start.21 = (f32[32,1,256]{2,1,0:T(1,128)S(1)}, f32[32,1,256]{2,1,0:T(1,128)}, u32[]{:S(2)}) copy-start(f32[32,1,256]{2,1,0:T(1,128)} %div.103) | copy-start | bytes 98308
  574.3 71.0 %copy-start.18 = (f32[32,256]{1,0:T(8,128)S(1)}, f32[32,256]{1,0:T(8,128)}, u32[]{:S(2)}) copy-start(f32[32,256]{1,0:T(8,128)} %sub.113) | copy-start | bytes 98308
  574.3 71.0 %copy-start.19 = (f32[32,256]{1,0:T(8,128)S(1)}, f32[32,256]{1,0:T(8,128)}, u32[]{:S(2)}) copy-start(f32[32,256]{1,0:T(8,128)} %div.101) | copy-start | bytes 98308
  636.9 15.3 all-to-all-start.6
  652.2 51.1 %all-to-all-start.5 = ((bf16[32,256,128]{2,1,0:T(8,128)(2,1)}), bf16[32,256,128]{2,1,0:T(8,128)(2,1)}, u32[]{:S(2)}, u32[]{:S(2)}) async-start(bf16[32,256,128]{2,1,0:T(8,128)(2,1)} %fusion.63), calls=%async_computation.5 | async-start | bytes 4194304 | tf_op jit(solution)/shard_map/all_to_all | solution.py:321
  916.7 4.7 copy-start.10
  921.9 2.2 copy-start.3
  925.3 3.5 copy-start.13
  974.0 35.4 %all-to-all-start.7 = ((bf16[32,1,128,256]{3,2,1,0:T(8,128)(2,1)}), bf16[32,1,128,256]{3,2,1,0:T(8,128)(2,1)S(1)}, u32[]{:S(2)}, u32[]{:S(2)}) async-start(bf16[32,1,128,256]{3,2,1,0:T(8,128)(2,1)} %get-tuple-element.336), calls=%async_computation.7 | async-start | bytes 4194304 | tf_op jit(solution)/shard_map/all_to_all | solution.py:47
  981.5 161.5 %reduce-scatter.11.cloned.1.call-start = ((), (), s32[]{:S(2)}) async-start(), calls=%async_computation.15 | async-start | bytes 2162688
  1009.4 35.6 %all-to-all-start.8 = ((bf16[32,1,128,256]{3,2,1,0:T(8,128)(2,1)}), bf16[32,1,128,256]{3,2,1,0:T(8,128)(2,1)}, u32[]{:S(2)}, u32[]{:S(2)}) async-start(bf16[32,1,128,256]{3,2,1,0:T(8,128)(2,1)} %get-tuple-element.337), calls=%async_computation.8 | async-start | bytes 4194304 | tf_op jit(solution)/shard_map/all_to_all | solution.py:47
  1016.3 6.4 copy-start.12
  1016.3 134.2 %reduce-scatter.9.cloned.1.call-start = ((), (), s32[]{:S(2)}) async-start(), calls=%async_computation.13 | async-start | bytes 2162688 | tf_op jit(solution)/shard_map/reduce_scatter | solution.py:380
  1022.4 784.4 %reduce-scatter.13.cloned.1.call-start = ((), (), s32[]{:S(2)}) async-start(), calls=%async_computation.16 | async-start | bytes 13209600
  1047.6 3.1 copy-start.6
  1047.6 3.1 copy-start.24
  1047.6 3.1 copy-start.26
  1048.3 5.0 copy-start.39
  1048.3 5.0 copy-start.31
  1050.7 3.4 copy-start.35
  1053.3 8.5 copy-start.9
  1109.2 1.6 copy-start.42
  1114.7 37.3 %copy-start.15 = (bf16[1,256,1024]{2,1,0:T(8,128)(2,1)S(1)}, bf16[1,256,1024]{2,1,0:T(8,128)(2,1)}, u32[]{:S(2)}) copy-start(bf16[1,256,1024]{2,1,0:T(8,128)(2,1)} %param.33) | copy-start | bytes 1572868
  1114.8 696.3 %copy-start.1 = (bf16[1024,1024]{1,0:T(8,128)(2,1)S(1)}, bf16[1024,1024]{1,0:T(8,128)(2,1)}, u32[]{:S(2)}) copy-start(bf16[1024,1024]{1,0:T(8,128)(2,1)} %param.30) | copy-start | bytes 6291460
Sparse Core Ops, SparseCore 0:
  458.6 30.8 all-gather.3
  491.2 30.9 all-gather.5
  991.6 77.3 reduce-scatter.10
  1072.4 78.0 reduce-scatter.8
  1152.8 654.0 reduce-scatter.12
where the time goes:
time: 1840 us; the launch traced here: 1820 us
  waiting for transfers between devices  795 us (43%)
  local copies, waits for them, and re-layouts  471 us (26%)
  matrix products  275 us (15%)
  other arithmetic  177 us (10%)
  starting transfers between devices  57.7 us (3%)
  blocking collectives  26.9 us (1%)
    unnamed x7, waiting for transfers between devices  653 us
    gather x1, local copies, waits for them, and re-layouts, attend(): key_totals[backward_index]  80.6 us
    reduce_sum x2, other arithmetic, combine(): return jnp.sum(round_weight[..., None] * per_round, axis=1)  62.6 us
    unnamed x2, other arithmetic  48.4 us
    gather x1, local copies, waits for them, and re-layouts, attend_back(): grad_totals[order]  45.5 us
    gather x1, local copies, waits for them, and re-layouts, attend(): sorted_seg = segment[order]  45.5 us
    dot_general x16, matrix products, block_backward(): jnp.einsum('cqk,cqd->ckd', grad_dots, block_in[0], preferred_element_type...  45.3 us
    dot_general x32, matrix products, block_scores(): jnp.einsum('cqd,ckd->cqk', queries, keys, preferred_element_type=jnp.floa...  44 us
  transfers between devices with their start and end apart: 13, of which 9 were waited for; matrix products, arithmetic and copies ran while one was open for 19% of the time, Pallas kernels for 0%

commit v1 on v0

v1 whole, which is shorter than its diff:
```python
import functools
import jax
import jax.numpy as jnp
from jax import lax
from jax.experimental import pallas as pl
from jax.experimental.pallas import tpu as pltpu
from jax.sharding import PartitionSpec as P
HEADS = 8
DH = 128
ROUNDS = 4
SPAN = 64
EPS_NORM = 1e-05
EPS_KEY = 1e-06
SCALE = DH ** (-0.5)
EXTRA = 16
F32, BF16 = jnp.float32, jnp.bfloat16
VMEM_LIMIT = 60 * 2**20

def vm(n):
    return [pl.BlockSpec(memory_space=pltpu.VMEM)] * n

def split3(x):
    a = x.astype(BF16)
    r = x - a.astype(F32)
    b = r.astype(BF16)
    c = (r - b.astype(F32)).astype(BF16)
    return a, b, c

def attend_kernel(order, rows, bias, msg, q_out, keys, vals, probs, xq, xv, sq, sv):
    length = rows.shape[0]
    own = msg.shape[0] // (length // 256) - EXTRA

    def widen(b, c):
        at = pl.ds(b * 256, 256)
        xq[at, :] = rows[at, :DH].astype(F32)
        xv[at, :] = rows[at, DH:].astype(F32)
        return c
    lax.fori_loop(0, length // 256, widen, 0)

    def gather(b, c):
        for u in range(64):
            i = b * 64 + u
            src = order[i]
            sq[pl.ds(i, 1), :] = xq[pl.ds(src, 1), :]
            sv[pl.ds(i, 1), :] = xv[pl.ds(src, 1), :]
        return c
    lax.fori_loop(0, length // 64, gather, 0)

    def keys_of(b, c):
        at = pl.ds(b * 256, 256)
        q = sq[at, :]
        unit = q * lax.rsqrt(jnp.sum(q * q, axis=1, keepdims=True) + EPS_KEY)
        q_out[at, :] = q.astype(BF16)
        ahead = pl.ds(b * 256 + SPAN, 256)
        keys[ahead, :] = unit.astype(BF16)
        vals[ahead, :] = sv[at, :].astype(BF16)
        return c
    lax.fori_loop(0, length // 256, keys_of, 0)
    keys[0:SPAN, :] = keys[length:length + SPAN, :]
    vals[0:SPAN, :] = vals[length:length + SPAN, :]

    def block(b, c):
        for u in range(8):
            base = pl.multiple_of((b * 8 + u) * SPAN, SPAN)
            at, win = pl.ds(base, SPAN), pl.ds(base, 2 * SPAN)
            s = lax.dot_general(q_out[at, :], keys[win, :], (((1,), (1,)), ((), ())), preferred_element_type=F32)
            s = s * SCALE + bias[at, :].astype(F32)
            top = jnp.max(s, axis=1, keepdims=True)
            e = jnp.exp(s - top)
            total = jnp.sum(e, axis=1, keepdims=True)
            p = (e * (1.0 / total)).astype(BF16)
            probs[at, :] = p
            sq[at, :] = jnp.dot(p, vals[win, :], preferred_element_type=F32)
            sv[at, :] = jnp.broadcast_to(top + jnp.log(total), (SPAN, DH))
        return c
    lax.fori_loop(0, length // (8 * SPAN), block, 0)

    def scatter(b, c):
        for u in range(64):
            i = b * 64 + u
            dst = order[i]
            xq[pl.ds(dst, 1), :] = sq[pl.ds(i, 1), :]
            xv[pl.ds(dst, 1), :] = sv[pl.ds(i, 1), :]
        return c
    lax.fori_loop(0, length // 64, scatter, 0)

    eye = (lax.broadcasted_iota(jnp.int32, (128, 128), 0) == lax.broadcasted_iota(jnp.int32, (128, 128), 1))

    def send(b, c):
        at = pl.ds(b * 256, 256)
        to = pl.multiple_of(b * (256 + EXTRA), EXTRA)
        msg[pl.ds(to, 256), :] = xq[at, :].astype(BF16)
        lo = jnp.sum(jnp.where(eye, xv[pl.ds(b * 256, 128), :], 0.0), axis=0, keepdims=True)
        hi = jnp.sum(jnp.where(eye, xv[pl.ds(b * 256 + 128, 128), :], 0.0), axis=0, keepdims=True)
        parts = split3(lo) + split3(hi)
        tail = jnp.concatenate([p.astype(F32) for p in parts] + [jnp.zeros((EXTRA - 6, 128), F32)], axis=0)
        msg[pl.ds(to + 256, EXTRA), :] = tail.astype(BF16)
        return c
    lax.fori_loop(0, length // 256, send, 0)

def attend(order, rows, bias):
    length = rows.shape[0]
    blocks = length // 256
    sd = jax.ShapeDtypeStruct
    return pl.pallas_call(
        attend_kernel,
        out_shape=[sd((blocks * (256 + EXTRA), DH), BF16), sd((length, DH), BF16), sd((length + SPAN, DH), BF16), sd((length + SPAN, DH), BF16), sd((length, DH), BF16)],
        in_specs=[pl.BlockSpec(memory_space=pltpu.SMEM)] + vm(2),
        out_specs=vm(5),
        scratch_shapes=[pltpu.VMEM((length, DH), F32)] * 4,
        compiler_params=pltpu.CompilerParams(vmem_limit_bytes=VMEM_LIMIT),
        name="attend",
    )(order, rows, bias)

def back_kernel(order, msg, q_in, keys, vals, probs, out, xg, xd, sg, sd_, du, dv):
    length = q_in.shape[0]

    def widen(b, c):
        at = pl.ds(b * 256, 256)
        frm = pl.multiple_of(b * (256 + EXTRA), EXTRA)
        xg[at, :] = msg[pl.ds(frm, 256), :].astype(F32)
        t = msg[pl.ds(frm + 256, EXTRA), :].astype(F32)
        lo = t[0:1] + t[1:2] + t[2:3]
        hi = t[3:4] + t[4:5] + t[5:6]
        xd[pl.ds(b * 256, 128), :] = jnp.transpose(jnp.broadcast_to(lo, (128, 128)))
        xd[pl.ds(b * 256 + 128, 128), :] = jnp.transpose(jnp.broadcast_to(hi, (128, 128)))
        return c
    lax.fori_loop(0, length // 256, widen, 0)

    def gather(b, c):
        for u in range(64):
            i = b * 64 + u
            src = order[i]
            sg[pl.ds(i, 1), :] = xg[pl.ds(src, 1), :]
            sd_[pl.ds(i, 1), :] = xd[pl.ds(src, 1), :]
        return c
    lax.fori_loop(0, length // 64, gather, 0)

    du[0:SPAN, :] = jnp.zeros((SPAN, DH), F32)
    dv[0:SPAN, :] = jnp.zeros((SPAN, DH), F32)

    def block(b, c):
        for u in range(8):
            base = pl.multiple_of((b * 8 + u) * SPAN, SPAN)
            at, win, nxt = pl.ds(base, SPAN), pl.ds(base, 2 * SPAN), pl.ds(base + SPAN, SPAN)
            g = sg[at, :].astype(BF16)
            p = probs[at, :]
            gp = lax.dot_general(g, vals[win, :], (((1,), (1,)), ((), ())), preferred_element_type=F32)
            gs = p.astype(F32) * (gp - sd_[at, :])
            gd = (gs * SCALE).astype(BF16)
            sg[at, :] = jnp.dot(gd, keys[win, :], preferred_element_type=F32)
            wu = lax.dot_general(gd, q_in[at, :], (((0,), (0,)), ((), ())), preferred_element_type=F32)
            wv = lax.dot_general(p, g, (((0,), (0,)), ((), ())), preferred_element_type=F32)
            du[at, :] += wu[:SPAN]
            du[nxt, :] = wu[SPAN:]
            dv[at, :] += wv[:SPAN]
            dv[nxt, :] = wv[SPAN:]
        return c
    lax.fori_loop(0, length // (8 * SPAN), block, 0)
    du[length:length + SPAN, :] += du[0:SPAN, :]
    dv[length:length + SPAN, :] += dv[0:SPAN, :]

    def norm(b, c):
        at, ahead = pl.ds(b * 256, 256), pl.ds(b * 256 + SPAN, 256)
        q = q_in[at, :].astype(F32)
        r = lax.rsqrt(jnp.sum(q * q, axis=1, keepdims=True) + EPS_KEY)
        d = du[ahead, :]
        along = jnp.sum(q * d, axis=1, keepdims=True)
        sg[at, :] = sg[at, :] + r * d - q * (r * r * r * along)
        return c
    lax.fori_loop(0, length // 256, norm, 0)

    def scatter(b, c):
        for u in range(64):
            i = b * 64 + u
            dst = order[i]
            xg[pl.ds(dst, 1), :] = sg[pl.ds(i, 1), :]
            xd[pl.ds(dst, 1), :] = dv[pl.ds(i + SPAN, 1), :]
        return c
    lax.fori_loop(0, length // 64, scatter, 0)

    def narrow(b, c):
        at = pl.ds(b * 256, 256)
        out[at, :DH] = xg[at, :].astype(BF16)
        out[at, DH:] = xd[at, :].astype(BF16)
        return c
    lax.fori_loop(0, length // 256, narrow, 0)

def attend_back(order, msg, q_in, keys, vals, probs):
    length = q_in.shape[0]
    return pl.pallas_call(
        back_kernel,
        out_shape=jax.ShapeDtypeStruct((length, 2 * DH), BF16),
        in_specs=[pl.BlockSpec(memory_space=pltpu.SMEM)] + vm(5),
        out_specs=pl.BlockSpec(memory_space=pltpu.VMEM),
        scratch_shapes=[pltpu.VMEM((length, DH), F32)] * 4 + [pltpu.VMEM((length + SPAN, DH), F32)] * 2,
        compiler_params=pltpu.CompilerParams(vmem_limit_bytes=VMEM_LIMIT),
        name="attend_back",
    )(order, msg, q_in, keys, vals, probs)

def prepare(bucket_row, ends):
    length = bucket_row.shape[0]
    places = jnp.arange(length, dtype=jnp.int32)
    _, order = lax.sort((bucket_row * length + places, places), num_keys=1)
    pos = order.reshape(-1, SPAN)
    start = jnp.max(jnp.where(ends <= pos[..., None], ends, 0), axis=-1)
    window = jnp.concatenate([jnp.roll(pos, 1, 0), pos], axis=1)
    k, q = window[:, None, :], pos[:, :, None]
    bias = jnp.where((k >= start[:, :, None]) & (k <= q), jnp.where(k == q, -1000.0, 0.0), -1e9)
    return order, bias.astype(BF16).reshape(length, 2 * SPAN)

def layer_rows(x, gain, offset):
    centred = x - jnp.mean(x, axis=1, keepdims=True)
    inverse = lax.rsqrt(jnp.mean(centred * centred, axis=1, keepdims=True) + EPS_NORM)
    return centred * inverse * gain + offset


def layer_back(x, grad, gain):
    centred = x - jnp.mean(x, axis=1, keepdims=True)
    inverse = lax.rsqrt(jnp.mean(centred * centred, axis=1, keepdims=True) + EPS_NORM)
    unit = centred * inverse
    grad_gain = jnp.sum(grad * unit, axis=0, keepdims=True)
    grad_offset = jnp.sum(grad, axis=0, keepdims=True)
    scaled = grad * gain
    inner = jnp.mean(scaled * unit, axis=1, keepdims=True)
    grad_x = inverse * (scaled - jnp.mean(scaled, axis=1, keepdims=True) - unit * inner)
    return grad_x, grad_gain, grad_offset


def project_kernel(x, gain, offset, w_qk, w_value, msg, normed_out):
    rows = x.shape[0]
    normed = layer_rows(x[...].astype(F32), gain[...], offset[...]).astype(BF16)
    normed_out[...] = normed
    for h in range(HEADS):
        at = slice(h * DH, (h + 1) * DH)
        q = jnp.dot(normed, w_qk[:, at], preferred_element_type=F32).astype(BF16)
        v = jnp.dot(normed, w_value[:, at], preferred_element_type=F32).astype(BF16)
        for r in range(ROUNDS):
            msg[h * ROUNDS + r, :, :DH] = q
            msg[h * ROUNDS + r, :, DH:] = v


def project(x, gain, offset, w_qk, w_value):
    rows, width = x.shape
    return pl.pallas_call(
        project_kernel,
        out_shape=[
            jax.ShapeDtypeStruct((HEADS * ROUNDS, rows, 2 * DH), BF16),
            jax.ShapeDtypeStruct((rows, width), BF16),
        ],
        in_specs=vm(5),
        out_specs=vm(2),
        compiler_params=pltpu.CompilerParams(vmem_limit_bytes=VMEM_LIMIT),
        name="project",
    )(x, gain, offset, w_qk, w_value)


def combine_kernel(msg, x, w_out, gain, offset, mix, low_mix, first, first_low, normed, weights):
    rows = x.shape[0]
    for half in range(2):
        logs = []
        for r in range(ROUNDS):
            lines = []
            for h in range(HEADS):
                tail = msg[h * ROUNDS + r, rows : rows + EXTRA, :].astype(F32)
                k = half * 3
                lines.append(tail[k : k + 1] + tail[k + 1 : k + 2] + tail[k + 2 : k + 3])
            logs.append(jnp.concatenate(lines, axis=0))
        top = jnp.maximum(jnp.maximum(logs[0], logs[1]), jnp.maximum(logs[2], logs[3]))
        powers = [jnp.exp(v - top) for v in logs]
        inverse = 1.0 / (powers[0] + powers[1] + powers[2] + powers[3])
        lines = [v * inverse for v in powers]
        lines.append(jnp.zeros((128 - HEADS * ROUNDS, 128), F32))
        weights[half * 128 : half * 128 + 128, :] = jnp.transpose(jnp.concatenate(lines, axis=0))
    for h in range(HEADS):
        total = jnp.zeros((rows, DH), F32)
        for r in range(ROUNDS):
            j = r * HEADS + h
            total = total + weights[:, j : j + 1] * msg[h * ROUNDS + r, 0:rows, :].astype(F32)
        mix[:, h * DH : (h + 1) * DH] = total
        low_mix[:, h * DH : (h + 1) * DH] = total.astype(BF16)
    summed = x[...].astype(F32) + jnp.dot(low_mix[...], w_out[...], preferred_element_type=F32)
    first[...] = summed
    first_low[...] = summed.astype(BF16)
    normed[...] = layer_rows(summed, gain[...], offset[...]).astype(BF16)


def combine(msg, x, w_out, gain, offset):
    rows, width = x.shape
    sd = jax.ShapeDtypeStruct
    return pl.pallas_call(
        combine_kernel,
        out_shape=[
            sd((rows, width), F32),
            sd((rows, width), BF16),
            sd((rows, width), F32),
            sd((rows, width), BF16),
            sd((rows, width), BF16),
            sd((rows, 128), F32),
        ],
        in_specs=vm(5),
        out_specs=vm(6),
        compiler_params=pltpu.CompilerParams(vmem_limit_bytes=VMEM_LIMIT),
        name="combine",
    )(msg, x, w_out, gain, offset)


def uncombine_kernel(
    grads, first, gain, grad_one, w_out, mix, weights, grad_first, low_first, msg, grad_gain, grad_offset
):
    rows = first.shape[0]
    total = grads[0].astype(F32)
    for k in range(1, grads.shape[0]):
        total = total + grads[k].astype(F32)
    grad_x, gg, go = layer_back(first[...], total, gain[...])
    grad_gain[...] = gg
    grad_offset[...] = go
    grad_x = grad_x + grad_one[...].astype(F32)
    grad_first[...] = grad_x
    low = grad_x.astype(BF16)
    low_first[...] = low
    lane = lax.broadcasted_iota(jnp.int32, (rows, 128), 1)
    inner = jnp.zeros((rows, 128), F32)
    for h in range(HEADS):
        at = slice(h * DH, (h + 1) * DH)
        grad_mix = lax.dot_general(low, w_out[at, :], (((1,), (1,)), ((), ())), preferred_element_type=F32)
        dots = jnp.sum(grad_mix * mix[:, at], axis=1, keepdims=True)
        inner = jnp.where(lane % HEADS == h, dots, inner)
        for r in range(ROUNDS):
            j = r * HEADS + h
            msg[h * ROUNDS + r, 0:rows, :] = (weights[:, j : j + 1] * grad_mix).astype(BF16)
    inner = inner * weights[...]
    low_lines = [p.astype(F32) for p in split3(jnp.transpose(inner[0:128]))]
    high_lines = [p.astype(F32) for p in split3(jnp.transpose(inner[128:256]))]
    blank = jnp.zeros((EXTRA - 6, 128), F32)
    for h in range(HEADS):
        for r in range(ROUNDS):
            j = r * HEADS + h
            tail = [p[j : j + 1] for p in low_lines + high_lines] + [blank]
            msg[h * ROUNDS + r, rows : rows + EXTRA, :] = jnp.concatenate(tail, axis=0).astype(BF16)


def uncombine(grads, first, gain, grad_one, w_out, mix, weights):
    rows, width = first.shape
    sd = jax.ShapeDtypeStruct
    return pl.pallas_call(
        uncombine_kernel,
        out_shape=[
            sd((rows, width), F32),
            sd((rows, width), BF16),
            sd((HEADS * ROUNDS, rows + EXTRA, DH), BF16),
            sd((1, width), F32),
            sd((1, width), F32),
        ],
        in_specs=vm(7),
        out_specs=vm(5),
        compiler_params=pltpu.CompilerParams(vmem_limit_bytes=VMEM_LIMIT),
        name="uncombine",
    )(grads, first, gain, grad_one, w_out, mix, weights)


def finish_kernel(
    msg, normed, x, gain, w_qk, w_value, grad_two, grad_second, part_qk, part_value, grad_gain, grad_offset, gq, gv
):
    rows = x.shape[0]
    for h in range(HEADS):
        at = slice(h * DH, (h + 1) * DH)
        total = msg[h * ROUNDS].astype(F32)
        for r in range(1, ROUNDS):
            total = total + msg[h * ROUNDS + r].astype(F32)
        gq[:, at] = total[:, :DH].astype(BF16)
        gv[:, at] = total[:, DH:].astype(BF16)
    flip = (((0,), (0,)), ((), ()))
    part_qk[...] = lax.dot_general(normed[...], gq[...], flip, preferred_element_type=F32).astype(BF16)
    part_value[...] = lax.dot_general(normed[...], gv[...], flip, preferred_element_type=F32).astype(BF16)
    across = (((1,), (1,)), ((), ()))
    grad_normed = lax.dot_general(gq[...], w_qk[...], across, preferred_element_type=F32)
    grad_normed = grad_normed + lax.dot_general(gv[...], w_value[...], across, preferred_element_type=F32)
    grad_x, gg, go = layer_back(x[...].astype(F32), grad_normed, gain[...])
    grad_gain[...] = gg
    grad_offset[...] = go
    grad_second[...] = grad_x + grad_two[...].astype(F32)


def finish(msg, normed, x, gain, w_qk, w_value, grad_two):
    rows, width = x.shape
    sd = jax.ShapeDtypeStruct
    return pl.pallas_call(
        finish_kernel,
        out_shape=[
            sd((rows, width), F32),
            sd((width, width), BF16),
            sd((width, width), BF16),
            sd((1, width), F32),
            sd((1, width), F32),
        ],
        in_specs=vm(7),
        out_specs=vm(5),
        scratch_shapes=[pltpu.VMEM((rows, width), BF16)] * 2,
        compiler_params=pltpu.CompilerParams(vmem_limit_bytes=VMEM_LIMIT),
        name="finish",
    )(msg, normed, x, gain, w_qk, w_value, grad_two)


def gelu_exact(values):
    return jax.nn.gelu(values, approximate=False)


def swap(array, axis):
    return lax.all_to_all(array, axis, split_axis=0, concat_axis=0, tiled=True)


def summed_rows(array):
    rows, width = array.shape
    seqs, ffns = lax.axis_size("seq"), lax.axis_size("ffn")
    near = swap(array.reshape(seqs, rows // seqs, width), "seq").astype(F32).sum(axis=0)
    near = near.astype(BF16).reshape(ffns, -1, width)
    return swap(near, "ffn").astype(F32).sum(axis=0)


def shards(
    stream_one,
    stream_two,
    doc_lengths,
    bucket_ids,
    norm1_gain,
    norm1_bias,
    w_qk,
    w_value,
    w_out,
    norm2_gain,
    norm2_bias,
    w_up,
    w_down,
    grad_out_one,
    grad_out_two,
):
    rows, width = stream_one.shape[1:]
    gain_one, bias_one = norm1_gain.reshape(1, -1), norm1_bias.reshape(1, -1)
    gain_two, bias_two = norm2_gain.reshape(1, -1), norm2_bias.reshape(1, -1)
    grad_rows = lax.all_gather(grad_out_two[0], "ffn", axis=0, tiled=True)
    msg, normed_one = project(stream_two[0], gain_one, bias_one, w_qk, w_value)
    received = swap(msg, "seq").reshape(-1, 2 * DH)
    order, bias = prepare(bucket_ids[0, 0], jnp.cumsum(doc_lengths[0]))
    sent, queries, keys, vals, probs = attend(order, received, bias)
    per_round = swap(sent.reshape(-1, rows + EXTRA, DH), "seq")
    mix, low_mix, first, first_low, normed_two, weights = combine(
        per_round, stream_one[0], w_out, gain_two, bias_two
    )

    gathered = lax.all_gather(normed_two, "ffn", axis=0, tiled=True)
    pre_act = jnp.dot(gathered, w_up, preferred_element_type=F32)
    hidden = gelu_exact(pre_act).astype(BF16)
    across = (((1,), (1,)), ((), ()))
    out_part = lax.dot_general(hidden, w_down, across, preferred_element_type=F32).astype(BF16)
    sum_two = stream_two[0].astype(F32) + swap(out_part.reshape(-1, rows, width), "ffn").astype(F32).sum(axis=0)
    grad_hidden = jnp.dot(grad_rows, w_down, preferred_element_type=F32)
    grad_pre = jax.vjp(gelu_exact, pre_act)[1](grad_hidden)[0].astype(BF16)
    flip = (((0,), (0,)), ((), ()))
    grad_down_part = lax.dot_general(grad_rows, hidden, flip, preferred_element_type=F32).astype(BF16)
    grad_up_part = lax.dot_general(gathered, grad_pre, flip, preferred_element_type=F32).astype(BF16)
    grad_part = lax.dot_general(grad_pre, w_up, across, preferred_element_type=F32).astype(BF16)
    arrived = swap(grad_part.reshape(-1, rows, width), "ffn")

    grad_first, low_first, msg, grad_gain_two, grad_bias_two = uncombine(
        arrived, first, gain_two, grad_out_one[0], w_out, mix, weights
    )
    part_out = lax.dot_general(low_mix, low_first, flip, preferred_element_type=F32).astype(BF16)
    far = swap(msg, "seq").reshape(-1, DH)
    copies = attend_back(order, far, queries, keys, vals, probs)
    back = swap(copies.reshape(-1, rows, 2 * DH), "seq")
    grad_second, part_qk, part_value, grad_gain_one, grad_bias_one = finish(
        back, normed_one, stream_two[0], gain_one, w_qk, w_value, grad_out_two[0]
    )
    small = jnp.concatenate([grad_gain_one, grad_bias_one, grad_gain_two, grad_bias_two], axis=0)
    small = lax.psum_scatter(small.T, ("seq", "ffn"), scatter_dimension=0, tiled=True)
    heavy = summed_rows(jnp.concatenate([part_qk, part_value], axis=1))
    grad_w_out = summed_rows(part_out)
    seqs = lax.axis_size("seq")
    grad_up = swap(grad_up_part.reshape(seqs, -1, width), "seq").astype(F32).sum(axis=0)
    grad_down = swap(grad_down_part.reshape(seqs, -1, width), "seq").astype(F32).sum(axis=0)
    return (
        first_low[None],
        sum_two.astype(BF16)[None],
        grad_first[None],
        grad_second[None],
        small[:, 0],
        small[:, 1],
        heavy[:, :width],
        heavy[:, width:],
        grad_w_out,
        small[:, 2],
        small[:, 3],
        grad_up,
        grad_down,
    )


def solution(mesh):
    return jax.shard_map(
        shards,
        mesh=mesh,
        in_specs=(
            P("ffn", "seq", None),
            P("ffn", "seq", None),
            P("ffn", None),
            P("ffn", "seq", None),
            P(),
            P(),
            P(),
            P(),
            P(),
            P(),
            P(),
            P(None, "ffn"),
            P(None, "ffn"),
            P("ffn", "seq", None),
            P("ffn", "seq", None),
        ),
        out_specs=(
            P("ffn", "seq", None),
            P("ffn", "seq", None),
            P("ffn", "seq", None),
            P("ffn", "seq", None),
            P(("seq", "ffn")),
            P(("seq", "ffn")),
            P(("seq", "ffn"), None),
            P(("seq", "ffn"), None),
            P(("seq", "ffn"), None),
            P(("seq", "ffn")),
            P(("seq", "ffn")),
            P("seq", "ffn"),
            P("seq", "ffn"),
        ),
        check_vma=False,
    )
```

time: 1840 us -> 710 us (0.39)
  waiting for transfers between devices: 795 us -> 239 us
  local copies, waits for them, and re-layouts: 471 us -> 1.77 us
  matrix products: 275 us -> 45.2 us
  Pallas kernels: 0 us -> 163 us
  other arithmetic: 177 us -> 31.8 us
  blocking collectives: 26.9 us -> 135 us
    unnamed x7 -> x2, waiting for transfers between devices: 653 us -> 0.54 us
    gather x7 -> x0, local copies, waits for them, and re-layouts: 299 us -> none  [the longest x1 80.6 us: attend(): key_totals[backward_index]]
    dot_general x127 -> x7, matrix products: 275 us -> 45.2 us  [the longest x1 14.1 us: shards(): pre_act = jnp.dot(gathered, w_up, preferred_element_type=F32)]
    pallas_call x0 -> x6, Pallas kernels: none -> 163 us  [the longest x1 74 us: attend(): pl.pallas_call(attend_kernel, out_shape=[sd((blocks * (256 + EXTRA), DH),...]
    all_to_all x8 -> x11, waiting for transfers between devices: 87.4 us -> 191 us  [swap(): return lax.all_to_all(array, axis, split_axis=0, concat_axis=0, tiled=True)]
    unnamed x0 -> x1, blocking collectives: none -> 96.7 us
    reduce_sum x32 -> x7, other arithmetic: 80.9 us -> 14.4 us  [the longest x2 6.25 us: summed_rows(): swap(array.reshape(seqs, rows // seqs, width), 'seq').astype(F32)]
    unnamed x2 -> x0, other arithmetic: 48.4 us -> none
  transfers between devices with their start and end apart: 13 -> 13, of which waited for: 9 -> 10; matrix products, arithmetic and copies ran while one was open for 19% -> 9% of each run, Pallas kernels for 0% -> 11%
where the time goes in v1:
time: 710 us; the launch traced here: 701 us
  waiting for transfers between devices  239 us (34%)
  Pallas kernels  163 us (23%)
  blocking collectives  135 us (19%)
  starting transfers between devices  70.1 us (10%)
  matrix products  45.2 us (6%)
  other arithmetic  31.8 us (4%)
  between operations  14.8 us (2%)
    all_to_all x11, waiting for transfers between devices, swap(): return lax.all_to_all(array, axis, split_axis=0, concat_axis=0, tiled=True)  191 us
    unnamed x1, blocking collectives  96.7 us
    pallas_call x1, Pallas kernels, attend(): pl.pallas_call(attend_kernel, out_shape=[sd((blocks * (256 + EXTRA), DH),...  74 us
    all_to_all x11, starting transfers between devices, swap(): return lax.all_to_all(array, axis, split_axis=0, concat_axis=0, tiled=True)  69.8 us
    pallas_call x1, Pallas kernels, attend_back(): pl.pallas_call(back_kernel, out_shape=jax.ShapeDtypeStruct((length, 2 * D...  60.4 us
    all_to_all x1, blocking collectives, swap(): return lax.all_to_all(array, axis, split_axis=0, concat_axis=0, tiled=True)  38.2 us
    all_gather x1, waiting for transfers between devices, shards(): gathered = lax.all_gather(normed_two, 'ffn', axis=0, tiled=True)  28.9 us
    all_gather x1, waiting for transfers between devices, shards(): grad_rows = lax.all_gather(grad_out_two[0], 'ffn', axis=0, tiled=True)  18.5 us
  transfers between devices with their start and end apart: 13, of which 10 were waited for; matrix products, arithmetic and copies ran while one was open for 9% of the time, Pallas kernels for 11%

profile of v1, /device:TPU:1, one launch (start us, length us, event | category | flops | bytes accessed | tf_op | source)
XLA Modules:
  0.0 700.6 jit_solution(1109637433926672111)
XLA Ops:
  7.2 0.0 copy-start
  7.2 7.4 %project.1 = (bf16[32,256,256]{2,1,0:T(8,128)(2,1)}, bf16[256,1024]{1,0:T(8,128)(2,1)}) custom-call(bf16[256,1024]{1,0:T(8,128)(2,1)} %bitcast.83, f32[1,1024]{1,0:T(1,128)} %bitcast.97, f32[1,1024]{1,0:T(1,128)} %bitcast.99, bf16[1024,1024]{1,0:T(8,128)(2,1)} %w_qk.3, bf16[1024,1024]{1,0:T(8,128)(2,1)} %w_value.3), custom_call_target="tpu_custom_call" | custom-call | tf_op jit(solution)/shard_map/project/pallas_call | solution.py:245
  14.6 8.8 %all-to-all-start = ((bf16[32,256,256]{2,1,0:T(8,128)(2,1)}), bf16[32,256,256]{2,1,0:T(8,128)(2,1)}, u32[]{:S(2)}, u32[]{:S(2)}) async-start(bf16[32,256,256]{2,1,0:T(8,128)(2,1)} %get-tuple-element.38), calls=%async_computation | async-start | bytes 8388608 | tf_op jit(solution)/shard_map/all_to_all | solution.py:410
  23.4 0.0 all-gather.4.cloned.1.call-start
  23.5 6.8 sort.15
  30.3 0.1 reshape.130
  30.4 0.1 slice.43
  30.4 0.1 copy.28
  30.5 0.0 copy-done.15
  30.5 0.2 reduce-window.8
  30.7 0.1 select_reduce_fusion
  30.8 0.1 copy.29
  30.9 0.1 ge.20
  31.0 0.1 slice_bitcast_fusion.4
  31.1 0.1 pad_add_fusion
  31.2 4.6 select_convert_fusion.bias
  35.7 37.9 %all-to-all-done = bf16[32,256,256]{2,1,0:T(8,128)(2,1)} async-done(((bf16[32,256,256]{2,1,0:T(8,128)(2,1)}), bf16[32,256,256]{2,1,0:T(8,128)(2,1)}, u32[]{:S(2)}, u32[]{:S(2)}) %all-to-all-start) | async-done | bytes 4194336 | tf_op jit(solution)/shard_map/all_to_all | solution.py:410
  73.7 74.0 %attend.1 = (bf16[8704,128]{1,0:T(8,128)(2,1)}, bf16[8192,128]{1,0:T(8,128)(2,1)}, bf16[8256,128]{1,0:T(8,128)(2,1)}, bf16[8256,128]{1,0:T(8,128)(2,1)}, bf16[8192,128]{1,0:T(8,128)(2,1)}) custom-call(s32[8192]{0:T(1024)} %copy-done.6, bf16[8192,256]{1,0:T(8,128)(2,1)} %bitcast.4.rows, bf16[8192,128]{1,0:T(8,128)(2,1)} %select_convert_fusion.bias), custom_call_target="tpu_custom_call" | custom-call | tf_op jit(solution)/shard_map/attend/pallas_call | solution.py:105
  147.6 38.2 %all_to_all.60.msg = bf16[32,272,128]{2,1,0:T(8,128)(2,1)} all-to-all(bf16[32,272,128]{2,1,0:T(8,128)(2,1)} %bitcast.85), channel_id=1, replica_groups=mesh['seq'=32,'ffn'=4] {'seq'}, dimensions={0} | all-to-all | bytes 4456448 | tf_op jit(solution)/shard_map/all_to_all | solution.py:410
  185.8 6.2 combine.1
  192.0 0.0 all-gather.4.cloned.1.call-update
  192.0 0.2 all-gather.6.cloned.1.call-start
  192.3 0.5 all-gather.6.cloned.1.call-update
  192.8 28.9 %all-gather.4.cloned.1.call-done = bf16[1024,1024]{1,0:T(8,128)(2,1)} async-done(((bf16[256,1024]{1,0:T(8,128)(2,1)}), bf16[1024,1024]{1,0:T(8,128)(2,1)}) %all-gather.4.cloned.1.call-update) | async-done | bytes 2097168 | tf_op jit(solution)/shard_map/all_gather | solution.py:451
  221.7 14.1 %multiply_convert_fusion = (bf16[1024,1024]{1,0:T(8,128)(2,1)}, f32[1024,1024]{1,0:T(8,128)}, f32[1024,1024]{1,0:T(8,128)}) fusion(bf16[1024,1024]{1,0:T(8,128)(2,1)} %all-gather.4.cloned.1.call-done, bf16[1024,1024]{1,0:T(8,128)(2,1)S(1)} %copy-done), kind=kOutput, calls=%fused_computation.10 | convolution fusion | flops 2215641088 | bytes 14680064 | tf_op jit(solution)/shard_map/dot_general | solution.py:452
  235.8 18.5 %all-gather.6.cloned.1.call-done = bf16[1,1024,1024]{2,1,0:T(8,128)(2,1)} async-done(((bf16[1,256,1024]{2,1,0:T(8,128)(2,1)}), bf16[1,1024,1024]{2,1,0:T(8,128)(2,1)}) %all-gather.6.cloned.1.call-update) | async-done | bytes 2097168 | tf_op jit(solution)/shard_map/all_gather | solution.py:441
  254.3 8.0 %add_convert_fusion = bf16[1024,1024]{1,0:T(8,128)(2,1)S(1)} fusion(f32[1024,1024]{1,0:T(8,128)} %get-tuple-element.62, f32[1024,1024]{1,0:T(8,128)} %get-tuple-element.69, bf16[1024,1024]{1,0:T(8,128)(2,1)} %param.27, bf16[1,1024,1024]{2,1,0:T(8,128)(2,1)} %all-gather.6.cloned.1.call-done), kind=kOutput, calls=%fused_computation.8 | convolution fusion | flops 2162163712 | bytes 14680064 | tf_op jit(solution)/shard_map/dot_general | solution.py:457
  262.3 3.7 convolution_convert_fusion.2
  266.1 3.6 all-to-all-start.3
  269.7 5.9 convolution_convert_fusion.3
  275.6 19.8 %all-to-all-done.3.grads = bf16[4,256,1024]{2,1,0:T(8,128)(2,1)S(1)} async-done(((bf16[4,256,1024]{2,1,0:T(8,128)(2,1)}), bf16[4,256,1024]{2,1,0:T(8,128)(2,1)S(1)}, u32[]{:S(2)}, u32[]{:S(2)}) %all-to-all-start.3) | async-done | bytes 2097184 | tf_op jit(solution)/shard_map/all_to_all | solution.py:410
  295.4 4.4 all-to-all-start.2
  299.8 6.0 convolution_convert_fusion
  305.8 18.9 %all-to-all-done.2 = bf16[4,256,1024]{2,1,0:T(8,128)(2,1)} async-done(((bf16[4,256,1024]{2,1,0:T(8,128)(2,1)}), bf16[4,256,1024]{2,1,0:T(8,128)(2,1)}, u32[]{:S(2)}, u32[]{:S(2)}) %all-to-all-start.2) | async-done | bytes 2097184 | tf_op jit(solution)/shard_map/all_to_all | solution.py:410
  324.7 9.5 %all-to-all-start.10 = ((bf16[32,32,1024]{2,1,0:T(8,128)(2,1)}), bf16[32,32,1024]{2,1,0:T(8,128)(2,1)S(1)}, u32[]{:S(2)}, u32[]{:S(2)}) async-start(bf16[32,32,1024]{2,1,0:T(8,128)(2,1)} %bitcast.88), calls=%async_computation.10 | async-start | bytes 4194304 | tf_op jit(solution)/shard_map/all_to_all | solution.py:410
  334.3 7.5 %uncombine.1 = (f32[256,1024]{1,0:T(8,128)}, bf16[256,1024]{1,0:T(8,128)(2,1)}, bf16[32,272,128]{2,1,0:T(8,128)(2,1)}, f32[1,1024]{1,0:T(1,128)}, f32[1,1024]{1,0:T(1,128)}) custom-call(bf16[4,256,1024]{2,1,0:T(8,128)(2,1)} %copy-done.2, f32[256,1024]{1,0:T(8,128)} %get-tuple-element.42.first, f32[1,1024]{1,0:T(1,128)} %bitcast.96, ...), custom_call_target="tpu_custom_call" | custom-call | tf_op jit(solution)/shard_map/uncombine/pallas_call | solution.py:346
  341.7 20.4 %all-to-all-done.10 = bf16[32,32,1024]{2,1,0:T(8,128)(2,1)S(1)} async-done(((bf16[32,32,1024]{2,1,0:T(8,128)(2,1)}), bf16[32,32,1024]{2,1,0:T(8,128)(2,1)S(1)}, u32[]{:S(2)}, u32[]{:S(2)}) %all-to-all-start.10) | async-done | bytes 2097184 | tf_op jit(solution)/shard_map/all_to_all | solution.py:410
  362.1 6.8 all-to-all-start.4
  368.9 2.2 convolution_convert_fusion.1
  371.0 27.3 %all-to-all-done.4 = bf16[32,272,128]{2,1,0:T(8,128)(2,1)} async-done(((bf16[32,272,128]{2,1,0:T(8,128)(2,1)}), bf16[32,272,128]{2,1,0:T(8,128)(2,1)}, u32[]{:S(2)}, u32[]{:S(2)}) %all-to-all-start.4) | async-done | bytes 2228256 | tf_op jit(solution)/shard_map/all_to_all | solution.py:410
  398.3 6.9 all-to-all-start.8
  405.2 60.4 %attend_back.1 = bf16[8192,256]{1,0:T(8,128)(2,1)} custom-call(s32[8192]{0:T(1024)} %copy-done.6, bf16[8704,128]{1,0:T(8,128)(2,1)} %bitcast.20.msg, bf16[8192,128]{1,0:T(8,128)(2,1)} %get-tuple-element.47.q_in, bf16[8256,128]{1,0:T(8,128)(2,1)} %get-tuple-element.48.keys, bf16[8256,128]{1,0:T(8,128)(2,1)} %get-tuple-element.49.vals, ...), custom_call_target="tpu_custom_call" | custom-call | tf_op jit(solution)/shard_map/attend_back/pallas_call | solution.py:191
  465.6 7.7 %all-to-all-start.5 = ((bf16[32,256,256]{2,1,0:T(8,128)(2,1)}), bf16[32,256,256]{2,1,0:T(8,128)(2,1)}, u32[]{:S(2)}, u32[]{:S(2)}) async-start(bf16[32,256,256]{2,1,0:T(8,128)(2,1)} %bitcast.80), calls=%async_computation.5 | async-start | bytes 8388608 | tf_op jit(solution)/shard_map/all_to_all | solution.py:410
  473.3 5.3 fusion.13
  478.6 44.9 %all-to-all-done.5.msg = bf16[32,256,256]{2,1,0:T(8,128)(2,1)} async-done(((bf16[32,256,256]{2,1,0:T(8,128)(2,1)}), bf16[32,256,256]{2,1,0:T(8,128)(2,1)}, u32[]{:S(2)}, u32[]{:S(2)}) %all-to-all-start.5) | async-done | bytes 4194336 | tf_op jit(solution)/shard_map/all_to_all | solution.py:410
  523.5 7.5 %all-to-all-start.11 = ((bf16[32,32,1024]{2,1,0:T(8,128)(2,1)}), bf16[32,32,1024]{2,1,0:T(8,128)(2,1)S(1)}, u32[]{:S(2)}, u32[]{:S(2)}) async-start(bf16[32,32,1024]{2,1,0:T(8,128)(2,1)} %bitcast.87), calls=%async_computation.11 | async-start | bytes 4194304 | tf_op jit(solution)/shard_map/all_to_all | solution.py:410
  531.1 2.6 reduce_sum.75
  533.7 7.9 %finish.1 = (f32[256,1024]{1,0:T(8,128)}, bf16[1024,1024]{1,0:T(8,128)(2,1)}, bf16[1024,1024]{1,0:T(8,128)(2,1)}, f32[1,1024]{1,0:T(1,128)}, f32[1,1024]{1,0:T(1,128)}) custom-call(bf16[32,256,256]{2,1,0:T(8,128)(2,1)} %all-to-all-done.5.msg, bf16[256,1024]{1,0:T(8,128)(2,1)} %get-tuple-element.51.normed, bf16[256,1024]{1,0:T(8,128)(2,1)} %bitcast.84, ...), custom_call_target="tpu_custom_call" | custom-call | tf_op jit(solution)/shard_map/finish/pallas_call | solution.py:388
  541.6 17.3 %all-to-all-done.11 = bf16[32,32,1024]{2,1,0:T(8,128)(2,1)S(1)} async-done(((bf16[32,32,1024]{2,1,0:T(8,128)(2,1)}), bf16[32,32,1024]{2,1,0:T(8,128)(2,1)S(1)}, u32[]{:S(2)}, u32[]{:S(2)}) %all-to-all-start.11) | async-done | bytes 2097184 | tf_op jit(solution)/shard_map/all_to_all | solution.py:410
  558.9 3.3 all-to-all-start.9
  562.2 4.7 pad_maximum_fusion
  566.9 7.8 %all-to-all-start.6 = ((bf16[32,32,2048]{2,1,0:T(8,128)(2,1)}), bf16[32,32,2048]{2,1,0:T(8,128)(2,1)}, u32[]{:S(2)}, u32[]{:S(2)}) async-start(bf16[32,32,2048]{2,1,0:T(8,128)(2,1)} %bitcast.81), calls=%async_computation.6 | async-start | bytes 8388608 | tf_op jit(solution)/shard_map/all_to_all | solution.py:410
  574.8 2.1 convert_reduce_fusion.2
  576.9 0.9 fusion.16
  577.9 2.8 convert_reduce_fusion.1
  580.6 2.6 convert_reduce_fusion
  583.2 0.6 convert_reduce_fusion.4
  583.9 96.7 %all-reduce = f32[1024,4]{0,1:T(4,128)S(1)} all-reduce(f32[1024,4]{0,1:T(4,128)S(1)} %maximum_bitcast_fusion), channel_id=3, replica_groups=mesh['seq'=32,'ffn'=4] {'seq','ffn'}, use_global_device_ids=true, to_apply=%region_4.5.clone | all-reduce | flops 4096 | bytes 32768
  680.6 0.1 constant_dynamic-slice_fusion
  680.7 3.7 reduce_sum.73
  684.4 3.5 all-to-all-start.7
  687.9 0.5 slice_bitcast_fusion
  688.4 4.3 all-to-all-done.7
  692.7 0.6 fusion.18
  (40 shorter events, 0.2 us)
Async XLA Ops:
  7.2 214.5 %copy-start = (bf16[1024,1024]{1,0:T(8,128)(2,1)S(1)}, bf16[1024,1024]{1,0:T(8,128)(2,1)}, u32[]{:S(2)}) copy-start(bf16[1024,1024]{1,0:T(8,128)(2,1)} %param.26) | copy-start | bytes 6291460
  14.6 8.8 %copy-start.9 = (s32[1,1,8192]{2,1,0:T(1,128)S(1)}, s32[1,1,8192]{2,1,0:T(1,128)}, u32[]{:S(2)}) copy-start(s32[1,1,8192]{2,1,0:T(1,128)} %param.18) | copy-start | bytes 98308
  14.6 15.9 %copy-start.15 = (s32[1,9]{1,0:T(1,128)S(1)}, s32[1,9]{1,0:T(1,128)}, u32[]{:S(2)}) copy-start(s32[1,9]{1,0:T(1,128)} %param.17) | copy-start | bytes 112
  14.6 59.0 %all-to-all-start = ((bf16[32,256,256]{2,1,0:T(8,128)(2,1)}), bf16[32,256,256]{2,1,0:T(8,128)(2,1)}, u32[]{:S(2)}, u32[]{:S(2)}) async-start(bf16[32,256,256]{2,1,0:T(8,128)(2,1)} %get-tuple-element.38), calls=%async_computation | async-start | bytes 8388608 | tf_op jit(solution)/shard_map/all_to_all | solution.py:410
  23.4 198.3 %all-gather.4.cloned.1.call-start = ((), (), s32[]{:S(2)}) async-start(), calls=%async_computation.12 | async-start | bytes 2621440 | tf_op jit(solution)/shard_map/all_gather | solution.py:451
  30.3 43.4 %copy-start.6 = (s32[8192]{0:T(1024)}, s32[8192]{0:T(1024)S(1)}, u32[]{:S(2)}) copy-start(s32[8192]{0:T(1024)S(1)} %get-tuple-element.37.order) | copy-start | bytes 98308
  192.0 62.3 %all-gather.6.cloned.1.call-start = ((), (), s32[]{:S(2)}) async-start(), calls=%async_computation.13 | async-start | bytes 2621440 | tf_op jit(solution)/shard_map/all_gather | solution.py:441
  262.3 3.7 copy-start.16
  266.1 29.3 %all-to-all-start.3 = ((bf16[4,256,1024]{2,1,0:T(8,128)(2,1)}), bf16[4,256,1024]{2,1,0:T(8,128)(2,1)S(1)}, u32[]{:S(2)}, u32[]{:S(2)}) async-start(bf16[4,256,1024]{2,1,0:T(8,128)(2,1)} %bitcast.90), calls=%async_computation.3 | async-start | bytes 4194304 | tf_op jit(solution)/shard_map/all_to_all | solution.py:410
  295.4 10.4 %copy-start.2 = (bf16[4,256,1024]{2,1,0:T(8,128)(2,1)}, bf16[4,256,1024]{2,1,0:T(8,128)(2,1)S(1)}, u32[]{:S(2)}) copy-start(bf16[4,256,1024]{2,1,0:T(8,128)(2,1)S(1)} %all-to-all-done.3.grads) | copy-start | bytes 6291460
  295.4 29.3 %all-to-all-start.2 = ((bf16[4,256,1024]{2,1,0:T(8,128)(2,1)}), bf16[4,256,1024]{2,1,0:T(8,128)(2,1)}, u32[]{:S(2)}, u32[]{:S(2)}) async-start(bf16[4,256,1024]{2,1,0:T(8,128)(2,1)} %bitcast.89), calls=%async_computation.2 | async-start | bytes 4194304 | tf_op jit(solution)/shard_map/all_to_all | solution.py:410
  324.7 37.4 %all-to-all-start.10 = ((bf16[32,32,1024]{2,1,0:T(8,128)(2,1)}), bf16[32,32,1024]{2,1,0:T(8,128)(2,1)S(1)}, u32[]{:S(2)}, u32[]{:S(2)}) async-start(bf16[32,32,1024]{2,1,0:T(8,128)(2,1)} %bitcast.88), calls=%async_computation.10 | async-start | bytes 4194304 | tf_op jit(solution)/shard_map/all_to_all | solution.py:410
  334.2 34.6 %copy-start.7 = (bf16[256,1024]{1,0:T(8,128)(2,1)S(1)}, bf16[256,1024]{1,0:T(8,128)(2,1)}, u32[]{:S(2)}) copy-start(bf16[256,1024]{1,0:T(8,128)(2,1)} %get-tuple-element.59) | copy-start | bytes 1572868
  341.7 27.1 %copy-start.8 = (bf16[256,1024]{1,0:T(8,128)(2,1)S(1)}, bf16[256,1024]{1,0:T(8,128)(2,1)}, u32[]{:S(2)}) copy-start(bf16[256,1024]{1,0:T(8,128)(2,1)} %get-tuple-element.60) | copy-start | bytes 1572868
  362.1 36.2 %copy-start.3 = (bf16[32,32,1024]{2,1,0:T(8,128)(2,1)}, bf16[32,32,1024]{2,1,0:T(8,128)(2,1)S(1)}, u32[]{:S(2)}) copy-start(bf16[32,32,1024]{2,1,0:T(8,128)(2,1)S(1)} %all-to-all-done.10) | copy-start | bytes 6291460
  362.1 36.2 %all-to-all-start.4 = ((bf16[32,272,128]{2,1,0:T(8,128)(2,1)}), bf16[32,272,128]{2,1,0:T(8,128)(2,1)}, u32[]{:S(2)}, u32[]{:S(2)}) async-start(bf16[32,272,128]{2,1,0:T(8,128)(2,1)} %get-tuple-element.46), calls=%async_computation.4 | async-start | bytes 4456448 | tf_op jit(solution)/shard_map/all_to_all | solution.py:410
  398.3 67.3 %all-to-all-start.8 = ((bf16[32,32,1024]{2,1,0:T(8,128)(2,1)}), bf16[32,32,1024]{2,1,0:T(8,128)(2,1)}, u32[]{:S(2)}, u32[]{:S(2)}) async-start(bf16[32,32,1024]{2,1,0:T(8,128)(2,1)} %bitcast.82), calls=%async_computation.8 | async-start | bytes 4194304 | tf_op jit(solution)/shard_map/all_to_all | solution.py:410
  465.6 7.7 %copy-start.14 = (bf16[1,1024,1024]{2,1,0:T(8,128)(2,1)S(1)}, bf16[1,1024,1024]{2,1,0:T(8,128)(2,1)}, u32[]{:S(2)}) copy-start(bf16[1,1024,1024]{2,1,0:T(8,128)(2,1)} %all-gather.6.cloned.1.call-done) | copy-start | bytes 6291460
  465.6 57.9 %all-to-all-start.5 = ((bf16[32,256,256]{2,1,0:T(8,128)(2,1)}), bf16[32,256,256]{2,1,0:T(8,128)(2,1)}, u32[]{:S(2)}, u32[]{:S(2)}) async-start(bf16[32,256,256]{2,1,0:T(8,128)(2,1)} %bitcast.80), calls=%async_computation.5 | async-start | bytes 8388608 | tf_op jit(solution)/shard_map/all_to_all | solution.py:410
  523.5 35.4 %all-to-all-start.11 = ((bf16[32,32,1024]{2,1,0:T(8,128)(2,1)}), bf16[32,32,1024]{2,1,0:T(8,128)(2,1)S(1)}, u32[]{:S(2)}, u32[]{:S(2)}) async-start(bf16[32,32,1024]{2,1,0:T(8,128)(2,1)} %bitcast.87), calls=%async_computation.11 | async-start | bytes 4194304 | tf_op jit(solution)/shard_map/all_to_all | solution.py:410
  558.9 8.0 %copy-start.4 = (bf16[32,32,1024]{2,1,0:T(8,128)(2,1)}, bf16[32,32,1024]{2,1,0:T(8,128)(2,1)S(1)}, u32[]{:S(2)}) copy-start(bf16[32,32,1024]{2,1,0:T(8,128)(2,1)S(1)} %all-to-all-done.11) | copy-start | bytes 6291460
  558.9 8.0 %all-to-all-start.9 = ((bf16[4,8,1024]{2,1,0:T(8,128)(2,1)}), bf16[4,8,1024]{2,1,0:T(8,128)(2,1)S(1)}, u32[]{:S(2)}, u32[]{:S(2)}) async-start(bf16[4,8,1024]{2,1,0:T(8,128)(2,1)} %bitcast.30), calls=%async_computation.9 | async-start | bytes 131072 | tf_op jit(solution)/shard_map/all_to_all | solution.py:410
  566.9 10.0 %copy-start.5 = (bf16[1,256,1024]{2,1,0:T(8,128)(2,1)S(1)}, bf16[1,256,1024]{2,1,0:T(8,128)(2,1)}, u32[]{:S(2)}) copy-start(bf16[1,256,1024]{2,1,0:T(8,128)(2,1)} %param.16) | copy-start | bytes 1572868
  566.9 113.8 %all-to-all-start.6 = ((bf16[32,32,2048]{2,1,0:T(8,128)(2,1)}), bf16[32,32,2048]{2,1,0:T(8,128)(2,1)}, u32[]{:S(2)}, u32[]{:S(2)}) async-start(bf16[32,32,2048]{2,1,0:T(8,128)(2,1)} %bitcast.81), calls=%async_computation.6 | async-start | bytes 8388608 | tf_op jit(solution)/shard_map/all_to_all | solution.py:410
  574.8 9.1 %copy-start.10 = (f32[1,1024]{1,0:T(1,128)S(1)}, f32[1,1024]{1,0:T(1,128)}, u32[]{:S(2)}) copy-start(f32[1,1024]{1,0:T(1,128)} %get-tuple-element.55) | copy-start | bytes 12292
  574.8 9.1 %copy-start.11 = (f32[1,1024]{1,0:T(1,128)S(1)}, f32[1,1024]{1,0:T(1,128)}, u32[]{:S(2)}) copy-start(f32[1,1024]{1,0:T(1,128)} %get-tuple-element.56) | copy-start | bytes 12292
  574.8 9.1 %copy-start.12 = (f32[1,1024]{1,0:T(1,128)S(1)}, f32[1,1024]{1,0:T(1,128)}, u32[]{:S(2)}) copy-start(f32[1,1024]{1,0:T(1,128)} %get-tuple-element.53) | copy-start | bytes 12292
  574.8 9.1 %copy-start.13 = (f32[1,1024]{1,0:T(1,128)S(1)}, f32[1,1024]{1,0:T(1,128)}, u32[]{:S(2)}) copy-start(f32[1,1024]{1,0:T(1,128)} %get-tuple-element.54) | copy-start | bytes 12292
  577.9 115.5 %copy-start.1 = (bf16[1024,1024]{1,0:T(8,128)(2,1)S(1)}, bf16[1024,1024]{1,0:T(8,128)(2,1)}, u32[]{:S(2)}) copy-start(bf16[1024,1024]{1,0:T(8,128)(2,1)} %param.26) | copy-start | bytes 6291460
  684.4 8.3 %all-to-all-start.7 = ((bf16[4,8,2048]{2,1,0:T(8,128)(2,1)}), bf16[4,8,2048]{2,1,0:T(8,128)(2,1)S(1)}, u32[]{:S(2)}, u32[]{:S(2)}) async-start(bf16[4,8,2048]{2,1,0:T(8,128)(2,1)} %bitcast.28), calls=%async_computation.7 | async-start | bytes 262144 | tf_op jit(solution)/shard_map/all_to_all | solution.py:410
Sparse Core Ops, SparseCore 0:
  192.2 29.4 all-gather.3
  223.4 30.9 all-gather.5

commit v2 on v1

v2 whole, which is shorter than its diff:
```python
import jax
import jax.numpy as jnp
from jax import lax
from jax.experimental import pallas as pl
from jax.experimental.pallas import tpu as pltpu
from jax.sharding import PartitionSpec as P

HEADS = 8
DH = 128
ROUNDS = 4
SPAN = 64
EPS_NORM = 1e-05
EPS_KEY = 1e-06
SCALE = DH ** (-0.5)
EXTRA = 16
F32, BF16 = jnp.float32, jnp.bfloat16
VMEM_LIMIT = 60 * 2**20
ACROSS = (((1,), (1,)), ((), ()))
FLIP = (((0,), (0,)), ((), ()))


def vm(n):
    return [pl.BlockSpec(memory_space=pltpu.VMEM)] * n


def sd(shape, kind):
    return jax.ShapeDtypeStruct(shape, kind)


def params():
    return pltpu.CompilerParams(vmem_limit_bytes=VMEM_LIMIT)


def takes(us):
    return pl.CostEstimate(flops=0, transcendentals=0, bytes_accessed=int(us * 3.5e6))


def split3(x):
    a = x.astype(BF16)
    r = x - a.astype(F32)
    b = r.astype(BF16)
    c = (r - b.astype(F32)).astype(BF16)
    return a, b, c


def layer_rows(x, gain, offset):
    centred = x - jnp.mean(x, axis=1, keepdims=True)
    inverse = lax.rsqrt(jnp.mean(centred * centred, axis=1, keepdims=True) + EPS_NORM)
    return centred * inverse * gain + offset


def layer_back(x, grad, gain):
    centred = x - jnp.mean(x, axis=1, keepdims=True)
    inverse = lax.rsqrt(jnp.mean(centred * centred, axis=1, keepdims=True) + EPS_NORM)
    unit = centred * inverse
    grad_gain = jnp.sum(grad * unit, axis=0, keepdims=True)
    grad_offset = jnp.sum(grad, axis=0, keepdims=True)
    scaled = grad * gain
    inner = jnp.mean(scaled * unit, axis=1, keepdims=True)
    grad_x = inverse * (scaled - jnp.mean(scaled, axis=1, keepdims=True) - unit * inner)
    return grad_x, grad_gain, grad_offset


def split_by_core(turned, keep, give):
    core = lax.axis_index("seq") % 2
    for j in range(keep.shape[0]):
        keep[j] = turned[pl.ds(pl.multiple_of(j * 64 + core * 32, 32), 32), :]
        give[j] = turned[pl.ds(pl.multiple_of(j * 64 + (1 - core) * 32, 32), 32), :]


def project_kernel(x, gain, offset, w_qk, w_value, msg, normed_out, keep, give, turned):
    normed = layer_rows(x[...].astype(F32), gain[...], offset[...])
    low = normed.astype(BF16)
    normed_out[...] = low
    for h in range(HEADS):
        at = slice(h * DH, (h + 1) * DH)
        q = jnp.dot(low, w_qk[:, at], preferred_element_type=F32).astype(BF16)
        v = jnp.dot(low, w_value[:, at], preferred_element_type=F32).astype(BF16)
        for t in range(2):
            msg[h * 2 + t, :, :DH] = q
            msg[h * 2 + t, :, DH:] = v
    turned[...] = jnp.transpose(low.astype(F32)).astype(BF16)
    split_by_core(turned, keep, give)


def project(x, gain, offset, w_qk, w_value):
    rows, width = x.shape
    chips = 2 * HEADS
    return pl.pallas_call(
        project_kernel,
        out_shape=[
            sd((chips, rows, 2 * DH), BF16),
            sd((rows, width), BF16),
            sd((width // 64, 32, rows), BF16),
            sd((width // 64, 32, rows), BF16),
        ],
        in_specs=vm(5),
        out_specs=vm(4),
        scratch_shapes=[pltpu.VMEM((width, rows), BF16)],
        compiler_params=params(),
        name="project",
        cost_estimate=takes(7),
    )(x, gain, offset, w_qk, w_value)


BLOCK = 4 * SPAN


def shift_rows(order, base, pairs, gathers):
    for u in range(BLOCK):
        place = order[base + u]
        for src, dst in pairs:
            if gathers:
                dst[u : u + 1, :] = src[pl.ds(place, 1), :]
            else:
                dst[pl.ds(place, 1), :] = src[u : u + 1, :]


def by_core(array, keep, give):
    core = lax.axis_index("seq") % 2

    def narrow(j, c):
        for out, side in ((keep, core), (give, 1 - core)):
            at = pl.ds(pl.multiple_of((2 * j + side) * 256, 256), 256)
            out[j] = array[at, :].astype(BF16)
        return c

    lax.fori_loop(0, keep.shape[0], narrow, 0)


def attend_kernel(order, mine, other, bias, msg, q_out, keys, vals, probs, xq, xv, oq, ov, *slots):
    length = q_out.shape[0]
    blocks = length // BLOCK
    core = lax.axis_index("seq") % 2
    came, done = (slots[0:2], slots[2:4]), (slots[4:6], slots[6:8])

    def widen(j, c):
        for rows, side in ((mine, core), (other, 1 - core)):
            at = pl.ds(pl.multiple_of((2 * j + side) * 256, 256), 256)
            xq[at, :] = rows[j, :, :DH].astype(F32)
            xv[at, :] = rows[j, :, DH:].astype(F32)
        return c

    lax.fori_loop(0, length // 512, widen, 0)

    def gather(b, slot):
        shift_rows(order, b * BLOCK, list(zip((xq, xv), slot)), True)

    def scatter(b, slot):
        shift_rows(order, b * BLOCK, list(zip(slot, (oq, ov))), False)

    def ready(b, slot):
        q = slot[0][...]
        unit = q * lax.rsqrt(jnp.sum(q * q, axis=1, keepdims=True) + EPS_KEY)
        ahead = pl.ds(pl.multiple_of(b * BLOCK + SPAN, SPAN), BLOCK)
        keys[ahead, :] = unit.astype(BF16)
        vals[ahead, :] = slot[1][...].astype(BF16)
        return q.astype(BF16)

    gather(blocks - 1, came[1])
    ready(blocks - 1, came[1])
    keys[0:SPAN, :] = keys[length : length + SPAN, :]
    vals[0:SPAN, :] = vals[length : length + SPAN, :]
    gather(0, came[0])

    def compute(b, slot, out):
        base = pl.multiple_of(b * BLOCK, BLOCK)
        q = ready(b, slot)
        q_out[pl.ds(base, BLOCK), :] = q
        k = keys[pl.ds(base, BLOCK + SPAN), :]
        v = vals[pl.ds(base, BLOCK + SPAN), :]
        spans = range(BLOCK // SPAN)
        s = [
            lax.dot_general(
                q[u * SPAN : u * SPAN + SPAN], k[u * SPAN : u * SPAN + 2 * SPAN], ACROSS, preferred_element_type=F32
            )
            for u in spans
        ]
        s = jnp.concatenate(s, axis=0) * SCALE + bias[pl.ds(base, BLOCK), :].astype(F32)
        top = jnp.max(s, axis=1, keepdims=True)
        e = jnp.exp(s - top)
        total = jnp.sum(e, axis=1, keepdims=True)
        p = (e * (1.0 / total)).astype(BF16)
        probs[pl.ds(base, BLOCK), :] = p
        for u in spans:
            out[0][u * SPAN : u * SPAN + SPAN, :] = jnp.dot(
                p[u * SPAN : u * SPAN + SPAN], v[u * SPAN : u * SPAN + 2 * SPAN], preferred_element_type=F32
            )
        out[1][...] = jnp.broadcast_to(top + jnp.log(total), (BLOCK, DH))

    def step(i, c):
        b = 2 * i
        scatter(jnp.maximum(b - 1, 0), done[1])
        gather(b + 1, came[1])
        compute(b, came[0], done[0])
        scatter(b, done[0])
        gather(jnp.minimum(b + 2, blocks - 1), came[0])
        compute(b + 1, came[1], done[1])
        return c

    lax.fori_loop(0, blocks // 2, step, 0)
    scatter(blocks - 1, done[1])

    across = lax.broadcasted_iota(jnp.int32, (128, 128), 0)
    eye = across == lax.broadcasted_iota(jnp.int32, (128, 128), 1)

    def send(b, c):
        at = pl.ds(b * 256, 256)
        msg[b, 0:256, :] = oq[at, :].astype(BF16)
        lo = jnp.sum(jnp.where(eye, ov[pl.ds(b * 256, 128), :], 0.0), axis=0, keepdims=True)
        hi = jnp.sum(jnp.where(eye, ov[pl.ds(b * 256 + 128, 128), :], 0.0), axis=0, keepdims=True)
        parts = split3(lo) + split3(hi)
        tail = [p.astype(F32) for p in parts] + [jnp.zeros((EXTRA - 6, 128), F32)]
        msg[b, 256:, :] = jnp.concatenate(tail, axis=0).astype(BF16)
        return c

    lax.fori_loop(0, length // 256, send, 0)


def attend(order, mine, other, bias):
    length = order.shape[0]
    return pl.pallas_call(
        attend_kernel,
        out_shape=[
            sd((length // 256, 256 + EXTRA, DH), BF16),
            sd((length, DH), BF16),
            sd((length + SPAN, DH), BF16),
            sd((length + SPAN, DH), BF16),
            sd((length, DH), BF16),
        ],
        in_specs=[pl.BlockSpec(memory_space=pltpu.SMEM)] + vm(3),
        out_specs=vm(5),
        scratch_shapes=[pltpu.VMEM((length, DH), F32)] * 4 + [pltpu.VMEM((BLOCK, DH), F32)] * 8,
        compiler_params=params(),
        name="attend",
        cost_estimate=takes(37),
    )(order, mine, other, bias)


def back_value_kernel(order, msg, vals, probs, keep, give, gd_out, xg, xd, ov, saved, carry, *slots):
    length = probs.shape[0]
    blocks = length // BLOCK
    came, done = (slots[0:2], slots[2:4]), (slots[4:5], slots[5:6])

    def widen(b, c):
        xg[pl.ds(b * 256, 256), :] = msg[b, 0:256, :].astype(F32)
        t = msg[b, 256:, :].astype(F32)
        lo = t[0:1] + t[1:2] + t[2:3]
        hi = t[3:4] + t[4:5] + t[5:6]
        xd[pl.ds(b * 256, 128), :] = jnp.transpose(jnp.broadcast_to(lo, (128, 128)))
        xd[pl.ds(b * 256 + 128, 128), :] = jnp.transpose(jnp.broadcast_to(hi, (128, 128)))
        return c

    lax.fori_loop(0, length // 256, widen, 0)

    def gather(b, slot):
        shift_rows(order, b * BLOCK, list(zip((xg, xd), slot)), True)

    def scatter(b, slot):
        base = jnp.where(b == 0, length, b * BLOCK) - SPAN
        for u in range(BLOCK):
            if u == SPAN:
                base = b * BLOCK - SPAN
            ov[pl.ds(order[base + u], 1), :] = slot[0][u : u + 1, :]

    gather(0, came[0])
    carry[...] = jnp.zeros(carry.shape, F32)

    def compute(b, slot, out):
        base = pl.multiple_of(b * BLOCK, BLOCK)
        g = slot[0][...].astype(BF16)
        p = probs[pl.ds(base, BLOCK), :]
        v = vals[pl.ds(base, BLOCK + SPAN), :]
        spans = range(BLOCK // SPAN)
        cut = lambda a, u: a[u * SPAN : u * SPAN + SPAN]
        gp = [
            lax.dot_general(cut(g, u), v[u * SPAN : u * SPAN + 2 * SPAN], ACROSS, preferred_element_type=F32)
            for u in spans
        ]
        gs = p.astype(F32) * (jnp.concatenate(gp, axis=0) - slot[1][...])
        gd_out[pl.ds(base, BLOCK), :] = (gs * SCALE).astype(BF16)
        wide = [lax.dot_general(cut(p, u), cut(g, u), FLIP, preferred_element_type=F32) for u in spans]

        @pl.when(b == 0)
        def _():
            saved[...] = wide[0][:SPAN]

        out[0][0:SPAN, :] = carry[...] + wide[0][:SPAN]
        for u in spans[1:]:
            out[0][u * SPAN : u * SPAN + SPAN, :] = wide[u - 1][SPAN:] + wide[u][:SPAN]
        carry[...] = wide[-1][SPAN:]

    def step(i, c):
        b = 2 * i
        scatter(jnp.maximum(b - 1, 0), done[1])
        gather(b + 1, came[1])
        compute(b, came[0], done[0])
        scatter(b, done[0])
        gather(jnp.minimum(b + 2, blocks - 1), came[0])
        compute(b + 1, came[1], done[1])
        return c

    lax.fori_loop(0, blocks // 2, step, 0)
    scatter(blocks - 1, done[1])
    carry[...] += saved[...]
    for u in range(SPAN):
        ov[pl.ds(order[length - SPAN + u], 1), :] = carry[u : u + 1, :]
    by_core(ov, keep, give)


def back_value(order, msg, vals, probs):
    length = probs.shape[0]
    half = length // 512
    return pl.pallas_call(
        back_value_kernel,
        out_shape=[sd((half, 256, DH), BF16)] * 2 + [sd((length, DH), BF16)],
        in_specs=[pl.BlockSpec(memory_space=pltpu.SMEM)] + vm(3),
        out_specs=vm(3),
        scratch_shapes=[pltpu.VMEM((length, DH), F32)] * 3
        + [pltpu.VMEM((SPAN, DH), F32)] * 2
        + [pltpu.VMEM((BLOCK, DH), F32)] * 6,
        compiler_params=params(),
        name="back_value",
        cost_estimate=takes(26),
    )(order, msg, vals, probs)


def back_query_kernel(order, gd, q_in, keys, keep, give, oq, saved, carry, waiting, *done):
    length = q_in.shape[0]
    blocks = length // BLOCK

    def scatter(b, slot):
        base = jnp.where(b == 0, length, b * BLOCK) - SPAN
        for u in range(BLOCK):
            if u == SPAN:
                base = b * BLOCK - SPAN
            oq[pl.ds(order[base + u], 1), :] = slot[u : u + 1, :]

    carry[...] = jnp.zeros(carry.shape, F32)
    waiting[...] = jnp.zeros(waiting.shape, F32)

    def whole(direct, unit_grad, q):
        q = q.astype(F32)
        r = lax.rsqrt(jnp.sum(q * q, axis=1, keepdims=True) + EPS_KEY)
        along = jnp.sum(q * unit_grad, axis=1, keepdims=True)
        return direct + r * unit_grad - q * (r * r * r * along)

    def compute(b, out):
        base = pl.multiple_of(b * BLOCK, BLOCK)
        d = gd[pl.ds(base, BLOCK), :]
        q = q_in[pl.ds(base, BLOCK), :]
        k = keys[pl.ds(base, BLOCK + SPAN), :]
        back = q_in[pl.ds(pl.multiple_of(jnp.maximum(base - SPAN, 0), SPAN), SPAN), :]
        spans = range(BLOCK // SPAN)
        cut = lambda a, u: a[u * SPAN : u * SPAN + SPAN]
        direct = [jnp.dot(cut(d, u), k[u * SPAN : u * SPAN + 2 * SPAN], preferred_element_type=F32) for u in spans]
        wide = [lax.dot_general(cut(d, u), cut(q, u), FLIP, preferred_element_type=F32) for u in spans]

        @pl.when(b == 0)
        def _():
            saved[...] = wide[0][:SPAN]

        folded = [carry[...] + wide[0][:SPAN]] + [wide[u - 1][SPAN:] + wide[u][:SPAN] for u in spans[1:]]
        straight = [waiting[...]] + direct[:-1]
        behind = jnp.concatenate([back, q[: BLOCK - SPAN]], axis=0)
        out[...] = whole(jnp.concatenate(straight, axis=0), jnp.concatenate(folded, axis=0), behind)
        carry[...] = wide[-1][SPAN:]
        waiting[...] = direct[-1]

    def step(i, c):
        b = 2 * i
        scatter(jnp.maximum(b - 1, 0), done[1])
        compute(b, done[0])
        scatter(b, done[0])
        compute(b + 1, done[1])
        return c

    lax.fori_loop(0, blocks // 2, step, 0)
    scatter(blocks - 1, done[1])
    waiting[...] = whole(waiting[...], carry[...] + saved[...], q_in[length - SPAN : length, :])
    for u in range(SPAN):
        oq[pl.ds(order[length - SPAN + u], 1), :] = waiting[u : u + 1, :]
    by_core(oq, keep, give)


def back_query(order, gd, q_in, keys):
    length = q_in.shape[0]
    half = length // 512
    return pl.pallas_call(
        back_query_kernel,
        out_shape=[sd((half, 256, DH), BF16)] * 2,
        in_specs=[pl.BlockSpec(memory_space=pltpu.SMEM)] + vm(3),
        out_specs=vm(2),
        scratch_shapes=[pltpu.VMEM((length, DH), F32)]
        + [pltpu.VMEM((SPAN, DH), F32)] * 3
        + [pltpu.VMEM((BLOCK, DH), F32)] * 2,
        compiler_params=params(),
        name="back_query",
        cost_estimate=takes(17),
    )(order, gd, q_in, keys)


def prepare(bucket_row, ends):
    length = bucket_row.shape[0]
    places = jnp.arange(length, dtype=jnp.int32)
    _, order = lax.sort((bucket_row * length + places, places), num_keys=1)
    pos = order.reshape(-1, SPAN)
    start = jnp.max(jnp.where(ends <= pos[..., None], ends, 0), axis=-1)
    window = jnp.concatenate([jnp.roll(pos, 1, 0), pos], axis=1)
    k, q = window[:, None, :], pos[:, :, None]
    bias = jnp.where((k >= start[:, :, None]) & (k <= q), jnp.where(k == q, -1000.0, 0.0), -1e9)
    return order, bias.astype(BF16).reshape(length, 2 * SPAN)


def combine_kernel(msg, x, w_out, gain, offset, mix, low_mix, first_out, first_low, normed, weights):
    rows = x.shape[0]
    for half in range(2):
        logs = []
        for r in range(ROUNDS):
            lines = []
            for h in range(HEADS):
                tail = msg[h * ROUNDS + r, rows : rows + EXTRA, :].astype(F32)
                k = half * 3
                lines.append(tail[k : k + 1] + tail[k + 1 : k + 2] + tail[k + 2 : k + 3])
            logs.append(jnp.concatenate(lines, axis=0))
        top = jnp.maximum(jnp.maximum(logs[0], logs[1]), jnp.maximum(logs[2], logs[3]))
        powers = [jnp.exp(v - top) for v in logs]
        inverse = 1.0 / (powers[0] + powers[1] + powers[2] + powers[3])
        lines = [v * inverse for v in powers]
        lines.append(jnp.zeros((128 - HEADS * ROUNDS, 128), F32))
        weights[half * 128 : half * 128 + 128, :] = jnp.transpose(jnp.concatenate(lines, axis=0))
    for h in range(HEADS):
        total = jnp.zeros((rows, DH), F32)
        for r in range(ROUNDS):
            j = r * HEADS + h
            total = total + weights[:, j : j + 1] * msg[h * ROUNDS + r, 0:rows, :].astype(F32)
        mix[:, h * DH : (h + 1) * DH] = total
        low_mix[:, h * DH : (h + 1) * DH] = total.astype(BF16)
    first = x[...].astype(F32) + jnp.dot(low_mix[...], w_out[...], preferred_element_type=F32)
    first_out[...] = first
    first_low[...] = first.astype(BF16)
    normed[...] = layer_rows(first, gain[...], offset[...]).astype(BF16)


def combine(msg, x, w_out, gain, offset):
    rows, width = x.shape
    return pl.pallas_call(
        combine_kernel,
        out_shape=[
            sd((rows, width), F32),
            sd((rows, width), BF16),
            sd((rows, width), F32),
            sd((rows, width), BF16),
            sd((rows, width), BF16),
            sd((rows, 128), F32),
        ],
        in_specs=vm(5),
        out_specs=vm(6),
        compiler_params=params(),
        name="combine",
        cost_estimate=takes(6),
    )(msg, x, w_out, gain, offset)


def gelu_both(act, grad):
    share = 0.5 + 0.5 * lax.erf(act * 0.7071067811865476)
    slope = share + act * (jnp.exp(act * act * -0.5) * 0.3989422804014327)
    return (act * share).astype(BF16), (grad * slope).astype(BF16)


def middle_kernel(*refs):
    (mix, low_mix, first, normed, weights, x_two, g_one, g_two, w_out, gain, up0, down0) = refs[:12]
    far = refs[12:24]
    (two_low, grad_first, sent, grad_gain, grad_offset, keep_mix, give_mix, low_first, hid0, pre0) = refs[24:34]
    (turned, up, down, hid, pre, summed, sems) = refs[34:]
    rows = x_two.shape[0]
    core = lax.axis_index("seq") % 2

    def copies(flip):
        out = [pltpu.make_async_copy(up0, up.at[0], sems.at[0]), pltpu.make_async_copy(down0, down.at[0], sems.at[1])]
        for i in range(6):
            a, b = (far[i + 6], far[i]) if flip else (far[i], far[i + 6])
            at = pl.ds(i % 2 * 512, 512)
            out.append(pltpu.make_async_copy(a, up.at[1 + i // 2, at], sems.at[2 + 2 * i]))
            out.append(pltpu.make_async_copy(b, down.at[1 + i // 2, at], sems.at[3 + 2 * i]))
        return out

    @pl.when(core == 0)
    def _():
        for c in copies(False):
            c.start()

    @pl.when(core == 1)
    def _():
        for c in copies(True):
            c.start()

    for c in copies(False):
        c.wait()

    def hidden_part(i, c):
        k = i // 4
        at = pl.ds(pl.multiple_of((i % 4) * 256, 256), 256)
        act = jnp.dot(normed[...], up[k, :, at], preferred_element_type=F32)
        grad = jnp.dot(g_two[...], down[k, :, at], preferred_element_type=F32)
        hid[k, :, at], pre[k, :, at] = gelu_both(act, grad)
        return c

    lax.fori_loop(0, 16, hidden_part, 0)
    hid0[...] = hid[0]
    pre0[...] = pre[0]
    summed[...] = jnp.zeros(summed.shape, F32)

    def up_back(k, c):
        summed[...] += lax.dot_general(pre[k], up[k], ACROSS, preferred_element_type=F32)
        return c

    lax.fori_loop(0, 4, up_back, 0)
    grad_x, gg, go = layer_back(first[...], summed[...], gain[...])
    grad_gain[...] = gg
    grad_offset[...] = go
    grad_x = grad_x + g_one[...].astype(F32)
    grad_first[...] = grad_x
    low_first[...] = grad_x.astype(BF16)
    lane = lax.broadcasted_iota(jnp.int32, (rows, 128), 1)
    inner = jnp.zeros((rows, 128), F32)
    for h in range(HEADS):
        at = slice(h * DH, (h + 1) * DH)
        grad_mix = lax.dot_general(low_first[...], w_out[at, :], ACROSS, preferred_element_type=F32)
        dots = jnp.sum(grad_mix * mix[:, at], axis=1, keepdims=True)
        inner = jnp.where(lane % HEADS == h, dots, inner)
        for r in range(ROUNDS):
            j = r * HEADS + h
            sent[h * ROUNDS + r, 0:rows, :] = (weights[:, j : j + 1] * grad_mix).astype(BF16)
    inner = inner * weights[...]
    low_lines = [p.astype(F32) for p in split3(jnp.transpose(inner[0:128]))]
    high_lines = [p.astype(F32) for p in split3(jnp.transpose(inner[128:256]))]
    blank = jnp.zeros((EXTRA - 6, 128), F32)
    for h in range(HEADS):
        for r in range(ROUNDS):
            j = r * HEADS + h
            tail = [p[j : j + 1] for p in low_lines + high_lines] + [blank]
            sent[h * ROUNDS + r, rows : rows + EXTRA, :] = jnp.concatenate(tail, axis=0).astype(BF16)

    summed[...] = x_two[...].astype(F32)

    def down_out(k, c):
        summed[...] += lax.dot_general(hid[k], down[k], ACROSS, preferred_element_type=F32)
        return c

    lax.fori_loop(0, 4, down_out, 0)
    two_low[...] = summed[...].astype(BF16)
    turned[...] = jnp.transpose(low_mix[...].astype(F32)).astype(BF16)
    split_by_core(turned, keep_mix, give_mix)


def middle(mix, low_mix, first, normed, weights, x_two, g_one, g_two, w_out, gain, up0, down0, mine, other):
    rows, width = x_two.shape
    anywhere = [pl.BlockSpec(memory_space=pl.ANY)] * 14
    return pl.pallas_call(
        middle_kernel,
        out_shape=[
            sd((rows, width), BF16),
            sd((rows, width), F32),
            sd((HEADS * ROUNDS, rows + EXTRA, DH), BF16),
            sd((1, width), F32),
            sd((1, width), F32),
            sd((width // 64, 32, rows), BF16),
            sd((width // 64, 32, rows), BF16),
            sd((rows, width), BF16),
            sd((rows, 1024), BF16),
            sd((rows, 1024), BF16),
        ],
        in_specs=vm(10) + anywhere,
        out_specs=vm(10),
        scratch_shapes=[
            pltpu.VMEM((width, rows), BF16),
            pltpu.VMEM((4, width, 1024), BF16),
            pltpu.VMEM((4, width, 1024), BF16),
            pltpu.VMEM((4, rows, 1024), BF16),
            pltpu.VMEM((4, rows, 1024), BF16),
            pltpu.VMEM((rows, width), F32),
            pltpu.SemaphoreType.DMA((14,)),
        ],
        compiler_params=params(),
        name="middle",
        cost_estimate=takes(25),
    )(mix, low_mix, first, normed, weights, x_two, g_one, g_two, w_out, gain, up0, down0, *mine, *other)


def feed_kernel(normed, grads, hid0, pre0, n1, n2, n3, g1, g2, g3, up, down, keep, give, hid, pre, turned, total):
    core = lax.axis_index("seq") % 2
    hid[0] = hid0[...]
    pre[0] = pre0[...]
    for k, (n, g) in enumerate(((n1, g1), (n2, g2), (n3, g3)), start=1):

        def hidden_part(i, c):
            at = pl.ds(pl.multiple_of(i * 256, 256), 256)
            act = jnp.dot(n[...], up[:, at], preferred_element_type=F32)
            grad = jnp.dot(g[...], down[:, at], preferred_element_type=F32)
            hid[k, :, at], pre[k, :, at] = gelu_both(act, grad)
            return c

        lax.fori_loop(0, 4, hidden_part, 0)
    for first, lefts, rights in ((0, (normed, n1, n2, n3), pre), (1024, (grads, g1, g2, g3), hid)):
        left = jnp.concatenate([x[...] for x in lefts], axis=0)
        turned[...] = jnp.transpose(left.astype(F32)).astype(BF16)

        def piece(i, c):
            left = turned[pl.ds(pl.multiple_of(i * 256, 256), 256), :]
            total[...] = jnp.dot(left, rights[...].reshape(4 * n1.shape[0], 1024), preferred_element_type=F32)
            for out, side in ((keep, core), (give, 1 - core)):
                for j in range(4):
                    rows = total[pl.ds(pl.multiple_of(j * 64 + side * 32, 32), 32), :]
                    out[i * 4 + j, :, first : first + 1024] = rows.astype(BF16)
            return c

        lax.fori_loop(0, keep.shape[0] // 4, piece, 0)


def feed(normed, grads, hid0, pre0, normed_far, grads_far, up, down):
    rows, width = normed.shape
    return pl.pallas_call(
        feed_kernel,
        out_shape=[sd((width // 64, 32, 2048), BF16)] * 2,
        in_specs=vm(12),
        out_specs=vm(2),
        scratch_shapes=[pltpu.VMEM((4, rows, 1024), BF16)] * 2
        + [pltpu.VMEM((width, 4 * rows), BF16), pltpu.VMEM((256, 1024), F32)],
        compiler_params=params(),
        name="feed",
        cost_estimate=takes(18),
    )(normed, grads, hid0, pre0, *normed_far, *grads_far, up, down)


def sum_rounds_kernel(back, out):
    for h in range(HEADS):
        total = back[2 * h].astype(F32) + back[2 * h + 1].astype(F32)
        for half in range(2):
            at = slice(half * HEADS * DH + h * DH, half * HEADS * DH + (h + 1) * DH)
            out[:, at] = total[:, half * DH : (half + 1) * DH].astype(BF16)


def sum_rounds(back):
    rows = back.shape[1]
    return pl.pallas_call(
        sum_rounds_kernel,
        out_shape=sd((rows, 2 * HEADS * DH), BF16),
        in_specs=vm(1),
        out_specs=pl.BlockSpec(memory_space=pltpu.VMEM),
        compiler_params=params(),
        name="sum_rounds",
        cost_estimate=takes(3),
    )(back)


def finish_kernel(grads, x, gain, w_qk, w_value, grad_two, gain_two, offset_two, grad_second, small, near, far):
    width = x.shape[1]
    grad_normed = lax.dot_general(grads[:, :width], w_qk[...], ACROSS, preferred_element_type=F32)
    grad_normed = grad_normed + lax.dot_general(grads[:, width:], w_value[...], ACROSS, preferred_element_type=F32)
    grad_x, gg, go = layer_back(x[...].astype(F32), grad_normed, gain[...])
    grad_second[...] = grad_x + grad_two[...].astype(F32)
    lines = []
    for line in (gg, go, gain_two[...], offset_two[...]):
        high = line.astype(BF16).astype(F32)
        lines += [high, line - high]
    blank = jnp.zeros((8, width), F32)
    rest = jnp.zeros((112, width), F32)
    near[...] = jnp.transpose(jnp.concatenate(lines + [blank, rest], axis=0))
    far[...] = jnp.transpose(jnp.concatenate([blank] + lines + [rest], axis=0))
    core = lax.axis_index("seq") % 2
    for j in range(small.shape[0]):
        a = near[pl.ds(pl.multiple_of(j * 64 + core * 32, 32), 32), :]
        b = far[pl.ds(pl.multiple_of(j * 64 + (1 - core) * 32, 32), 32), :]
        small[j] = (a + b).astype(BF16)


def finish(grads, x, gain, w_qk, w_value, grad_two, gain_two, offset_two):
    rows, width = x.shape
    return pl.pallas_call(
        finish_kernel,
        out_shape=[sd((rows, width), F32), sd((width // 64, 32, 128), BF16)],
        in_specs=vm(8),
        out_specs=vm(2),
        scratch_shapes=[pltpu.VMEM((width, 128), F32)] * 2,
        compiler_params=params(),
        name="finish",
        cost_estimate=takes(5),
    )(grads, x, gain, w_qk, w_value, grad_two, gain_two, offset_two)


def pair_kernel(left, left_other, right, right_other, *rest):
    blocks, lines, rows = left.shape
    out, width = rest[-1], right.shape[1]
    total = jnp.dot(left[...].reshape(blocks * lines, rows), right[...], preferred_element_type=F32)
    total = total + jnp.dot(left_other[...].reshape(blocks * lines, rows), right_other[...], preferred_element_type=F32)
    out[:, :, :width] = total.astype(BF16).reshape(blocks, lines, width)
    if len(rest) == 2:
        out[:, :, width:] = rest[0][...]


def pair(left, left_other, right, right_other, *extra):
    blocks, lines, rows = left.shape
    width = right.shape[1] + sum(e.shape[2] for e in extra)
    return pl.pallas_call(
        pair_kernel,
        out_shape=sd((blocks, lines, width), BF16),
        in_specs=vm(4 + len(extra)),
        out_specs=pl.BlockSpec(memory_space=pltpu.VMEM),
        compiler_params=params(),
        name="pair",
        cost_estimate=takes(3),
    )(left, left_other, right, right_other, *extra)


def swap_seq(array):
    return lax.all_to_all(array, "seq", split_axis=0, concat_axis=0, tiled=True)


def same_core():
    count = lax.axis_size("seq")
    return [list(range(c, count, 2)) for c in range(2)]


def swap_chips(array):
    return lax.all_to_all(
        array, "seq", split_axis=0, concat_axis=0, tiled=True, axis_index_groups=same_core()
    )


def flip_bit(array, axis, bit):
    return lax.ppermute(array, axis, [(i, i ^ bit) for i in range(lax.axis_size(axis))])


def swap_cores(array):
    return flip_bit(array, "seq", 1)


def from_ahead(array, step):
    count = lax.axis_size("ffn")
    return lax.ppermute(array, "ffn", [((i + step) % count, i) for i in range(count)])


def tied(array, *others):
    return lax.optimization_barrier((array, others))[0]


def add_low(a, b):
    return (a.astype(F32) + b.astype(F32)).astype(BF16)


def shards(
    stream_one,
    stream_two,
    doc_lengths,
    bucket_ids,
    norm1_gain,
    norm1_bias,
    w_qk,
    w_value,
    w_out,
    norm2_gain,
    norm2_bias,
    w_up,
    w_down,
    grad_out_one,
    grad_out_two,
):
    rows, width = stream_one.shape[1:]
    seq, ffn = lax.axis_index("seq"), lax.axis_index("ffn")
    core = seq % 2
    gain_one, bias_one = norm1_gain.reshape(1, -1), norm1_bias.reshape(1, -1)
    gain_two, bias_two = norm2_gain.reshape(1, -1), norm2_bias.reshape(1, -1)

    msg, normed_one, keep_rows, give_rows = project(stream_two[0], gain_one, bias_one, w_qk, w_value)
    received = swap_chips(msg)
    order, bias = prepare(bucket_ids[0, 0], jnp.cumsum(doc_lengths[0]))
    top, low = [jnp.where(core == 0, w_up[at], w_down[at]) for at in (slice(0, 512), slice(512, 1024))]
    top1, low3 = from_ahead(top, 1), from_ahead(low, 3)
    received, order, bias, top, low, top1, low3 = lax.optimization_barrier(
        (received, order, bias, top, low, top1, low3)
    )
    low1, top3 = from_ahead(low, 1), from_ahead(top, 3)
    grads1, grads3 = from_ahead(grad_out_two[0], 1), from_ahead(grad_out_two[0], 3)
    other_rows = swap_cores(give_rows)
    top1_other, low3_other = swap_cores(top1), swap_cores(low3)
    sent, queries, keys, vals, probs = attend(order, received, swap_cores(received), bias)
    (sent, top1, low3, low1, top3, grads1, grads3, grad_rows, top1_other, low3_other) = lax.optimization_barrier(
        (sent, top1, low3, low1, top3, grads1, grads3, grad_out_two[0], top1_other, low3_other)
    )
    per_round = swap_seq(sent)
    top2, low2 = from_ahead(top1, 1), from_ahead(low3, 3)
    grads2 = from_ahead(grad_rows, 2)
    low1_other, top3_other = swap_cores(low1), swap_cores(top3)
    per_round, top2, low2, low1_other, top3_other, grads2 = lax.optimization_barrier(
        (per_round, top2, low2, low1_other, top3_other, grads2)
    )
    mine = [top1, low1, top2, low2, top3, low3]
    other = [top1_other, low1_other, swap_cores(top2), swap_cores(low2), top3_other, low3_other]
    mix, low_mix, first, one_low, normed_two, weights = combine(per_round, stream_one[0], w_out, gain_two, bias_two)
    normed_far = [from_ahead(normed_two, k) for k in (1, 2, 3)]
    two_low, grad_first, msg, grad_gain_two, grad_bias_two, keep_mix, give_mix, low_first, hid0, pre0 = middle(
        mix,
        low_mix,
        first,
        normed_two,
        weights,
        stream_two[0],
        grad_out_one[0],
        grad_rows,
        w_out,
        gain_two,
        w_up,
        w_down,
        mine,
        other,
    )
    far = swap_seq(msg)
    keep_feed, give_feed = feed(normed_two, grad_rows, hid0, pre0, normed_far, [grads1, grads2, grads3], w_up, w_down)
    part_out = pair(keep_mix, swap_cores(give_mix), low_first, swap_cores(low_first))
    part_feed = add_low(keep_feed, swap_cores(give_feed))
    far, part_feed, part_out = lax.optimization_barrier((far, part_feed, part_out))
    near_feed = swap_chips(jnp.concatenate([part_feed, part_out], axis=2))

    keep_v, give_v, grad_dots = back_value(order, far, vals, probs)
    keep_q, give_q = back_query(order, grad_dots, queries, keys)
    came_v, came_q = swap_cores(give_v), swap_cores(give_q)
    back = swap_chips(jnp.concatenate([add_low(keep_q, came_q), add_low(keep_v, came_v)], axis=2))
    grads = sum_rounds(back)
    grads_other = swap_cores(grads)
    near_feed = near_feed.astype(F32).sum(axis=0)
    grad_second, small = finish(
        grads, stream_two[0], gain_one, w_qk, w_value, grad_out_two[0], grad_gain_two, grad_bias_two
    )
    part = pair(keep_rows, other_rows, grads, grads_other, small)
    near = swap_chips(part).astype(F32).sum(axis=0)
    near = jnp.concatenate([near, near_feed[:, 2048:]], axis=1).reshape(4, 8, -1)
    whole = lax.dynamic_index_in_dim(near, ffn, 0, keepdims=False)
    for k in (1, 2, 3):
        whole = whole + from_ahead(lax.dynamic_index_in_dim(near, (ffn + 4 - k) % 4, 0, keepdims=False), k)
    small = whole[:, 2 * width : 2 * width + 128]
    lines = small[:, :8] + swap_cores(small)[:, 8:16]
    lines = lines[:, 0::2] + lines[:, 1::2]
    return (
        one_low[None],
        two_low[None],
        grad_first[None],
        grad_second[None],
        lines[:, 0],
        lines[:, 1],
        whole[:, :width],
        whole[:, width : 2 * width],
        whole[:, 2 * width + 128 :],
        lines[:, 2],
        lines[:, 3],
        near_feed[:, :1024],
        near_feed[:, 1024:2048],
    )


def solution(mesh):
    return jax.shard_map(
        shards,
        mesh=mesh,
        in_specs=(
            P("ffn", "seq", None),
            P("ffn", "seq", None),
            P("ffn", None),
            P("ffn", "seq", None),
            P(),
            P(),
            P(),
            P(),
            P(),
            P(),
            P(),
            P(None, "ffn"),
            P(None, "ffn"),
            P("ffn", "seq", None),
            P("ffn", "seq", None),
        ),
        out_specs=(
            P("ffn", "seq", None),
            P("ffn", "seq", None),
            P("ffn", "seq", None),
            P("ffn", "seq", None),
            P(("seq", "ffn")),
            P(("seq", "ffn")),
            P(("seq", "ffn"), None),
            P(("seq", "ffn"), None),
            P(("seq", "ffn"), None),
            P(("seq", "ffn")),
            P(("seq", "ffn")),
            P("seq", "ffn"),
            P("seq", "ffn"),
        ),
        check_vma=False,
    )
```

time: 710 us -> 451 us (0.64)
  blocking collectives: 135 us -> 0 us
  waiting for transfers between devices: 239 us -> 172 us
  matrix products: 45.2 us -> 0 us
  between operations: 14.8 us -> 1.56 us
  local copies, waits for them, and re-layouts: 1.77 us -> 13.3 us
    unnamed x1 -> x0, blocking collectives: 96.7 us -> none
    all_to_all x11 -> x6, waiting for transfers between devices: 191 us -> 110 us  [the longest x4 92 us: swap_chips(): lax.all_to_all(array, 'seq', split_axis=0, concat_axis=0, tiled=True, axi...]
    ppermute x0 -> x30, waiting for transfers between devices: none -> 61.9 us  [the longest x15 57.5 us: from_ahead(): lax.ppermute(array, 'ffn', [((i + step) % count, i) for i in range(count)])]
    all_gather x2 -> x0, waiting for transfers between devices: 47.4 us -> none  [the longest x1 28.9 us: shards(): gathered = lax.all_gather(normed_two, 'ffn', axis=0, tiled=True)]
    dot_general x7 -> x0, matrix products: 45.2 us -> none  [the longest x1 14.1 us: shards(): pre_act = jnp.dot(gathered, w_up, preferred_element_type=F32)]
    all_to_all x1 -> x0, blocking collectives: 38.2 us -> none  [swap(): return lax.all_to_all(array, axis, split_axis=0, concat_axis=0, tiled=True)]
    ppermute x0 -> x30, starting transfers between devices: none -> 36.6 us  [the longest x15 18.8 us: from_ahead(): lax.ppermute(array, 'ffn', [((i + step) % count, i) for i in range(count)])]
    all_to_all x11 -> x6, starting transfers between devices: 69.8 us -> 34.9 us  [the longest x4 20.7 us: swap_chips(): lax.all_to_all(array, 'seq', split_axis=0, concat_axis=0, tiled=True, axi...]
  transfers between devices with their start and end apart: 13 -> 36, of which waited for: 10 -> 13; matrix products, arithmetic and copies ran while one was open for 9% -> 5% of each run, Pallas kernels for 11% -> 24%
where the time goes in v2:
time: 451 us; the launch traced here: 443 us
  waiting for transfers between devices  172 us (38%)
  Pallas kernels  158 us (35%)
  starting transfers between devices  71.5 us (16%)
  other arithmetic  26.1 us (6%)
  local copies, waits for them, and re-layouts  13.3 us (3%)
    all_to_all x4, waiting for transfers between devices, swap_chips(): lax.all_to_all(array, 'seq', split_axis=0, concat_axis=0, tiled=True, axi...  92 us
    ppermute x15, waiting for transfers between devices, from_ahead(): lax.ppermute(array, 'ffn', [((i + step) % count, i) for i in range(count)])  57.5 us
    pallas_call x1, Pallas kernels, attend(): pl.pallas_call(attend_kernel, out_shape=[sd((length // 256, 256 + EXTRA,...  37.3 us
    pallas_call x1, Pallas kernels, middle(): pl.pallas_call(middle_kernel, out_shape=[sd((rows, width), BF16), sd((row...  28.4 us
    pallas_call x1, Pallas kernels, back_value(): pl.pallas_call(back_value_kernel, out_shape=[sd((half, 256, DH), BF16)] *...  25.6 us
    pallas_call x1, Pallas kernels, feed(): pl.pallas_call(feed_kernel, out_shape=[sd((width // 64, 32, 2048), BF16)]...  20.7 us
    all_to_all x4, starting transfers between devices, swap_chips(): lax.all_to_all(array, 'seq', split_axis=0, concat_axis=0, tiled=True, axi...  20.7 us
    ppermute x15, starting transfers between devices, from_ahead(): lax.ppermute(array, 'ffn', [((i + step) % count, i) for i in range(count)])  18.8 us
  transfers between devices with their start and end apart: 36, of which 13 were waited for; matrix products, arithmetic and copies ran while one was open for 5% of the time, Pallas kernels for 24%

profile of v2, /device:TPU:1, one launch (start us, length us, event | category | flops | bytes accessed | tf_op | source)
XLA Modules:
  0.0 442.8 jit_solution(3778117074611838319)
XLA Ops:
  0.6 6.9 %project.1 = (bf16[16,256,256]{2,1,0:T(8,128)(2,1)}, bf16[256,1024]{1,0:T(8,128)(2,1)}, bf16[16,32,256]{2,1,0:T(8,128)(2,1)}, bf16[16,32,256]{2,1,0:T(8,128)(2,1)}) custom-call(bf16[256,1024]{1,0:T(8,128)(2,1)} %bitcast.44, f32[1,1024]{1,0:T(1,128)} %bitcast.59, f32[1,1024]{1,0:T(1,128)} %bitcast.61, bf16[1024,1024]{1,0:T(8,128)(2,1)} %w_qk.3, ...), custom_call_target="tpu_custom_call" | custom-call | bytes 24500000 | tf_op jit(solution)/shard_map/project/pallas_call | solution.py:89
  7.5 7.8 %all-to-all-start = ((bf16[16,256,256]{2,1,0:T(8,128)(2,1)}), bf16[16,256,256]{2,1,0:T(8,128)(2,1)}, u32[]{:S(2)}, u32[]{:S(2)}) async-start(bf16[16,256,256]{2,1,0:T(8,128)(2,1)} %get-tuple-element.73), calls=%async_computation | async-start | bytes 4194304 | tf_op jit(solution)/shard_map/all_to_all | solution.py:726
  15.4 3.1 slice_select_fusion
  18.4 3.8 collective-permute-start
  22.2 6.8 %sort.15 = (s32[8192]{0:T(1024)}, s32[8192]{0:T(1024)S(1)}) sort(s32[8192]{0:T(1024)S(1)} %iota_add_fusion, s32[8192]{0:T(1024)S(1)} %iota.6), dimensions={0}, to_apply=%region_0.1 | sort | flops 106496 | bytes 131072 | tf_op jit(solution)/shard_map/sort | solution.py:406
  29.9 4.5 %select_convert_fusion.bias = bf16[8192,128]{1,0:T(8,128)(2,1)} fusion(s32[8192]{0:T(1024)S(1)} %get-tuple-element.75.order, s32[8192]{0:T(1024)S(1)} %ge.20, s32[128,128]{1,0:T(8,128)S(1)} %pad_add_fusion), kind=kLoop, calls=%fused_computation.6 | loop fusion | flops 7340032 | bytes 2228224 | tf_op jit(solution)/shard_map/convert_element_type | solution.py:412
  34.4 9.6 %collective-permute-done.refs_12_ = bf16[512,1024]{1,0:T(8,128)(2,1)S(1)} collective-permute-done((bf16[512,1024]{1,0:T(8,128)(2,1)}, bf16[512,1024]{1,0:T(8,128)(2,1)S(1)}, u32[]{:S(2)}, u32[]{:S(2)}) %collective-permute-start) | collective-permute-done | bytes 1048608 | tf_op jit(solution)/shard_map/ppermute | solution.py:741
  44.0 3.1 collective-permute-done.1.refs_17_
  47.1 1.0 copy-done.9
  48.1 2.1 collective-permute-start.2
  50.2 1.5 collective-permute-start.5
  51.9 1.3 collective-permute-start.4
  53.2 0.8 collective-permute-start.7
  54.0 9.7 %collective-permute-done.5.g1 = bf16[256,1024]{1,0:T(8,128)(2,1)S(1)} collective-permute-done((bf16[256,1024]{1,0:T(8,128)(2,1)S(1)}, bf16[256,1024]{1,0:T(8,128)(2,1)S(1)}, u32[]{:S(2)}, u32[]{:S(2)}) %collective-permute-start.5) | collective-permute-done | bytes 524320 | tf_op jit(solution)/shard_map/ppermute | solution.py:741
  63.8 1.2 collective-permute-start.8
  65.2 1.1 copy-done.6
  66.3 37.3 %attend.1 = (bf16[32,272,128]{2,1,0:T(8,128)(2,1)}, bf16[8192,128]{1,0:T(8,128)(2,1)}, bf16[8256,128]{1,0:T(8,128)(2,1)}, bf16[8256,128]{1,0:T(8,128)(2,1)}, bf16[8192,128]{1,0:T(8,128)(2,1)}) custom-call(s32[8192]{0:T(1024)} %copy-done.7, bf16[16,256,256]{2,1,0:T(8,128)(2,1)} %all-to-all-done.mine, bf16[16,256,256]{2,1,0:T(8,128)(2,1)} %copy-done.6, ...), custom_call_target="tpu_custom_call" | custom-call | bytes 129500000 | tf_op jit(solution)/shard_map/attend/pallas_call | solution.py:222
  103.7 0.8 copy-done.17
  104.5 7.0 %all-to-all-start.1 = ((bf16[32,272,128]{2,1,0:T(8,128)(2,1)}), bf16[32,272,128]{2,1,0:T(8,128)(2,1)S(1)}, u32[]{:S(2)}, u32[]{:S(2)}) async-start(bf16[32,272,128]{2,1,0:T(8,128)(2,1)} %get-tuple-element.83), calls=%async_computation.1 | async-start | bytes 4456448 | tf_op jit(solution)/shard_map/all_to_all | solution.py:717
  111.5 2.3 collective-permute-start.9
  114.4 2.0 collective-permute-start.13
  116.4 33.4 %collective-permute-done.13.g2 = bf16[256,1024]{1,0:T(8,128)(2,1)S(1)} collective-permute-done((bf16[256,1024]{1,0:T(8,128)(2,1)S(1)}, bf16[256,1024]{1,0:T(8,128)(2,1)S(1)}, u32[]{:S(2)}, u32[]{:S(2)}) %collective-permute-start.13) | collective-permute-done | bytes 524320 | tf_op jit(solution)/shard_map/ppermute | solution.py:741
  149.9 0.8 copy-done.18
  151.4 1.0 copy-done.12
  152.4 1.7 collective-permute-start.14
  154.2 6.3 %combine.1 = (f32[256,1024]{1,0:T(8,128)}, bf16[256,1024]{1,0:T(8,128)(2,1)}, f32[256,1024]{1,0:T(8,128)}, bf16[256,1024]{1,0:T(8,128)(2,1)}, bf16[256,1024]{1,0:T(8,128)(2,1)}, /*index=5*/f32[256,128]{1,0:T(8,128)}) custom-call(bf16[32,272,128]{2,1,0:T(8,128)(2,1)} %copy-done.1, bf16[256,1024]{1,0:T(8,128)(2,1)} %bitcast.54, bf16[1024,1024]{1,0:T(8,128)(2,1)} %refs_8_.1, ...), custom_call_target="tpu_custom_call" | custom-call | bytes 21000000 | tf_op jit(solution)/shard_map/combine/pallas_call | solution.py:447
  161.5 1.0 collective-permute-start.18
  162.6 1.0 copy-done.13
  163.6 28.4 %middle.1 = (bf16[256,1024]{1,0:T(8,128)(2,1)}, f32[256,1024]{1,0:T(8,128)}, bf16[32,272,128]{2,1,0:T(8,128)(2,1)}, f32[1,1024]{1,0:T(1,128)}, f32[1,1024]{1,0:T...) custom-call(f32[256,1024]{1,0:T(8,128)} %get-tuple-element.91.refs_0, ...), custom_call_target="tpu_custom_call" | custom-call | bytes 87500000 | tf_op jit(solution)/shard_map/middle/pallas_call | solution.py:560
  192.0 0.7 copy-done.20
  193.1 20.7 %feed.1 = (bf16[16,32,2048]{2,1,0:T(8,128)(2,1)}, bf16[16,32,2048]{2,1,0:T(8,128)(2,1)}) custom-call(bf16[256,1024]{1,0:T(8,128)(2,1)} %get-tuple-element.94.refs_3_.normed, bf16[256,1024]{1,0:T(8,128)(2,1)} %bitcast.48, bf16[256,1024]{1,0:T(8,128)(2,1)} %get-tuple-element.105.hid0, bf16[256,1024]{1,0:T(8,128)(2,1)} %get-tuple-element.106.pre0, ...), custom_call_target="tpu_custom_call" | custom-call | bytes 63000000 | tf_op jit(solution)/shard_map/feed/pallas_call | solution.py:623
  213.8 1.9 collective-permute-start.19
  215.7 7.3 %all-to-all-start.2 = ((bf16[32,272,128]{2,1,0:T(8,128)(2,1)}), bf16[32,272,128]{2,1,0:T(8,128)(2,1)S(1)}, u32[]{:S(2)}, u32[]{:S(2)}) async-start(bf16[32,272,128]{2,1,0:T(8,128)(2,1)} %get-tuple-element.104), calls=%async_computation.2 | async-start | bytes 4456448 | tf_op jit(solution)/shard_map/all_to_all | solution.py:717
  223.8 1.5 collective-permute-done.20.left_other
  225.4 0.7 copy-done.25
  226.2 3.1 pair.2
  229.3 4.5 %add_convert_fusion = bf16[16,32,2048]{2,1,0:T(8,128)(2,1)} fusion(bf16[16,32,2048]{2,1,0:T(8,128)(2,1)} %collective-permute-done.19, bf16[16,32,2048]{2,1,0:T(8,128)(2,1)} %get-tuple-element.110), kind=kLoop, calls=%fused_computation.5 | loop fusion | flops 4194304 | bytes 6291456 | tf_op jit(solution)/shard_map/convert_element_type | solution.py:749
  233.9 18.4 %all-to-all-done.2.msg = bf16[32,272,128]{2,1,0:T(8,128)(2,1)S(1)} async-done(((bf16[32,272,128]{2,1,0:T(8,128)(2,1)}), bf16[32,272,128]{2,1,0:T(8,128)(2,1)S(1)}, u32[]{:S(2)}, u32[]{:S(2)}) %all-to-all-start.2) | async-done | bytes 2228256 | tf_op jit(solution)/shard_map/all_to_all | solution.py:717
  252.2 1.4 copy-done.2
  253.6 25.6 %back_value.1 = (bf16[16,256,128]{2,1,0:T(8,128)(2,1)}, bf16[16,256,128]{2,1,0:T(8,128)(2,1)}, bf16[8192,128]{1,0:T(8,128)(2,1)}) custom-call(s32[8192]{0:T(1024)} %copy-done.7, bf16[32,272,128]{2,1,0:T(8,128)(2,1)} %copy-done.2, bf16[8256,128]{1,0:T(8,128)(2,1)} %get-tuple-element.116.vals, bf16[8192,128]{1,0:T(8,128)(2,1)} %get-tuple-element.117.probs), custom_call_target="tpu_custom_call" | custom-call | bytes 91000000 | tf_op jit(solution)/shard_map/back_value/pallas_call | solution.py:314
  279.2 2.5 collective-permute-start.23
  281.7 16.9 %back_query.1 = (bf16[16,256,128]{2,1,0:T(8,128)(2,1)}, bf16[16,256,128]{2,1,0:T(8,128)(2,1)}) custom-call(s32[8192]{0:T(1024)} %copy-done.7, bf16[8192,128]{1,0:T(8,128)(2,1)} %get-tuple-element.118.gd, bf16[8192,128]{1,0:T(8,128)(2,1)} %get-tuple-element.119.q_in, bf16[8256,128]{1,0:T(8,128)(2,1)} %get-tuple-element.120.keys), custom_call_target="tpu_custom_call" | custom-call | bytes 59500000 | tf_op jit(solution)/shard_map/back_query/pallas_call | solution.py:389
  299.0 2.6 collective-permute-done.22
  301.8 1.6 pad_maximum_fusion.1
  303.5 4.7 %all-to-all-start.3 = ((bf16[16,256,256]{2,1,0:T(8,128)(2,1)}), bf16[16,256,256]{2,1,0:T(8,128)(2,1)}, u32[]{:S(2)}, u32[]{:S(2)}) async-start(bf16[16,256,256]{2,1,0:T(8,128)(2,1)} %pad_maximum_fusion.1), calls=%async_computation.3 | async-start | bytes 4194304 | tf_op jit(solution)/shard_map/all_to_all | solution.py:726
  308.2 1.9 pad_maximum_fusion
  310.1 31.7 %all-to-all-done.3.back = bf16[16,256,256]{2,1,0:T(8,128)(2,1)} async-done(((bf16[16,256,256]{2,1,0:T(8,128)(2,1)}), bf16[16,256,256]{2,1,0:T(8,128)(2,1)}, u32[]{:S(2)}, u32[]{:S(2)}) %all-to-all-start.3) | async-done | bytes 2097184 | tf_op jit(solution)/shard_map/all_to_all | solution.py:726
  341.8 3.7 all-to-all-start.5
  345.5 2.9 sum_rounds.1.grads.right
  348.5 1.0 collective-permute-start.25
  349.5 5.7 %finish.1 = (f32[256,1024]{1,0:T(8,128)}, bf16[16,32,128]{2,1,0:T(8,128)(2,1)}) custom-call(bf16[256,2048]{1,0:T(8,128)(2,1)} %sum_rounds.1.grads.right, bf16[256,1024]{1,0:T(8,128)(2,1)} %bitcast.46, f32[1,1024]{1,0:T(1,128)} %bitcast.60, bf16[1024,1024]{1,0:T(8,128)(2,1)} %w_qk.3, bf16[1024,1024]{1,0:T(8,128)(2,1)} %w_value.3, bf16[256,1024]{1,0:T(8,128)(2,1)} %bitcast.49, ...), custom_call_target="tpu_custom_call" | custom-call | bytes 17500000 | tf_op jit(solution)/shard_map/finish/pallas_call | solution.py:680
  355.2 0.7 copy-done.24
  355.9 4.3 pair.3
  360.2 31.9 %all-to-all-done.5 = bf16[16,32,3072]{2,1,0:T(8,128)(2,1)S(1)} async-done(((bf16[16,32,3072]{2,1,0:T(8,128)(2,1)}), bf16[16,32,3072]{2,1,0:T(8,128)(2,1)S(1)}, u32[]{:S(2)}, u32[]{:S(2)}) %all-to-all-start.5) | async-done | bytes 3145760 | tf_op jit(solution)/shard_map/all_to_all | solution.py:726
  392.1 4.4 %all-to-all-start.4 = ((bf16[16,32,2176]{2,1,0:T(8,128)(2,1)}), bf16[16,32,2176]{2,1,0:T(8,128)(2,1)}, u32[]{:S(2)}, u32[]{:S(2)}) async-start(bf16[16,32,2176]{2,1,0:T(8,128)(2,1)} %pair.3), calls=%async_computation.4 | async-start | bytes 4456448 | tf_op jit(solution)/shard_map/all_to_all | solution.py:726
  397.1 0.7 fusion.3
  397.9 28.4 %all-to-all-done.4 = bf16[16,32,2176]{2,1,0:T(8,128)(2,1)} async-done(((bf16[16,32,2176]{2,1,0:T(8,128)(2,1)}), bf16[16,32,2176]{2,1,0:T(8,128)(2,1)}, u32[]{:S(2)}, u32[]{:S(2)}) %all-to-all-start.4) | async-done | bytes 2228256 | tf_op jit(solution)/shard_map/all_to_all | solution.py:726
  426.3 2.0 convert_reduce_fusion.1
  428.3 1.4 collective-permute-start.28
  429.7 2.1 collective-permute-start.27
  431.8 2.0 collective-permute-start.26
  433.8 1.1 collective-permute-done.27
  435.5 5.1 %collective-permute-start.29 = (f32[8,128]{1,0:T(8,128)S(1)}, f32[8,128]{1,0:T(8,128)S(1)}, u32[]{:S(2)}, u32[]{:S(2)}) collective-permute-start(f32[8,128]{1,0:T(8,128)S(1)} %slice.105), channel_id=1, source_target_pairs={{0,4},{4,0},{8,12},{12,8},{16,20},{20,16},{24,28},{28,24},{32,36},... | collective-permute-start | bytes 12296 | tf_op jit(solution)/shard_map/ppermute | solution.py:732
  441.6 0.7 slice_reduce_fusion
  (112 shorter events, 8.0 us)
Async XLA Ops:
  7.5 7.8 %copy-start = (bf16[1024,1024]{1,0:T(8,128)(2,1)S(1)}, bf16[1024,1024]{1,0:T(8,128)(2,1)}, u32[]{:S(2)}) copy-start(bf16[1024,1024]{1,0:T(8,128)(2,1)} %up.1) | copy-start | bytes 6291460
  7.5 40.6 %all-to-all-start = ((bf16[16,256,256]{2,1,0:T(8,128)(2,1)}), bf16[16,256,256]{2,1,0:T(8,128)(2,1)}, u32[]{:S(2)}, u32[]{:S(2)}) async-start(bf16[16,256,256]{2,1,0:T(8,128)(2,1)} %get-tuple-element.73), calls=%async_computation | async-start | bytes 4194304 | tf_op jit(solution)/shard_map/all_to_all | solution.py:726
  15.3 6.9 %copy-start.26 = (s32[1,1,8192]{2,1,0:T(1,128)S(1)}, s32[1,1,8192]{2,1,0:T(1,128)}, u32[]{:S(2)}) copy-start(s32[1,1,8192]{2,1,0:T(1,128)} %param.18) | copy-start | bytes 98308
  15.3 13.8 %copy-start.29 = (s32[1,9]{1,0:T(1,128)S(1)}, s32[1,9]{1,0:T(1,128)}, u32[]{:S(2)}) copy-start(s32[1,9]{1,0:T(1,128)} %param.17) | copy-start | bytes 112
  18.4 31.7 %copy-start.4 = (bf16[1,256,1024]{2,1,0:T(8,128)(2,1)S(1)}, bf16[1,256,1024]{2,1,0:T(8,128)(2,1)}, u32[]{:S(2)}) copy-start(bf16[1,256,1024]{2,1,0:T(8,128)(2,1)} %param.29) | copy-start | bytes 1572868
  18.4 25.6 %collective-permute-start = (bf16[512,1024]{1,0:T(8,128)(2,1)}, bf16[512,1024]{1,0:T(8,128)(2,1)S(1)}, u32[]{:S(2)}, u32[]{:S(2)}) collective-permute-start(bf16[512,1024]{1,0:T(8,128)(2,1)} %get-tuple-element.82), channel_id=1, source_target_pairs={{1,0},{2,1},{3,2},{0,3},{5,4},{6,5},{7,6},{4,7},{9,8},{10,9},{11,1... | collective-permute-start | bytes 3145736 | tf_op jit(solution)/shard_map/ppermute | solution.py:741
  22.2 24.9 %collective-permute-start.1 = (bf16[512,1024]{1,0:T(8,128)(2,1)}, bf16[512,1024]{1,0:T(8,128)(2,1)S(1)}, u32[]{:S(2)}, u32[]{:S(2)}) collective-permute-start(bf16[512,1024]{1,0:T(8,128)(2,1)} %get-tuple-element.81), channel_id=1, source_target_pairs={{3,0},{0,1},{1,2},{2,3},{7,4},{4,5},{5,6},{6,7},{11,8},{8,9},{9,10... | collective-permute-start | bytes 3145736 | tf_op jit(solution)/shard_map/ppermute | solution.py:741
  29.0 36.1 %copy-start.7 = (s32[8192]{0:T(1024)}, s32[8192]{0:T(1024)S(1)}, u32[]{:S(2)}) copy-start(s32[8192]{0:T(1024)S(1)} %get-tuple-element.75.order) | copy-start | bytes 98308
  44.0 3.1 copy-start.8
  47.1 1.0 copy-start.9
  48.1 16.9 %collective-permute-start.2 = (bf16[16,256,256]{2,1,0:T(8,128)(2,1)}, bf16[16,256,256]{2,1,0:T(8,128)(2,1)S(1)}, u32[]{:S(2)}, u32[]{:S(2)}) collective-permute-start(bf16[16,256,256]{2,1,0:T(8,128)(2,1)} %all-to-all-done.mine), channel_id=1, source_target_pairs={{0,4},{4,0},{8,12},{12,8},{16,20},{20,16},{24,28},{28,24},{32,36},... | collective-permute-start | bytes 6291464 | tf_op jit(solution)/shard_map/ppermute | solution.py:732
  50.2 13.6 %collective-permute-start.5 = (bf16[256,1024]{1,0:T(8,128)(2,1)S(1)}, bf16[256,1024]{1,0:T(8,128)(2,1)S(1)}, u32[]{:S(2)}, u32[]{:S(2)}) collective-permute-start(bf16[256,1024]{1,0:T(8,128)(2,1)S(1)} %bitcast.50), channel_id=1, source_target_pairs={{1,0},{2,1},{3,2},{0,3},{5,4},{6,5},{7,6},{4,7},{9,8},{10,9},{11,1... | collective-permute-start | bytes 1572872 | tf_op jit(solution)/shard_map/ppermute | solution.py:741
  51.7 51.9 %collective-permute-start.3 = (bf16[512,1024]{1,0:T(8,128)(2,1)}, bf16[512,1024]{1,0:T(8,128)(2,1)}, u32[]{:S(2)}, u32[]{:S(2)}) collective-permute-start(bf16[512,1024]{1,0:T(8,128)(2,1)} %get-tuple-element.81), channel_id=1, source_target_pairs={{1,0},{2,1},{3,2},{0,3},{5,4},{6,5},{7,6},{4,7},{9,8},{10,9},{11,1... | collective-permute-start | bytes 3145736 | tf_op jit(solution)/shard_map/ppermute | solution.py:741
  51.9 51.8 %collective-permute-start.4 = (bf16[512,1024]{1,0:T(8,128)(2,1)}, bf16[512,1024]{1,0:T(8,128)(2,1)}, u32[]{:S(2)}, u32[]{:S(2)}) collective-permute-start(bf16[512,1024]{1,0:T(8,128)(2,1)} %get-tuple-element.82), channel_id=1, source_target_pairs={{3,0},{0,1},{1,2},{2,3},{7,4},{4,5},{5,6},{6,7},{11,8},{8,9},{9,10... | collective-permute-start | bytes 3145736 | tf_op jit(solution)/shard_map/ppermute | solution.py:741
  53.2 50.5 %collective-permute-start.7 = (bf16[512,1024]{1,0:T(8,128)(2,1)}, bf16[512,1024]{1,0:T(8,128)(2,1)}, u32[]{:S(2)}, u32[]{:S(2)}) collective-permute-start(bf16[512,1024]{1,0:T(8,128)(2,1)} %copy-done.8), channel_id=1, source_target_pairs={{0,4},{4,0},{8,12},{12,8},{16,20},{20,16},{24,28},{28,24},{32,36},... | collective-permute-start | bytes 3145736 | tf_op jit(solution)/shard_map/ppermute | solution.py:732
  63.8 39.9 %copy-start.16 = (bf16[256,1024]{1,0:T(8,128)(2,1)}, bf16[256,1024]{1,0:T(8,128)(2,1)S(1)}, u32[]{:S(2)}) copy-start(bf16[256,1024]{1,0:T(8,128)(2,1)S(1)} %collective-permute-done.5.g1) | copy-start | bytes 1572868
  63.8 39.9 %collective-permute-start.8 = (bf16[512,1024]{1,0:T(8,128)(2,1)}, bf16[512,1024]{1,0:T(8,128)(2,1)}, u32[]{:S(2)}, u32[]{:S(2)}) collective-permute-start(bf16[512,1024]{1,0:T(8,128)(2,1)} %copy-done.9), channel_id=1, source_target_pairs={{0,4},{4,0},{8,12},{12,8},{16,20},{20,16},{24,28},{28,24},{32,36},... | collective-permute-start | bytes 3145736 | tf_op jit(solution)/shard_map/ppermute | solution.py:732
  65.0 1.3 copy-start.6
  65.0 38.7 %collective-permute-start.6 = (bf16[256,1024]{1,0:T(8,128)(2,1)S(1)}, bf16[256,1024]{1,0:T(8,128)(2,1)S(1)}, u32[]{:S(2)}, u32[]{:S(2)}) collective-permute-start(bf16[256,1024]{1,0:T(8,128)(2,1)S(1)} %bitcast.51), channel_id=1, source_target_pairs={{3,0},{0,1},{1,2},{2,3},{7,4},{4,5},{5,6},{6,7},{11,8},{8,9},{9,10... | collective-permute-start | bytes 1572872 | tf_op jit(solution)/shard_map/ppermute | solution.py:741
  103.6 0.9 copy-start.17
  104.5 47.9 %all-to-all-start.1 = ((bf16[32,272,128]{2,1,0:T(8,128)(2,1)}), bf16[32,272,128]{2,1,0:T(8,128)(2,1)S(1)}, u32[]{:S(2)}, u32[]{:S(2)}) async-start(bf16[32,272,128]{2,1,0:T(8,128)(2,1)} %get-tuple-element.83), calls=%async_computation.1 | async-start | bytes 4456448 | tf_op jit(solution)/shard_map/all_to_all | solution.py:717
  111.5 38.3 %collective-permute-start.9 = (bf16[512,1024]{1,0:T(8,128)(2,1)}, bf16[512,1024]{1,0:T(8,128)(2,1)S(1)}, u32[]{:S(2)}, u32[]{:S(2)}) collective-permute-start(bf16[512,1024]{1,0:T(8,128)(2,1)} %copy-done.8), channel_id=1, source_target_pairs={{1,0},{2,1},{3,2},{0,3},{5,4},{6,5},{7,6},{4,7},{9,8},{10,9},{11,1... | collective-permute-start | bytes 3145736 | tf_op jit(solution)/shard_map/ppermute | solution.py:741
  113.9 36.0 %collective-permute-start.10 = (bf16[512,1024]{1,0:T(8,128)(2,1)}, bf16[512,1024]{1,0:T(8,128)(2,1)S(1)}, u32[]{:S(2)}, u32[]{:S(2)}) collective-permute-start(bf16[512,1024]{1,0:T(8,128)(2,1)} %copy-done.9), channel_id=1, source_target_pairs={{3,0},{0,1},{1,2},{2,3},{7,4},{4,5},{5,6},{6,7},{11,8},{8,9},{9,10... | collective-permute-start | bytes 3145736 | tf_op jit(solution)/shard_map/ppermute | solution.py:741
  113.9 36.0 %collective-permute-start.11 = (bf16[512,1024]{1,0:T(8,128)(2,1)}, bf16[512,1024]{1,0:T(8,128)(2,1)S(1)}, u32[]{:S(2)}, u32[]{:S(2)}) collective-permute-start(bf16[512,1024]{1,0:T(8,128)(2,1)} %collective-permute-done.3.refs_13_), channel_id=1, source_target_pairs={{0,4},{4,0},{8,12},{12,8},{16,20},{20,16},{24,28},{28,24},{32,36},... | collective-permute-start | bytes 3145736 | tf_op jit(solution)/shard_map/ppermute | solution.py:732
  114.4 38.0 %collective-permute-start.12 = (bf16[512,1024]{1,0:T(8,128)(2,1)}, bf16[512,1024]{1,0:T(8,128)(2,1)}, u32[]{:S(2)}, u32[]{:S(2)}) collective-permute-start(bf16[512,1024]{1,0:T(8,128)(2,1)} %collective-permute-done.4.refs_16_), channel_id=1, source_target_pairs={{0,4},{4,0},{8,12},{12,8},{16,20},{20,16},{24,28},{28,24},{32,36},... | collective-permute-start | bytes 3145736 | tf_op jit(solution)/shard_map/ppermute | solution.py:732
  114.4 35.5 %collective-permute-start.13 = (bf16[256,1024]{1,0:T(8,128)(2,1)S(1)}, bf16[256,1024]{1,0:T(8,128)(2,1)S(1)}, u32[]{:S(2)}, u32[]{:S(2)}) collective-permute-start(bf16[256,1024]{1,0:T(8,128)(2,1)S(1)} %bitcast.52), channel_id=1, source_target_pairs={{2,0},{3,1},{0,2},{1,3},{6,4},{7,5},{4,6},{5,7},{10,8},{11,9},{8,1... | collective-permute-start | bytes 1572872 | tf_op jit(solution)/shard_map/ppermute | solution.py:741
  149.9 0.8 copy-start.18
  149.9 1.2 copy-start.10
  149.9 1.5 copy-start.11
  151.4 1.0 copy-start.12
  152.4 1.8 copy-start.1
  152.4 10.2 %collective-permute-start.14 = (bf16[512,1024]{1,0:T(8,128)(2,1)}, bf16[512,1024]{1,0:T(8,128)(2,1)S(1)}, u32[]{:S(2)}, u32[]{:S(2)}) collective-permute-start(bf16[512,1024]{1,0:T(8,128)(2,1)} %copy-done.10), channel_id=1, source_target_pairs={{0,4},{4,0},{8,12},{12,8},{16,20},{20,16},{24,28},{28,24},{32,36},... | collective-permute-start | bytes 3145736 | tf_op jit(solution)/shard_map/ppermute | solution.py:732
  154.1 8.4 %collective-permute-start.15 = (bf16[512,1024]{1,0:T(8,128)(2,1)}, bf16[512,1024]{1,0:T(8,128)(2,1)}, u32[]{:S(2)}, u32[]{:S(2)}) collective-permute-start(bf16[512,1024]{1,0:T(8,128)(2,1)} %copy-done.11), channel_id=1, source_target_pairs={{0,4},{4,0},{8,12},{12,8},{16,20},{20,16},{24,28},{28,24},{32,36},... | collective-permute-start | bytes 3145736 | tf_op jit(solution)/shard_map/ppermute | solution.py:732
  160.5 31.5 %collective-permute-start.16 = (bf16[256,1024]{1,0:T(8,128)(2,1)}, bf16[256,1024]{1,0:T(8,128)(2,1)S(1)}, u32[]{:S(2)}, u32[]{:S(2)}) collective-permute-start(bf16[256,1024]{1,0:T(8,128)(2,1)} %get-tuple-element.94.refs_3_.normed), channel_id=1, source_target_pairs={{1,0},{2,1},{3,2},{0,3},{5,4},{6,5},{7,6},{4,7},{9,8},{10,9},{11,1... | collective-permute-start | bytes 1572872 | tf_op jit(solution)/shard_map/ppermute | solution.py:741
  161.1 30.9 %collective-permute-start.17 = (bf16[256,1024]{1,0:T(8,128)(2,1)}, bf16[256,1024]{1,0:T(8,128)(2,1)S(1)}, u32[]{:S(2)}, u32[]{:S(2)}) collective-permute-start(bf16[256,1024]{1,0:T(8,128)(2,1)} %get-tuple-element.94.refs_3_.normed), channel_id=1, source_target_pairs={{2,0},{3,1},{0,2},{1,3},{6,4},{7,5},{4,6},{5,7},{10,8},{11,9},{8,1... | collective-permute-start | bytes 1572872 | tf_op jit(solution)/shard_map/ppermute | solution.py:741
  161.5 30.4 %collective-permute-start.18 = (bf16[256,1024]{1,0:T(8,128)(2,1)}, bf16[256,1024]{1,0:T(8,128)(2,1)S(1)}, u32[]{:S(2)}, u32[]{:S(2)}) collective-permute-start(bf16[256,1024]{1,0:T(8,128)(2,1)} %get-tuple-element.94.refs_3_.normed), channel_id=1, source_target_pairs={{3,0},{0,1},{1,2},{2,3},{7,4},{4,5},{5,6},{6,7},{11,8},{8,9},{9,10... | collective-permute-start | bytes 1572872 | tf_op jit(solution)/shard_map/ppermute | solution.py:741
  162.6 1.0 copy-start.13
  192.0 0.8 copy-start.20
  192.0 0.9 copy-start.21
  192.0 1.1 copy-start.22
  213.8 15.5 %collective-permute-start.19 = (bf16[16,32,2048]{2,1,0:T(8,128)(2,1)}, bf16[16,32,2048]{2,1,0:T(8,128)(2,1)}, u32[]{:S(2)}, u32[]{:S(2)}) collective-permute-start(bf16[16,32,2048]{2,1,0:T(8,128)(2,1)} %get-tuple-element.111), channel_id=1, source_target_pairs={{0,4},{4,0},{8,12},{12,8},{16,20},{20,16},{24,28},{28,24},{32,36},... | collective-permute-start | bytes 6291464 | tf_op jit(solution)/shard_map/ppermute | solution.py:732
  215.7 7.3 %copy-start.19 = (bf16[256,1024]{1,0:T(8,128)(2,1)S(1)}, bf16[256,1024]{1,0:T(8,128)(2,1)}, u32[]{:S(2)}) copy-start(bf16[256,1024]{1,0:T(8,128)(2,1)} %get-tuple-element.114.right) | copy-start | bytes 1572868
  215.7 7.6 %copy-start.28 = (bf16[16,32,256]{2,1,0:T(8,128)(2,1)S(1)}, bf16[16,32,256]{2,1,0:T(8,128)(2,1)}, u32[]{:S(2)}) copy-start(bf16[16,32,256]{2,1,0:T(8,128)(2,1)} %get-tuple-element.113) | copy-start | bytes 786436
  215.7 36.5 %all-to-all-start.2 = ((bf16[32,272,128]{2,1,0:T(8,128)(2,1)}), bf16[32,272,128]{2,1,0:T(8,128)(2,1)S(1)}, u32[]{:S(2)}, u32[]{:S(2)}) async-start(bf16[32,272,128]{2,1,0:T(8,128)(2,1)} %get-tuple-element.104), calls=%async_computation.2 | async-start | bytes 4456448 | tf_op jit(solution)/shard_map/all_to_all | solution.py:717
  223.0 2.4 collective-permute-start.21
  223.3 2.0 collective-permute-start.20
  225.3 0.9 copy-start.23
  252.2 1.4 copy-start.2
  279.2 19.5 %collective-permute-start.23 = (bf16[16,256,128]{2,1,0:T(8,128)(2,1)}, bf16[16,256,128]{2,1,0:T(8,128)(2,1)S(1)}, u32[]{:S(2)}, u32[]{:S(2)}) collective-permute-start(bf16[16,256,128]{2,1,0:T(8,128)(2,1)} %get-tuple-element.124), channel_id=1, source_target_pairs={{0,4},{4,0},{8,12},{12,8},{16,20},{20,16},{24,28},{28,24},{32,36},... | collective-permute-start | bytes 3145736 | tf_op jit(solution)/shard_map/ppermute | solution.py:732
  281.7 16.9 %copy-start.14 = (bf16[16,256,128]{2,1,0:T(8,128)(2,1)S(1)}, bf16[16,256,128]{2,1,0:T(8,128)(2,1)}, u32[]{:S(2)}) copy-start(bf16[16,256,128]{2,1,0:T(8,128)(2,1)} %get-tuple-element.123) | copy-start | bytes 3145732
  298.7 2.9 copy-start.15
  298.7 2.9 collective-permute-start.22
  303.5 4.7 %copy-start.3 = (bf16[16,32,2048]{2,1,0:T(8,128)(2,1)S(1)}, bf16[16,32,2048]{2,1,0:T(8,128)(2,1)}, u32[]{:S(2)}) copy-start(bf16[16,32,2048]{2,1,0:T(8,128)(2,1)} %add_convert_fusion) | copy-start | bytes 6291460
  303.5 4.7 %copy-start.5 = (bf16[16,32,1024]{2,1,0:T(8,128)(2,1)S(1)}, bf16[16,32,1024]{2,1,0:T(8,128)(2,1)}, u32[]{:S(2)}) copy-start(bf16[16,32,1024]{2,1,0:T(8,128)(2,1)} %pair.2) | copy-start | bytes 3145732
  303.5 38.3 %all-to-all-start.3 = ((bf16[16,256,256]{2,1,0:T(8,128)(2,1)}), bf16[16,256,256]{2,1,0:T(8,128)(2,1)}, u32[]{:S(2)}, u32[]{:S(2)}) async-start(bf16[16,256,256]{2,1,0:T(8,128)(2,1)} %pad_maximum_fusion.1), calls=%async_computation.3 | async-start | bytes 4194304 | tf_op jit(solution)/shard_map/all_to_all | solution.py:726
  341.8 50.3 %all-to-all-start.5 = ((bf16[16,32,3072]{2,1,0:T(8,128)(2,1)}), bf16[16,32,3072]{2,1,0:T(8,128)(2,1)S(1)}, u32[]{:S(2)}, u32[]{:S(2)}) async-start(bf16[16,32,3072]{2,1,0:T(8,128)(2,1)} %pad_maximum_fusion), calls=%async_computation.5 | async-start | bytes 6291456 | tf_op jit(solution)/shard_map/all_to_all | solution.py:726
  345.5 3.9 copy-start.27
  348.5 6.7 %collective-permute-start.25 = (bf16[256,2048]{1,0:T(8,128)(2,1)}, bf16[256,2048]{1,0:T(8,128)(2,1)}, u32[]{:S(2)}, u32[]{:S(2)}) collective-permute-start(bf16[256,2048]{1,0:T(8,128)(2,1)} %sum_rounds.1.grads.right), channel_id=1, source_target_pairs={{0,4},{4,0},{8,12},{12,8},{16,20},{20,16},{24,28},{28,24},{32,36},... | collective-permute-start | bytes 3145736 | tf_op jit(solution)/shard_map/ppermute | solution.py:732
  349.4 5.7 %collective-permute-start.24 = (bf16[16,32,256]{2,1,0:T(8,128)(2,1)S(1)}, bf16[16,32,256]{2,1,0:T(8,128)(2,1)S(1)}, u32[]{:S(2)}, u32[]{:S(2)}) collective-permute-start(bf16[16,32,256]{2,1,0:T(8,128)(2,1)S(1)} %copy-done.27), channel_id=1, source_target_pairs={{0,4},{4,0},{8,12},{12,8},{16,20},{20,16},{24,28},{28,24},{32,36},... | collective-permute-start | bytes 786440 | tf_op jit(solution)/shard_map/ppermute | solution.py:732
  392.1 34.2 %all-to-all-start.4 = ((bf16[16,32,2176]{2,1,0:T(8,128)(2,1)}), bf16[16,32,2176]{2,1,0:T(8,128)(2,1)}, u32[]{:S(2)}, u32[]{:S(2)}) async-start(bf16[16,32,2176]{2,1,0:T(8,128)(2,1)} %pair.3), calls=%async_computation.4 | async-start | bytes 4456448 | tf_op jit(solution)/shard_map/all_to_all | solution.py:726
  428.3 5.5 %collective-permute-start.28 = (f32[8,3200]{1,0:T(8,128)S(1)}, f32[8,3200]{1,0:T(8,128)S(1)}, u32[]{:S(2)}, u32[]{:S(2)}) collective-permute-start(f32[8,3200]{1,0:T(8,128)S(1)} %get-tuple-element.140), channel_id=1, source_target_pairs={{3,0},{0,1},{1,2},{2,3},{7,4},{4,5},{5,6},{6,7},{11,8},{8,9},{9,10... | collective-permute-start | bytes 307208 | tf_op jit(solution)/shard_map/ppermute | solution.py:741
  429.7 5.2 %collective-permute-start.27 = (f32[8,3200]{1,0:T(8,128)S(1)}, f32[8,3200]{1,0:T(8,128)S(1)}, u32[]{:S(2)}, u32[]{:S(2)}) collective-permute-start(f32[8,3200]{1,0:T(8,128)S(1)} %get-tuple-element.141), channel_id=1, source_target_pairs={{2,0},{3,1},{0,2},{1,3},{6,4},{7,5},{4,6},{5,7},{10,8},{11,9},{8,1... | collective-permute-start | bytes 307208 | tf_op jit(solution)/shard_map/ppermute | solution.py:741
  431.8 3.7 collective-permute-start.26
  435.5 5.9 %collective-permute-start.29 = (f32[8,128]{1,0:T(8,128)S(1)}, f32[8,128]{1,0:T(8,128)S(1)}, u32[]{:S(2)}, u32[]{:S(2)}) collective-permute-start(f32[8,128]{1,0:T(8,128)S(1)} %slice.105), channel_id=1, source_target_pairs={{0,4},{4,0},{8,12},{12,8},{16,20},{20,16},{24,28},{28,24},{32,36},... | collective-permute-start | bytes 12296 | tf_op jit(solution)/shard_map/ppermute | solution.py:732
  (2 other events, 1.4 us)

commit v3 on v2

--- a/solution.py
+++ b/solution.py
@@ -412,7 +412,9 @@
     return order, bias.astype(BF16).reshape(length, 2 * SPAN)
 
 
-def combine_kernel(msg, x, w_out, gain, offset, mix, low_mix, first_out, first_low, normed, weights):
+def combine_kernel(
+    msg, x, w_out, gain, offset, mix, first_out, first_low, normed, weights, keep, give, normed_a, normed_b, low_mix, turned
+):
     rows = x.shape[0]
     for half in range(2):
         logs = []
@@ -440,6 +442,10 @@
     first_out[...] = first
     first_low[...] = first.astype(BF16)
     normed[...] = layer_rows(first, gain[...], offset[...]).astype(BF16)
+    normed_a[...] = normed[: rows // 2, :]
+    normed_b[...] = normed[rows // 2 :, :]
+    turned[...] = jnp.transpose(mix[...]).astype(BF16)
+    split_by_core(turned, keep, give)
 
 
 def combine(msg, x, w_out, gain, offset):
@@ -448,18 +454,50 @@
         combine_kernel,
         out_shape=[
             sd((rows, width), F32),
-            sd((rows, width), BF16),
             sd((rows, width), F32),
             sd((rows, width), BF16),
             sd((rows, width), BF16),
             sd((rows, 128), F32),
+            sd((width // 64, 32, rows), BF16),
+            sd((width // 64, 32, rows), BF16),
+            sd((rows // 2, width), BF16),
+            sd((rows // 2, width), BF16),
         ],
         in_specs=vm(5),
-        out_specs=vm(6),
+        out_specs=vm(9),
+        scratch_shapes=[pltpu.VMEM((rows, width), BF16), pltpu.VMEM((width, rows), BF16)],
         compiler_params=params(),
         name="combine",
         cost_estimate=takes(6),
     )(msg, x, w_out, gain, offset)
+
+
+def anywhere(n):
+    return [pl.BlockSpec(memory_space=pl.ANY)] * n
+
+
+def far_copies(own, far, to, sems, first, flip, pieces):
+    out = []
+    for i in pieces:
+        dst = to.at[(i + 1) // 2, pl.ds((i - 1) % 2 * 512, 512)] if i else to.at[0]
+        src = (far[i + 5] if flip else far[i - 1]).at[pl.ds(0, 512)] if i else own
+        out.append(pltpu.make_async_copy(src, dst, sems.at[first + i]))
+    return out
+
+
+def start_copies(copies):
+    core = lax.axis_index("seq") % 2
+    for side in range(2):
+
+        @pl.when(core == side)
+        def _():
+            for c in copies(side == 1):
+                c.start()
+
+
+def wait_copies(own, far, to, sems, first, k):
+    for c in far_copies(own, far, to, sems, first, False, (2 * k - 1, 2 * k) if k else (0,)):
+        c.wait()
 
 
 def gelu_both(act, grad):
@@ -469,54 +507,60 @@
 
 
 def middle_kernel(*refs):
-    (mix, low_mix, first, normed, weights, x_two, g_one, g_two, w_out, gain, up0, down0) = refs[:12]
-    far = refs[12:24]
-    (two_low, grad_first, sent, grad_gain, grad_offset, keep_mix, give_mix, low_first, hid0, pre0) = refs[24:34]
-    (turned, up, down, hid, pre, summed, sems) = refs[34:]
-    rows = x_two.shape[0]
-    core = lax.axis_index("seq") % 2
-
-    def copies(flip):
-        out = [pltpu.make_async_copy(up0, up.at[0], sems.at[0]), pltpu.make_async_copy(down0, down.at[0], sems.at[1])]
-        for i in range(6):
-            a, b = (far[i + 6], far[i]) if flip else (far[i], far[i + 6])
-            at = pl.ds(i % 2 * 512, 512)
-            out.append(pltpu.make_async_copy(a, up.at[1 + i // 2, at], sems.at[2 + 2 * i]))
-            out.append(pltpu.make_async_copy(b, down.at[1 + i // 2, at], sems.at[3 + 2 * i]))
-        return out
-
-    @pl.when(core == 0)
-    def _():
-        for c in copies(False):
-            c.start()
-
-    @pl.when(core == 1)
-    def _():
-        for c in copies(True):
-            c.start()
-
-    for c in copies(False):
-        c.wait()
-
-    def hidden_part(i, c):
-        k = i // 4
-        at = pl.ds(pl.multiple_of((i % 4) * 256, 256), 256)
-        act = jnp.dot(normed[...], up[k, :, at], preferred_element_type=F32)
-        grad = jnp.dot(g_two[...], down[k, :, at], preferred_element_type=F32)
-        hid[k, :, at], pre[k, :, at] = gelu_both(act, grad)
+    normed, g_two, up0, down0, far = refs[0], refs[1], refs[2], refs[3], refs[4:16]
+    grad_normed, hid, pre0, up, down, pre, sems = refs[16:]
+    pieces = range(7)
+    start_copies(
+        lambda flip: far_copies(up0, far, up, sems, 0, flip, pieces)
+        + far_copies(down0, far, down, sems, 7, not flip, pieces)
+    )
+    for k in range(4):
+        wait_copies(up0, far, up, sems, 0, k)
+        wait_copies(down0, far, down, sems, 7, k)
+
+        def hidden_part(i, c):
+            for u in range(2):
+                at = pl.ds(pl.multiple_of(i * 512 + u * 256, 256), 256)
+                act = jnp.dot(normed[...], up[k, :, at], preferred_element_type=F32)
+                grad = jnp.dot(g_two[...], down[k, :, at], preferred_element_type=F32)
+                hid[k, :, at], pre[k, :, at] = gelu_both(act, grad)
+            return c
+
+        lax.fori_loop(0, 2, hidden_part, 0)
+    pre0[...] = pre[0]
+    grad_normed[...] = jnp.zeros(grad_normed.shape, F32)
+
+    def up_back(k, c):
+        grad_normed[...] += lax.dot_general(pre[k], up[k], ACROSS, preferred_element_type=F32)
         return c
 
-    lax.fori_loop(0, 16, hidden_part, 0)
-    hid0[...] = hid[0]
-    pre0[...] = pre[0]
-    summed[...] = jnp.zeros(summed.shape, F32)
-
-    def up_back(k, c):
-        summed[...] += lax.dot_general(pre[k], up[k], ACROSS, preferred_element_type=F32)
-        return c
-
     lax.fori_loop(0, 4, up_back, 0)
-    grad_x, gg, go = layer_back(first[...], summed[...], gain[...])
+
+
+def middle(normed, g_two, up0, down0, far):
+    rows, width = normed.shape
+    return pl.pallas_call(
+        middle_kernel,
+        out_shape=[sd((rows, width), F32), sd((4, rows, 1024), BF16), sd((rows, 1024), BF16)],
+        in_specs=vm(2) + anywhere(14),
+        out_specs=vm(3),
+        scratch_shapes=[
+            pltpu.VMEM((4, width, 1024), BF16),
+            pltpu.VMEM((4, width, 1024), BF16),
+            pltpu.VMEM((4, rows, 1024), BF16),
+            pltpu.SemaphoreType.DMA((14,)),
+        ],
+        compiler_params=params(),
+        name="middle",
+        cost_estimate=takes(16),
+    )(normed, g_two, up0, down0, *far)
+
+
+def uncombine_kernel(
+    grad_normed, mix, first, weights, g_one, w_out, gain, grad_first, sent, grad_gain, grad_offset, low_first
+):
+    rows = g_one.shape[0]
+    grad_x, gg, go = layer_back(first[...], grad_normed[...], gain[...])
     grad_gain[...] = gg
     grad_offset[...] = go
     grad_x = grad_x + g_one[...].astype(F32)
@@ -542,95 +586,107 @@
             tail = [p[j : j + 1] for p in low_lines + high_lines] + [blank]
             sent[h * ROUNDS + r, rows : rows + EXTRA, :] = jnp.concatenate(tail, axis=0).astype(BF16)
 
-    summed[...] = x_two[...].astype(F32)
-
-    def down_out(k, c):
-        summed[...] += lax.dot_general(hid[k], down[k], ACROSS, preferred_element_type=F32)
-        return c
-
-    lax.fori_loop(0, 4, down_out, 0)
-    two_low[...] = summed[...].astype(BF16)
-    turned[...] = jnp.transpose(low_mix[...].astype(F32)).astype(BF16)
-    split_by_core(turned, keep_mix, give_mix)
-
-
-def middle(mix, low_mix, first, normed, weights, x_two, g_one, g_two, w_out, gain, up0, down0, mine, other):
-    rows, width = x_two.shape
-    anywhere = [pl.BlockSpec(memory_space=pl.ANY)] * 14
-    return pl.pallas_call(
-        middle_kernel,
+
+def uncombine(grad_normed, mix, first, weights, g_one, w_out, gain):
+    rows, width = g_one.shape
+    return pl.pallas_call(
+        uncombine_kernel,
         out_shape=[
-            sd((rows, width), BF16),
             sd((rows, width), F32),
             sd((HEADS * ROUNDS, rows + EXTRA, DH), BF16),
             sd((1, width), F32),
             sd((1, width), F32),
-            sd((width // 64, 32, rows), BF16),
-            sd((width // 64, 32, rows), BF16),
             sd((rows, width), BF16),
-            sd((rows, 1024), BF16),
-            sd((rows, 1024), BF16),
         ],
-        in_specs=vm(10) + anywhere,
-        out_specs=vm(10),
+        in_specs=vm(7),
+        out_specs=vm(5),
+        compiler_params=params(),
+        name="uncombine",
+        cost_estimate=takes(8),
+    )(grad_normed, mix, first, weights, g_one, w_out, gain)
+
+
+def down_out_kernel(*refs):
+    hid, x, down0, far = refs[0], refs[1], refs[2], refs[3:15]
+    out, down, summed, sems = refs[15:]
+    start_copies(lambda flip: far_copies(down0, far, down, sems, 0, not flip, range(7)))
+    summed[...] = x[...].astype(F32)
+    for k in range(4):
+        wait_copies(down0, far, down, sems, 0, k)
+        summed[...] += lax.dot_general(hid[k], down[k], ACROSS, preferred_element_type=F32)
+    out[...] = summed[...].astype(BF16)
+
+
+def down_out(hid, x, down0, far):
+    rows, width = x.shape
+    return pl.pallas_call(
+        down_out_kernel,
+        out_shape=sd((rows, width), BF16),
+        in_specs=vm(2) + anywhere(13),
+        out_specs=pl.BlockSpec(memory_space=pltpu.VMEM),
         scratch_shapes=[
-            pltpu.VMEM((width, rows), BF16),
             pltpu.VMEM((4, width, 1024), BF16),
-            pltpu.VMEM((4, width, 1024), BF16),
-            pltpu.VMEM((4, rows, 1024), BF16),
-            pltpu.VMEM((4, rows, 1024), BF16),
             pltpu.VMEM((rows, width), F32),
-            pltpu.SemaphoreType.DMA((14,)),
+            pltpu.SemaphoreType.DMA((7,)),
         ],
         compiler_params=params(),
-        name="middle",
-        cost_estimate=takes(25),
-    )(mix, low_mix, first, normed, weights, x_two, g_one, g_two, w_out, gain, up0, down0, *mine, *other)
-
-
-def feed_kernel(normed, grads, hid0, pre0, n1, n2, n3, g1, g2, g3, up, down, keep, give, hid, pre, turned, total):
+        name="down_out",
+        cost_estimate=takes(6),
+    )(hid, x, down0, *far)
+
+
+def feed_kernel(normed, grads, hid_own, pre0, *refs):
+    halves, (g1, g2, g3, up, down, keep, give, hid, pre, rest, turned, total) = refs[:6], refs[6:]
+    rows = normed.shape[0]
     core = lax.axis_index("seq") % 2
-    hid[0] = hid0[...]
+    hid[0] = hid_own[0]
     pre[0] = pre0[...]
+    for i, half in enumerate(halves):
+        rest[i // 2, i % 2 * (rows // 2) : (i % 2 + 1) * (rows // 2), :] = half[...]
+    n1, n2, n3 = rest.at[0], rest.at[1], rest.at[2]
     for k, (n, g) in enumerate(((n1, g1), (n2, g2), (n3, g3)), start=1):
 
         def hidden_part(i, c):
             at = pl.ds(pl.multiple_of(i * 256, 256), 256)
             act = jnp.dot(n[...], up[:, at], preferred_element_type=F32)
-            grad = jnp.dot(g[...], down[:, at], preferred_element_type=F32)
+            grad = jnp.dot(last_rows(g, rows), down[:, at], preferred_element_type=F32)
             hid[k, :, at], pre[k, :, at] = gelu_both(act, grad)
             return c
 
         lax.fori_loop(0, 4, hidden_part, 0)
     for first, lefts, rights in ((0, (normed, n1, n2, n3), pre), (1024, (grads, g1, g2, g3), hid)):
-        left = jnp.concatenate([x[...] for x in lefts], axis=0)
+        left = jnp.concatenate([last_rows(x, rows) for x in lefts], axis=0)
         turned[...] = jnp.transpose(left.astype(F32)).astype(BF16)
 
         def piece(i, c):
             left = turned[pl.ds(pl.multiple_of(i * 256, 256), 256), :]
-            total[...] = jnp.dot(left, rights[...].reshape(4 * n1.shape[0], 1024), preferred_element_type=F32)
+            total[...] = jnp.dot(left, rights[...].reshape(4 * rows, 1024), preferred_element_type=F32)
             for out, side in ((keep, core), (give, 1 - core)):
                 for j in range(4):
-                    rows = total[pl.ds(pl.multiple_of(j * 64 + side * 32, 32), 32), :]
-                    out[i * 4 + j, :, first : first + 1024] = rows.astype(BF16)
+                    lines = total[pl.ds(pl.multiple_of(j * 64 + side * 32, 32), 32), :]
+                    out[j * 4 + i, :, first : first + 1024] = lines.astype(BF16)
             return c
 
         lax.fori_loop(0, keep.shape[0] // 4, piece, 0)
 
 
-def feed(normed, grads, hid0, pre0, normed_far, grads_far, up, down):
+def last_rows(ref, rows):
+    return ref[ref.shape[0] - rows :, :]
+
+
+def feed(normed, grads, hid_own, pre0, normed_far, grads_far, up, down):
     rows, width = normed.shape
     return pl.pallas_call(
         feed_kernel,
         out_shape=[sd((width // 64, 32, 2048), BF16)] * 2,
-        in_specs=vm(12),
+        in_specs=vm(15),
         out_specs=vm(2),
         scratch_shapes=[pltpu.VMEM((4, rows, 1024), BF16)] * 2
-        + [pltpu.VMEM((width, 4 * rows), BF16), pltpu.VMEM((256, 1024), F32)],
+        + [pltpu.VMEM((3, rows, width), BF16), pltpu.VMEM((width, 4 * rows), BF16), pltpu.VMEM((256, 1024), F32)],
         compiler_params=params(),
         name="feed",
-        cost_estimate=takes(18),
-    )(normed, grads, hid0, pre0, *normed_far, *grads_far, up, down)
+        cost_estimate=takes(20),
+    )(normed, grads, hid_own, pre0, *normed_far, *grads_far, up, down)
 
 
 def sum_rounds_kernel(back, out):
@@ -695,8 +751,9 @@
     total = jnp.dot(left[...].reshape(blocks * lines, rows), right[...], preferred_element_type=F32)
     total = total + jnp.dot(left_other[...].reshape(blocks * lines, rows), right_other[...], preferred_element_type=F32)
     out[:, :, :width] = total.astype(BF16).reshape(blocks, lines, width)
-    if len(rest) == 2:
-        out[:, :, width:] = rest[0][...]
+    for extra in rest[:-1]:
+        out[:, :, width : width + extra.shape[2]] = extra[...]
+        width += extra.shape[2]
 
 
 def pair(left, left_other, right, right_other, *extra):
@@ -720,6 +777,14 @@
 def same_core():
     count = lax.axis_size("seq")
     return [list(range(c, count, 2)) for c in range(2)]
+
+
+def along_x():
+    return [[y * 8 + x * 2 + c for x in range(4)] for y in range(4) for c in range(2)]
+
+
+def along_y():
+    return [[y * 8 + x * 2 + c for y in range(4)] for x in range(4) for c in range(2)]
 
 
 def swap_chips(array):
@@ -774,73 +839,81 @@
 
     msg, normed_one, keep_rows, give_rows = project(stream_two[0], gain_one, bias_one, w_qk, w_value)
     received = swap_chips(msg)
-    order, bias = prepare(bucket_ids[0, 0], jnp.cumsum(doc_lengths[0]))
     top, low = [jnp.where(core == 0, w_up[at], w_down[at]) for at in (slice(0, 512), slice(512, 1024))]
+    buckets, top, low = lax.optimization_barrier((bucket_ids[0, 0], top, low))
     top1, low3 = from_ahead(top, 1), from_ahead(low, 3)
+    order, bias = prepare(buckets, jnp.cumsum(doc_lengths[0]))
     received, order, bias, top, low, top1, low3 = lax.optimization_barrier(
         (received, order, bias, top, low, top1, low3)
     )
-    low1, top3 = from_ahead(low, 1), from_ahead(top, 3)
-    grads1, grads3 = from_ahead(grad_out_two[0], 1), from_ahead(grad_out_two[0], 3)
+    lowg1 = from_ahead(jnp.concatenate([low, grad_out_two[0]], axis=0), 1)
+    topg3 = from_ahead(jnp.concatenate([top, grad_out_two[0]], axis=0), 3)
     other_rows = swap_cores(give_rows)
     top1_other, low3_other = swap_cores(top1), swap_cores(low3)
     sent, queries, keys, vals, probs = attend(order, received, swap_cores(received), bias)
-    (sent, top1, low3, low1, top3, grads1, grads3, grad_rows, top1_other, low3_other) = lax.optimization_barrier(
-        (sent, top1, low3, low1, top3, grads1, grads3, grad_out_two[0], top1_other, low3_other)
+    sent, top1, low3, lowg1, topg3, top1_other, low3_other, other_rows = lax.optimization_barrier(
+        (sent, top1, low3, lowg1, topg3, top1_other, low3_other, other_rows)
     )
     per_round = swap_seq(sent)
     top2, low2 = from_ahead(top1, 1), from_ahead(low3, 3)
-    grads2 = from_ahead(grad_rows, 2)
-    low1_other, top3_other = swap_cores(low1), swap_cores(top3)
-    per_round, top2, low2, low1_other, top3_other, grads2 = lax.optimization_barrier(
-        (per_round, top2, low2, low1_other, top3_other, grads2)
+    lowg1_other, topg3_other = swap_cores(lowg1), swap_cores(topg3)
+    per_round, top2, low2, lowg1_other, topg3_other = lax.optimization_barrier(
+        (per_round, top2, low2, lowg1_other, topg3_other)
     )
-    mine = [top1, low1, top2, low2, top3, low3]
-    other = [top1_other, low1_other, swap_cores(top2), swap_cores(low2), top3_other, low3_other]
-    mix, low_mix, first, one_low, normed_two, weights = combine(per_round, stream_one[0], w_out, gain_two, bias_two)
-    normed_far = [from_ahead(normed_two, k) for k in (1, 2, 3)]
-    two_low, grad_first, msg, grad_gain_two, grad_bias_two, keep_mix, give_mix, low_first, hid0, pre0 = middle(
-        mix,
-        low_mix,
-        first,
-        normed_two,
-        weights,
-        stream_two[0],
-        grad_out_one[0],
-        grad_rows,
-        w_out,
-        gain_two,
-        w_up,
-        w_down,
-        mine,
-        other,
+    far_weights = [top1, lowg1, top2, low2, topg3, low3]
+    far_weights += [top1_other, lowg1_other, swap_cores(top2), swap_cores(low2), topg3_other, low3_other]
+    grads2 = from_ahead(topg3[512:], 3)
+    mix, first, one_low, normed_two, weights, keep_mix, give_mix, *halves = combine(per_round, stream_one[0], w_out, gain_two, bias_two)
+    ahead, behind = [from_ahead(half, 1) for half in halves], [from_ahead(half, 3) for half in halves]
+    grad_normed, hid, pre0 = middle(normed_two, grad_out_two[0], w_up, w_down, far_weights)
+    grad_normed, ahead, behind, grads2 = lax.optimization_barrier((grad_normed, ahead, behind, grads2))
+    normed_far = ahead + [from_ahead(ahead[0], 1), from_ahead(behind[1], 3)] + behind
+    grad_first, msg, grad_gain_two, grad_bias_two, low_first = uncombine(
+        grad_normed, mix, first, weights, grad_out_one[0], w_out, gain_two
     )
     far = swap_seq(msg)
-    keep_feed, give_feed = feed(normed_two, grad_rows, hid0, pre0, normed_far, [grads1, grads2, grads3], w_up, w_down)
-    part_out = pair(keep_mix, swap_cores(give_mix), low_first, swap_cores(low_first))
-    part_feed = add_low(keep_feed, swap_cores(give_feed))
-    far, part_feed, part_out = lax.optimization_barrier((far, part_feed, part_out))
-    near_feed = swap_chips(jnp.concatenate([part_feed, part_out], axis=2))
-
+    keep_feed, give_feed = feed(
+        normed_two, grad_out_two[0], hid, pre0, normed_far, [lowg1, grads2, topg3], w_up, w_down
+    )
+    part_out = pair(keep_mix, swap_cores(give_mix), low_first, swap_cores(low_first)).reshape(-1, 4, 8, width)
+    far, keep_feed, give_feed, part_out = lax.optimization_barrier((far, keep_feed, give_feed, part_out))
+    came_feed = swap_cores(give_feed)
     keep_v, give_v, grad_dots = back_value(order, far, vals, probs)
     keep_q, give_q = back_query(order, grad_dots, queries, keys)
+    part_feed = add_low(keep_feed, came_feed)
+    near_feed = part_feed.reshape(-1, part_feed.shape[2])
+    for groups in (along_x(), along_y()):
+        near_feed = lax.psum_scatter(near_feed, "seq", tiled=True, axis_index_groups=groups)
+    part_out = tied(part_out, keep_q)
+    blocks = [
+        from_ahead(lax.dynamic_index_in_dim(part_out, (ffn + 4 - k) % 4, 1, keepdims=False), k) for k in (1, 2, 3)
+    ]
     came_v, came_q = swap_cores(give_v), swap_cores(give_q)
     back = swap_chips(jnp.concatenate([add_low(keep_q, came_q), add_low(keep_v, came_v)], axis=2))
+    back, blocks = lax.optimization_barrier((back, blocks))
+    sums_out = lax.dynamic_index_in_dim(part_out, ffn, 1, keepdims=False).astype(F32)
+    for block in blocks:
+        sums_out = sums_out + block.astype(F32)
+    sums_out = sums_out.astype(BF16).reshape(-1, 32, width // 4)
+    hid = tied(hid, keep_q)
+    two_low = down_out(hid, stream_two[0], w_down, far_weights)
     grads = sum_rounds(back)
     grads_other = swap_cores(grads)
-    near_feed = near_feed.astype(F32).sum(axis=0)
     grad_second, small = finish(
         grads, stream_two[0], gain_one, w_qk, w_value, grad_out_two[0], grad_gain_two, grad_bias_two
     )
-    part = pair(keep_rows, other_rows, grads, grads_other, small)
-    near = swap_chips(part).astype(F32).sum(axis=0)
-    near = jnp.concatenate([near, near_feed[:, 2048:]], axis=1).reshape(4, 8, -1)
+    part = pair(keep_rows, other_rows, grads, grads_other, small, sums_out)
+    near = swap_chips(part)
+    near, near_feed = lax.optimization_barrier((near, near_feed))
+    near = near.astype(F32).sum(axis=0)
+    near, near_out = near[:, : 2 * width + 128].reshape(4, 8, -1), near[:, 2 * width + 128 :]
     whole = lax.dynamic_index_in_dim(near, ffn, 0, keepdims=False)
     for k in (1, 2, 3):
         whole = whole + from_ahead(lax.dynamic_index_in_dim(near, (ffn + 4 - k) % 4, 0, keepdims=False), k)
-    small = whole[:, 2 * width : 2 * width + 128]
+    small = whole[:, 2 * width :]
     lines = small[:, :8] + swap_cores(small)[:, 8:16]
     lines = lines[:, 0::2] + lines[:, 1::2]
+    near_feed = near_feed.astype(F32)
     return (
         one_low[None],
         two_low[None],
@@ -850,7 +923,7 @@
         lines[:, 1],
         whole[:, :width],
         whole[:, width : 2 * width],
-        whole[:, 2 * width + 128 :],
+        near_out.reshape(8, width),
         lines[:, 2],
         lines[:, 3],
         near_feed[:, :1024],

time: 451 us -> 410 us (0.909)
  waiting for transfers between devices: 172 us -> 115 us
  between operations: 1.56 us -> 14.9 us
    all_to_all x4 -> x3, waiting for transfers between devices: 92 us -> 46.1 us  [swap_chips(): lax.all_to_all(array, 'seq', split_axis=0, concat_axis=0, tiled=True, axi...]
    all_to_all x2, waiting for transfers between devices: 18.4 us -> 0.01 us  [swap_seq(): return lax.all_to_all(array, 'seq', split_axis=0, concat_axis=0, tiled=True)]
    ppermute x15 -> x19, waiting for transfers between devices: 57.5 us -> 62.8 us  [from_ahead(): lax.ppermute(array, 'ffn', [((i + step) % count, i) for i in range(count)])]
    pallas_call x1 -> x3, Pallas kernels: 28.4 us -> 30.9 us  [the longest x1 16.6 us: middle(): pl.pallas_call(middle_kernel, out_shape=[sd((rows, width), F32), sd((4, r...]
    unnamed x60 -> x70, local copies, waits for them, and re-layouts: 10.6 us -> 8.82 us
    all_to_all x4 -> x3, starting transfers between devices: 20.7 us -> 19 us  [swap_chips(): lax.all_to_all(array, 'seq', split_axis=0, concat_axis=0, tiled=True, axi...]
    ppermute x15 -> x19, starting transfers between devices: 18.8 us -> 19.8 us  [from_ahead(): lax.ppermute(array, 'ffn', [((i + step) % count, i) for i in range(count)])]
  transfers between devices with their start and end apart: 36 -> 41, of which waited for: 13 -> 17; matrix products, arithmetic and copies ran while one was open for 5% -> 8% of each run, Pallas kernels for 24% -> 37%
where the time goes in v3:
time: 410 us; the launch traced here: 402 us
  Pallas kernels  161 us (39%)
  waiting for transfers between devices  115 us (28%)
  starting transfers between devices  70.2 us (17%)
  other arithmetic  27.9 us (7%)
  between operations  14.9 us (4%)
  local copies, waits for them, and re-layouts  13.2 us (3%)
    ppermute x19, waiting for transfers between devices, from_ahead(): lax.ppermute(array, 'ffn', [((i + step) % count, i) for i in range(count)])  62.8 us
    all_to_all x3, waiting for transfers between devices, swap_chips(): lax.all_to_all(array, 'seq', split_axis=0, concat_axis=0, tiled=True, axi...  46.1 us
    pallas_call x1, Pallas kernels, attend(): pl.pallas_call(attend_kernel, out_shape=[sd((length // 256, 256 + EXTRA,...  37.2 us
    pallas_call x1, Pallas kernels, back_value(): pl.pallas_call(back_value_kernel, out_shape=[sd((half, 256, DH), BF16)] *...  25.6 us
    pallas_call x1, Pallas kernels, feed(): pl.pallas_call(feed_kernel, out_shape=[sd((width // 64, 32, 2048), BF16)]...  21.7 us
    ppermute x19, starting transfers between devices, from_ahead(): lax.ppermute(array, 'ffn', [((i + step) % count, i) for i in range(count)])  19.8 us
    all_to_all x3, starting transfers between devices, swap_chips(): lax.all_to_all(array, 'seq', split_axis=0, concat_axis=0, tiled=True, axi...  19 us
    pallas_call x1, Pallas kernels, back_query(): pl.pallas_call(back_query_kernel, out_shape=[sd((half, 256, DH), BF16)] *...  16.9 us
  transfers between devices with their start and end apart: 41, of which 17 were waited for; matrix products, arithmetic and copies ran while one was open for 8% of the time, Pallas kernels for 37%

profile of v3, /device:TPU:1, one launch (start us, length us, event | category | flops | bytes accessed | tf_op | source)
XLA Modules:
  0.0 402.2 jit_solution(8188460262906972770)
XLA Ops:
  7.2 6.9 %project.1 = (bf16[16,256,256]{2,1,0:T(8,128)(2,1)}, bf16[256,1024]{1,0:T(8,128)(2,1)}, bf16[16,32,256]{2,1,0:T(8,128)(2,1)}, bf16[16,32,256]{2,1,0:T(8,128)(2,1)}) custom-call(bf16[256,1024]{1,0:T(8,128)(2,1)} %bitcast.60, f32[1,1024]{1,0:T(1,128)} %bitcast.72, f32[1,1024]{1,0:T(1,128)} %bitcast.74, bf16[1024,1024]{1,0:T(8,128)(2,1)} %w_qk.3, ...), custom_call_target="tpu_custom_call" | custom-call | bytes 24500000 | tf_op jit(solution)/shard_map/project/pallas_call | solution.py:89
  14.1 7.8 %all-to-all-start = ((bf16[16,256,256]{2,1,0:T(8,128)(2,1)}), bf16[16,256,256]{2,1,0:T(8,128)(2,1)}, u32[]{:S(2)}, u32[]{:S(2)}) async-start(bf16[16,256,256]{2,1,0:T(8,128)(2,1)} %get-tuple-element.89), calls=%async_computation | async-start | bytes 4194304 | tf_op jit(solution)/shard_map/all_to_all | solution.py:791
  21.9 3.1 slice_select_fusion
  25.0 3.8 collective-permute-start
  28.8 6.8 %sort.15 = (s32[8192]{0:T(1024)}, s32[8192]{0:T(1024)S(1)}) sort(s32[8192]{0:T(1024)S(1)} %iota_add_fusion, s32[8192]{0:T(1024)S(1)} %iota.6), dimensions={0}, to_apply=%region_0.1 | sort | flops 106496 | bytes 131072 | tf_op jit(solution)/shard_map/sort | solution.py:406
  36.4 4.5 %select_convert_fusion.bias = bf16[8192,128]{1,0:T(8,128)(2,1)} fusion(s32[8192]{0:T(1024)S(1)} %get-tuple-element.94.order, s32[8192]{0:T(1024)S(1)} %ge.20, s32[128,128]{1,0:T(8,128)S(1)} %pad_add_fusion), kind=kLoop, calls=%fused_computation.5 | loop fusion | flops 7340032 | bytes 2228224 | tf_op jit(solution)/shard_map/convert_element_type | solution.py:412
  41.0 9.6 %collective-permute-done.refs_4_.refs_3_ = bf16[512,1024]{1,0:T(8,128)(2,1)S(1)} collective-permute-done((bf16[512,1024]{1,0:T(8,128)(2,1)}, bf16[512,1024]{1,0:T(8,128)(2,1)S(1)}, u32[]{:S(2)}, u32[]{:S(2)}) %collective-permute-start) | collective-permute-done | bytes 1048608 | tf_op jit(solution)/shard_map/ppermute | solution.py:806
  50.5 3.1 collective-permute-done.1.refs_9_.refs_8_
  53.7 2.1 collective-permute-start.2
  55.7 3.6 pad_maximum_fusion.1
  59.3 2.6 collective-permute-start.3
  63.0 37.2 %attend.1 = (bf16[32,272,128]{2,1,0:T(8,128)(2,1)}, bf16[8192,128]{1,0:T(8,128)(2,1)}, bf16[8256,128]{1,0:T(8,128)(2,1)}, bf16[8256,128]{1,0:T(8,128)(2,1)}, bf16[8192,128]{1,0:T(8,128)(2,1)}) custom-call(s32[8192]{0:T(1024)} %copy-done.13, bf16[16,256,256]{2,1,0:T(8,128)(2,1)} %all-to-all-done.mine, bf16[16,256,256]{2,1,0:T(8,128)(2,1)} %collective-permute-done.2.other, ...), custom_call_target="tpu_custom_call" | custom-call | bytes 129500000 | tf_op jit(solution)/shard_map/attend/pallas_call | solution.py:222
  100.9 6.7 %all-to-all-start.1 = ((bf16[32,272,128]{2,1,0:T(8,128)(2,1)}), bf16[32,272,128]{2,1,0:T(8,128)(2,1)}, u32[]{:S(2)}, u32[]{:S(2)}) async-start(bf16[32,272,128]{2,1,0:T(8,128)(2,1)} %get-tuple-element.103), calls=%async_computation.1 | async-start | bytes 4456448 | tf_op jit(solution)/shard_map/all_to_all | solution.py:774
  108.2 1.6 collective-permute-start.8
  109.8 23.2 %collective-permute-done.8.refs_6_.refs_5_ = bf16[512,1024]{1,0:T(8,128)(2,1)S(1)} collective-permute-done((bf16[512,1024]{1,0:T(8,128)(2,1)}, bf16[512,1024]{1,0:T(8,128)(2,1)S(1)}, u32[]{:S(2)}, u32[]{:S(2)}) %collective-permute-start.8) | collective-permute-done | bytes 1048608 | tf_op jit(solution)/shard_map/ppermute | solution.py:806
  133.0 2.4 collective-permute-done.9.refs_7_.refs_6_
  135.3 1.0 copy-done.10
  136.3 1.2 copy-done.6
  137.5 1.9 collective-permute-start.12
  139.6 6.1 %combine.1 = (f32[256,1024]{1,0:T(8,128)}, f32[256,1024]{1,0:T(8,128)}, bf16[256,1024]{1,0:T(8,128)(2,1)}, bf16[256,1024]{1,0:T(8,128)(2,1)}, f32[256,128]{1,0:T...) custom-call(bf16[32,272,128]{2,1,0:T(8,128)(2,1)} %all-to-all-done.1, ...), custom_call_target="tpu_custom_call" | custom-call | bytes 21000000 | tf_op jit(solution)/shard_map/combine/pallas_call | solution.py:453
  145.7 2.6 collective-permute-start.14
  148.3 2.7 collective-permute-start.15
  151.5 16.6 %middle.1 = (f32[256,1024]{1,0:T(8,128)}, bf16[4,256,1024]{2,1,0:T(8,128)(2,1)}, bf16[256,1024]{1,0:T(8,128)(2,1)}) custom-call(bf16[256,1024]{1,0:T(8,128)(2,1)} %get-tuple-element.110.refs_0_.normed, bf16[256,1024]{1,0:T(8,128)(2,1)} %bitcast.56, bf16[1024,1024]{1,0:T(8,128)(2,1)} %refs_9_.1, bf16[1024,1024]{1,0:T(8,128)(2,1)} %refs_2_.3, ...), custom_call_target="tpu_custom_call" | custom-call | bytes 56000000 | tf_op jit(solution)/shard_map/middle/pallas_call | solution.py:542
  168.3 7.5 %uncombine.1 = (f32[256,1024]{1,0:T(8,128)}, bf16[32,272,128]{2,1,0:T(8,128)(2,1)}, f32[1,1024]{1,0:T(1,128)}, f32[1,1024]{1,0:T(1,128)}, bf16[256,1024]{1,0:T(8,128)(2,1)}) custom-call(f32[256,1024]{1,0:T(8,128)} %get-tuple-element.121.grad_normed, f32[256,1024]{1,0:T(8,128)} %get-tuple-element.122.mix, f32[256,1024]{1,0:T(8,128)} %get-tuple-element.123.first, ...), custom_call_target="tpu_custom_call" | custom-call | bytes 28000000 | tf_op jit(solution)/shard_map/uncombine/pallas_call | solution.py:592
  175.8 8.3 %all-to-all-start.2 = ((bf16[32,272,128]{2,1,0:T(8,128)(2,1)}), bf16[32,272,128]{2,1,0:T(8,128)(2,1)S(1)}, u32[]{:S(2)}, u32[]{:S(2)}) async-start(bf16[32,272,128]{2,1,0:T(8,128)(2,1)} %get-tuple-element.125), calls=%async_computation.2 | async-start | bytes 4456448 | tf_op jit(solution)/shard_map/all_to_all | solution.py:774
  184.5 2.9 collective-permute-start.19
  188.1 4.7 %collective-permute-done.19.refs_2_ = bf16[128,1024]{1,0:T(8,128)(2,1)S(1)} collective-permute-done((bf16[128,1024]{1,0:T(8,128)(2,1)S(1)}, bf16[128,1024]{1,0:T(8,128)(2,1)S(1)}, u32[]{:S(2)}, u32[]{:S(2)}) %collective-permute-start.19) | collective-permute-done | bytes 262176 | tf_op jit(solution)/shard_map/ppermute | solution.py:806
  192.9 3.1 collective-permute-done.20.refs_3_
  196.7 21.7 %feed.1 = (bf16[16,32,2048]{2,1,0:T(8,128)(2,1)}, bf16[16,32,2048]{2,1,0:T(8,128)(2,1)}) custom-call(bf16[256,1024]{1,0:T(8,128)(2,1)} %get-tuple-element.110.refs_0_.normed, bf16[256,1024]{1,0:T(8,128)(2,1)} %bitcast.57, bf16[4,256,1024]{2,1,0:T(8,128)(2,1)} %get-tuple-element.144.hid_own.refs_0_, bf16[256,1024]{1,0:T(8,128)(2,1)} %get-tuple-element.126.pre0, ...), custom_call_target="tpu_custom_call" | custom-call | bytes 70000000 | tf_op jit(solution)/shard_map/feed/pallas_call | solution.py:679
  219.3 3.1 pair.2
  222.4 1.4 collective-permute-start.29
  223.8 25.6 %back_value.1 = (bf16[16,256,128]{2,1,0:T(8,128)(2,1)}, bf16[16,256,128]{2,1,0:T(8,128)(2,1)}, bf16[8192,128]{1,0:T(8,128)(2,1)}) custom-call(s32[8192]{0:T(1024)} %copy-done.13, bf16[32,272,128]{2,1,0:T(8,128)(2,1)} %copy-done.3, bf16[8256,128]{1,0:T(8,128)(2,1)} %get-tuple-element.138.vals, bf16[8192,128]{1,0:T(8,128)(2,1)} %get-tuple-element.139.probs), custom_call_target="tpu_custom_call" | custom-call | bytes 91000000 | tf_op jit(solution)/shard_map/back_value/pallas_call | solution.py:314
  249.4 16.9 %back_query.1 = (bf16[16,256,128]{2,1,0:T(8,128)(2,1)}, bf16[16,256,128]{2,1,0:T(8,128)(2,1)}) custom-call(s32[8192]{0:T(1024)} %copy-done.13, bf16[8192,128]{1,0:T(8,128)(2,1)} %get-tuple-element.140.gd, bf16[8192,128]{1,0:T(8,128)(2,1)} %get-tuple-element.141.q_in, bf16[8256,128]{1,0:T(8,128)(2,1)} %get-tuple-element.142.keys), custom_call_target="tpu_custom_call" | custom-call | bytes 59500000 | tf_op jit(solution)/shard_map/back_query/pallas_call | solution.py:389
  266.4 1.3 collective-permute-start.23
  267.8 3.0 collective-permute-done.23
  270.8 1.5 add_convert_fusion.2
  272.6 1.6 pad_maximum_fusion
  274.3 6.8 %all-to-all-start.3 = ((bf16[16,256,256]{2,1,0:T(8,128)(2,1)}), bf16[16,256,256]{2,1,0:T(8,128)(2,1)S(1)}, u32[]{:S(2)}, u32[]{:S(2)}) async-start(bf16[16,256,256]{2,1,0:T(8,128)(2,1)} %pad_maximum_fusion), calls=%async_computation.3 | async-start | bytes 4194304 | tf_op jit(solution)/shard_map/all_to_all | solution.py:791
  281.2 4.5 %add_convert_fusion = bf16[16,32,2048]{2,1,0:T(8,128)(2,1)} fusion(bf16[16,32,2048]{2,1,0:T(8,128)(2,1)} %collective-permute-done.29, bf16[16,32,2048]{2,1,0:T(8,128)(2,1)} %get-tuple-element.161), kind=kLoop, calls=%fused_computation.4 | loop fusion | flops 4194304 | bytes 6291456 | tf_op jit(solution)/shard_map/convert_element_type | solution.py:814
  285.7 1.2 copy-done.12
  286.9 0.8 collective-permute-start.25
  287.7 0.8 collective-permute-start.27
  288.4 5.7 %collective-permute-done.25 = bf16[16,8,1024]{2,1,0:T(8,128)(2,1)S(1)} collective-permute-done((bf16[16,8,1024]{2,1,0:T(8,128)(2,1)S(1)}, bf16[16,8,1024]{2,1,0:T(8,128)(2,1)S(1)}, u32[]{:S(2)}, u32[]{:S(2)}) %collective-permute-start.25) | collective-permute-done | bytes 262176 | tf_op jit(solution)/shard_map/ppermute | solution.py:806
  294.2 1.9 collective-permute-done.26
  296.8 6.3 %collective-permute-done.27 = bf16[16,8,1024]{2,1,0:T(8,128)(2,1)} collective-permute-done((bf16[16,8,1024]{2,1,0:T(8,128)(2,1)S(1)}, bf16[16,8,1024]{2,1,0:T(8,128)(2,1)}, u32[]{:S(2)}, u32[]{:S(2)}) %collective-permute-start.27) | collective-permute-done | bytes 262176 | tf_op jit(solution)/shard_map/ppermute | solution.py:806
  303.1 15.0 %all-to-all-done.3.back = bf16[16,256,256]{2,1,0:T(8,128)(2,1)S(1)} async-done(((bf16[16,256,256]{2,1,0:T(8,128)(2,1)}), bf16[16,256,256]{2,1,0:T(8,128)(2,1)S(1)}, u32[]{:S(2)}, u32[]{:S(2)}) %all-to-all-start.3) | async-done | bytes 2097184 | tf_op jit(solution)/shard_map/all_to_all | solution.py:791
  318.1 1.4 copy-done.4
  319.5 2.9 sum_rounds.1.grads.right
  322.4 3.9 collective-permute-start.28
  326.2 1.2 fusion.3
  327.4 0.9 reshape.113.rest_1_
  328.3 5.7 %finish.1 = (f32[256,1024]{1,0:T(8,128)}, bf16[16,32,128]{2,1,0:T(8,128)(2,1)}) custom-call(bf16[256,2048]{1,0:T(8,128)(2,1)} %sum_rounds.1.grads.right, bf16[256,1024]{1,0:T(8,128)(2,1)} %bitcast.61, f32[1,1024]{1,0:T(1,128)} %bitcast.73, bf16[1024,1024]{1,0:T(8,128)(2,1)} %w_qk.3, bf16[1024,1024]{1,0:T(8,128)(2,1)} %w_value.3, bf16[256,1024]{1,0:T(8,128)(2,1)} %bitcast.58, ...), custom_call_target="tpu_custom_call" | custom-call | bytes 17500000 | tf_op jit(solution)/shard_map/finish/pallas_call | solution.py:736
  334.0 1.0 copy-done.15
  335.0 4.5 %pair.3 = bf16[16,32,2432]{2,1,0:T(8,128)(2,1)} custom-call(bf16[16,32,256]{2,1,0:T(8,128)(2,1)} %get-tuple-element.155.left, bf16[16,32,256]{2,1,0:T(8,128)(2,1)} %copy-done.30, bf16[256,2048]{1,0:T(8,128)(2,1)} %sum_rounds.1.grads.right, bf16[256,2048]{1,0:T(8,128)(2,1)} %copy-done.15, bf16[16,32,128]{2,1,0:T(8,128)(2,1)} %get-tuple-element.157.rest_0_, ...), custom_call_target="tpu_custom_call" | custom-call | bytes 10500000 | tf_op jit(solution)/shard_map/pair/pallas_call | solution.py:762
  339.5 4.4 %all-to-all-start.4 = ((bf16[16,32,2432]{2,1,0:T(8,128)(2,1)}), bf16[16,32,2432]{2,1,0:T(8,128)(2,1)S(1)}, u32[]{:S(2)}, u32[]{:S(2)}) async-start(bf16[16,32,2432]{2,1,0:T(8,128)(2,1)} %pair.3), calls=%async_computation.4 | async-start | bytes 4980736 | tf_op jit(solution)/shard_map/all_to_all | solution.py:791
  344.7 6.8 %down_out.1 = bf16[256,1024]{1,0:T(8,128)(2,1)} custom-call(bf16[4,256,1024]{2,1,0:T(8,128)(2,1)} %get-tuple-element.144.hid_own.refs_0_, bf16[256,1024]{1,0:T(8,128)(2,1)} %bitcast.62, bf16[1024,1024]{1,0:T(8,128)(2,1)} %refs_2_.3, bf16[512,1024]{1,0:T(8,128)(2,1)} %copy-done.7, bf16[768,1024]{1,0:T(8,128)(2,1)} %copy-done.2, bf16[512,1024]{1,0:T(8,128)(2,1)} %copy-done.9, ...), custom_call_target="tpu_custom_call" | custom-call | bytes 21000000 | tf_op jit(solution)/shard_map/down_out/pallas_call | solution.py:622
  351.5 31.2 %all-to-all-done.4 = bf16[16,32,2432]{2,1,0:T(8,128)(2,1)S(1)} async-done(((bf16[16,32,2432]{2,1,0:T(8,128)(2,1)}), bf16[16,32,2432]{2,1,0:T(8,128)(2,1)S(1)}, u32[]{:S(2)}, u32[]{:S(2)}) %all-to-all-start.4) | async-done | bytes 2490400 | tf_op jit(solution)/shard_map/all_to_all | solution.py:791
  382.6 1.8 reduce-scatter.5.cloned.1.call-done
  385.0 1.4 collective-permute-start.32
  386.4 0.7 fusion.6
  388.1 1.6 collective-permute-done.31
  389.7 0.8 collective-permute-done.32
  390.5 2.9 collective-permute-start.33
  394.4 0.7 slice_reduce_fusion
  (140 shorter events, 11.1 us)
Async XLA Ops:
  14.1 7.8 %copy-start = (bf16[1024,1024]{1,0:T(8,128)(2,1)S(1)}, bf16[1024,1024]{1,0:T(8,128)(2,1)}, u32[]{:S(2)}) copy-start(bf16[1024,1024]{1,0:T(8,128)(2,1)} %refs_2_.3) | copy-start | bytes 6291460
  14.1 39.6 %all-to-all-start = ((bf16[16,256,256]{2,1,0:T(8,128)(2,1)}), bf16[16,256,256]{2,1,0:T(8,128)(2,1)}, u32[]{:S(2)}, u32[]{:S(2)}) async-start(bf16[16,256,256]{2,1,0:T(8,128)(2,1)} %get-tuple-element.89), calls=%async_computation | async-start | bytes 4194304 | tf_op jit(solution)/shard_map/all_to_all | solution.py:791
  21.9 6.9 %copy-start.31 = (s32[1,1,8192]{2,1,0:T(1,128)S(1)}, s32[1,1,8192]{2,1,0:T(1,128)}, u32[]{:S(2)}) copy-start(s32[1,1,8192]{2,1,0:T(1,128)} %param.18) | copy-start | bytes 98308
  21.9 13.9 %copy-start.34 = (s32[1,9]{1,0:T(1,128)S(1)}, s32[1,9]{1,0:T(1,128)}, u32[]{:S(2)}) copy-start(s32[1,9]{1,0:T(1,128)} %param.17) | copy-start | bytes 112
  25.0 30.8 %copy-start.5 = (bf16[1,256,1024]{2,1,0:T(8,128)(2,1)S(1)}, bf16[1,256,1024]{2,1,0:T(8,128)(2,1)}, u32[]{:S(2)}) copy-start(bf16[1,256,1024]{2,1,0:T(8,128)(2,1)} %param.29) | copy-start | bytes 1572868
  25.0 25.6 %collective-permute-start = (bf16[512,1024]{1,0:T(8,128)(2,1)}, bf16[512,1024]{1,0:T(8,128)(2,1)S(1)}, u32[]{:S(2)}, u32[]{:S(2)}) collective-permute-start(bf16[512,1024]{1,0:T(8,128)(2,1)} %get-tuple-element.101), channel_id=1, source_target_pairs={{1,0},{2,1},{3,2},{0,3},{5,4},{6,5},{7,6},{4,7},{9,8},{10,9},{11,1... | collective-permute-start | bytes 3145736 | tf_op jit(solution)/shard_map/ppermute | solution.py:806
  28.7 24.9 %collective-permute-start.1 = (bf16[512,1024]{1,0:T(8,128)(2,1)}, bf16[512,1024]{1,0:T(8,128)(2,1)S(1)}, u32[]{:S(2)}, u32[]{:S(2)}) collective-permute-start(bf16[512,1024]{1,0:T(8,128)(2,1)} %get-tuple-element.100), channel_id=1, source_target_pairs={{3,0},{0,1},{1,2},{2,3},{7,4},{4,5},{5,6},{6,7},{11,8},{8,9},{9,10... | collective-permute-start | bytes 3145736 | tf_op jit(solution)/shard_map/ppermute | solution.py:806
  35.5 23.8 %copy-start.13 = (s32[8192]{0:T(1024)}, s32[8192]{0:T(1024)S(1)}, u32[]{:S(2)}) copy-start(s32[8192]{0:T(1024)S(1)} %get-tuple-element.94.order) | copy-start | bytes 98308
  50.5 8.8 %copy-start.7 = (bf16[512,1024]{1,0:T(8,128)(2,1)}, bf16[512,1024]{1,0:T(8,128)(2,1)S(1)}, u32[]{:S(2)}) copy-start(bf16[512,1024]{1,0:T(8,128)(2,1)S(1)} %collective-permute-done.refs_4_.refs_3_) | copy-start | bytes 3145732
  53.7 5.7 %copy-start.8 = (bf16[512,1024]{1,0:T(8,128)(2,1)}, bf16[512,1024]{1,0:T(8,128)(2,1)S(1)}, u32[]{:S(2)}) copy-start(bf16[512,1024]{1,0:T(8,128)(2,1)S(1)} %collective-permute-done.1.refs_9_.refs_8_) | copy-start | bytes 3145732
  53.7 8.8 %collective-permute-start.2 = (bf16[16,256,256]{2,1,0:T(8,128)(2,1)}, bf16[16,256,256]{2,1,0:T(8,128)(2,1)}, u32[]{:S(2)}, u32[]{:S(2)}) collective-permute-start(bf16[16,256,256]{2,1,0:T(8,128)(2,1)} %all-to-all-done.mine), channel_id=1, source_target_pairs={{0,4},{4,0},{8,12},{12,8},{16,20},{20,16},{24,28},{28,24},{32,36},... | collective-permute-start | bytes 6291464 | tf_op jit(solution)/shard_map/ppermute | solution.py:797
  55.7 6.7 %copy-start.33 = (bf16[16,32,256]{2,1,0:T(8,128)(2,1)S(1)}, bf16[16,32,256]{2,1,0:T(8,128)(2,1)}, u32[]{:S(2)}) copy-start(bf16[16,32,256]{2,1,0:T(8,128)(2,1)} %get-tuple-element.102) | copy-start | bytes 786436
  59.3 40.9 %collective-permute-start.3 = (bf16[768,1024]{1,0:T(8,128)(2,1)}, bf16[768,1024]{1,0:T(8,128)(2,1)S(1)}, u32[]{:S(2)}, u32[]{:S(2)}) collective-permute-start(bf16[768,1024]{1,0:T(8,128)(2,1)} %get-tuple-element.175), channel_id=1, source_target_pairs={{1,0},{2,1},{3,2},{0,3},{5,4},{6,5},{7,6},{4,7},{9,8},{10,9},{11,1... | collective-permute-start | bytes 4718600 | tf_op jit(solution)/shard_map/ppermute | solution.py:806
  61.9 38.3 %collective-permute-start.4 = (bf16[768,1024]{1,0:T(8,128)(2,1)}, bf16[768,1024]{1,0:T(8,128)(2,1)S(1)}, u32[]{:S(2)}, u32[]{:S(2)}) collective-permute-start(bf16[768,1024]{1,0:T(8,128)(2,1)} %get-tuple-element.174), channel_id=1, source_target_pairs={{3,0},{0,1},{1,2},{2,3},{7,4},{4,5},{5,6},{6,7},{11,8},{8,9},{9,10... | collective-permute-start | bytes 4718600 | tf_op jit(solution)/shard_map/ppermute | solution.py:806
  61.9 38.3 %collective-permute-start.5 = (bf16[512,1024]{1,0:T(8,128)(2,1)}, bf16[512,1024]{1,0:T(8,128)(2,1)}, u32[]{:S(2)}, u32[]{:S(2)}) collective-permute-start(bf16[512,1024]{1,0:T(8,128)(2,1)} %copy-done.7), channel_id=1, source_target_pairs={{0,4},{4,0},{8,12},{12,8},{16,20},{20,16},{24,28},{28,24},{32,36},... | collective-permute-start | bytes 3145736 | tf_op jit(solution)/shard_map/ppermute | solution.py:797
  62.2 38.0 %collective-permute-start.6 = (bf16[512,1024]{1,0:T(8,128)(2,1)}, bf16[512,1024]{1,0:T(8,128)(2,1)}, u32[]{:S(2)}, u32[]{:S(2)}) collective-permute-start(bf16[512,1024]{1,0:T(8,128)(2,1)} %copy-done.8), channel_id=1, source_target_pairs={{0,4},{4,0},{8,12},{12,8},{16,20},{20,16},{24,28},{28,24},{32,36},... | collective-permute-start | bytes 3145736 | tf_op jit(solution)/shard_map/ppermute | solution.py:797
  62.5 37.7 %collective-permute-start.7 = (bf16[16,32,256]{2,1,0:T(8,128)(2,1)S(1)}, bf16[16,32,256]{2,1,0:T(8,128)(2,1)S(1)}, u32[]{:S(2)}, u32[]{:S(2)}) collective-permute-start(bf16[16,32,256]{2,1,0:T(8,128)(2,1)S(1)} %copy-done.33), channel_id=1, source_target_pairs={{0,4},{4,0},{8,12},{12,8},{16,20},{20,16},{24,28},{28,24},{32,36},... | collective-permute-start | bytes 786440 | tf_op jit(solution)/shard_map/ppermute | solution.py:797
  100.2 7.3 %copy-start.2 = (bf16[768,1024]{1,0:T(8,128)(2,1)}, bf16[768,1024]{1,0:T(8,128)(2,1)S(1)}, u32[]{:S(2)}) copy-start(bf16[768,1024]{1,0:T(8,128)(2,1)S(1)} %collective-permute-done.3.refs_5_.refs_6_.refs_4_) | copy-start | bytes 4718596
  100.9 38.5 %copy-start.1 = (bf16[768,1024]{1,0:T(8,128)(2,1)}, bf16[768,1024]{1,0:T(8,128)(2,1)S(1)}, u32[]{:S(2)}) copy-start(bf16[768,1024]{1,0:T(8,128)(2,1)S(1)} %collective-permute-done.4.refs_8_.refs_7_) | copy-start | bytes 4718596
  100.9 36.6 %all-to-all-start.1 = ((bf16[32,272,128]{2,1,0:T(8,128)(2,1)}), bf16[32,272,128]{2,1,0:T(8,128)(2,1)}, u32[]{:S(2)}, u32[]{:S(2)}) async-start(bf16[32,272,128]{2,1,0:T(8,128)(2,1)} %get-tuple-element.103), calls=%async_computation.1 | async-start | bytes 4456448 | tf_op jit(solution)/shard_map/all_to_all | solution.py:774
  107.6 27.7 %collective-permute-start.10 = (bf16[768,1024]{1,0:T(8,128)(2,1)S(1)}, bf16[768,1024]{1,0:T(8,128)(2,1)S(1)}, u32[]{:S(2)}, u32[]{:S(2)}) collective-permute-start(bf16[768,1024]{1,0:T(8,128)(2,1)S(1)} %collective-permute-done.3.refs_5_.refs_6_.refs_4_), channel_id=1, source_target_pairs={{0,4},{4,0},{8,12},{12,8},{16,20},{20,16},{24,28},{28,24},{32,36},... | collective-permute-start | bytes 4718600 | tf_op jit(solution)/shard_map/ppermute | solution.py:797
  108.0 29.6 %collective-permute-start.11 = (bf16[768,1024]{1,0:T(8,128)(2,1)S(1)}, bf16[768,1024]{1,0:T(8,128)(2,1)}, u32[]{:S(2)}, u32[]{:S(2)}) collective-permute-start(bf16[768,1024]{1,0:T(8,128)(2,1)S(1)} %collective-permute-done.4.refs_8_.refs_7_), channel_id=1, source_target_pairs={{0,4},{4,0},{8,12},{12,8},{16,20},{20,16},{24,28},{28,24},{32,36},... | collective-permute-start | bytes 4718600 | tf_op jit(solution)/shard_map/ppermute | solution.py:797
  108.2 24.8 %collective-permute-start.8 = (bf16[512,1024]{1,0:T(8,128)(2,1)}, bf16[512,1024]{1,0:T(8,128)(2,1)S(1)}, u32[]{:S(2)}, u32[]{:S(2)}) collective-permute-start(bf16[512,1024]{1,0:T(8,128)(2,1)} %copy-done.7), channel_id=1, source_target_pairs={{1,0},{2,1},{3,2},{0,3},{5,4},{6,5},{7,6},{4,7},{9,8},{10,9},{11,1... | collective-permute-start | bytes 3145736 | tf_op jit(solution)/shard_map/ppermute | solution.py:806
  109.8 25.6 %collective-permute-start.9 = (bf16[512,1024]{1,0:T(8,128)(2,1)}, bf16[512,1024]{1,0:T(8,128)(2,1)S(1)}, u32[]{:S(2)}, u32[]{:S(2)}) collective-permute-start(bf16[512,1024]{1,0:T(8,128)(2,1)} %copy-done.8), channel_id=1, source_target_pairs={{3,0},{0,1},{1,2},{2,3},{7,4},{4,5},{5,6},{6,7},{11,8},{8,9},{9,10... | collective-permute-start | bytes 3145736 | tf_op jit(solution)/shard_map/ppermute | solution.py:806
  133.0 2.4 copy-start.9
  137.5 10.8 %collective-permute-start.12 = (bf16[512,1024]{1,0:T(8,128)(2,1)}, bf16[512,1024]{1,0:T(8,128)(2,1)S(1)}, u32[]{:S(2)}, u32[]{:S(2)}) collective-permute-start(bf16[512,1024]{1,0:T(8,128)(2,1)} %copy-done.9), channel_id=1, source_target_pairs={{0,4},{4,0},{8,12},{12,8},{16,20},{20,16},{24,28},{28,24},{32,36},... | collective-permute-start | bytes 3145736 | tf_op jit(solution)/shard_map/ppermute | solution.py:797
  139.4 11.6 %collective-permute-start.13 = (bf16[512,1024]{1,0:T(8,128)(2,1)}, bf16[512,1024]{1,0:T(8,128)(2,1)}, u32[]{:S(2)}, u32[]{:S(2)}) collective-permute-start(bf16[512,1024]{1,0:T(8,128)(2,1)} %copy-done.10), channel_id=1, source_target_pairs={{0,4},{4,0},{8,12},{12,8},{16,20},{20,16},{24,28},{28,24},{32,36},... | collective-permute-start | bytes 3145736 | tf_op jit(solution)/shard_map/ppermute | solution.py:797
  139.5 28.7 %collective-permute-start.18 = (bf16[256,1024]{1,0:T(8,128)(2,1)S(1)}, bf16[256,1024]{1,0:T(8,128)(2,1)S(1)}, u32[]{:S(2)}, u32[]{:S(2)}) collective-permute-start(bf16[256,1024]{1,0:T(8,128)(2,1)S(1)} %slice.91), channel_id=1, source_target_pairs={{3,0},{0,1},{1,2},{2,3},{7,4},{4,5},{5,6},{6,7},{11,8},{8,9},{9,10... | collective-permute-start | bytes 1572872 | tf_op jit(solution)/shard_map/ppermute | solution.py:806
  145.7 22.5 %collective-permute-start.14 = (bf16[128,1024]{1,0:T(8,128)(2,1)}, bf16[128,1024]{1,0:T(8,128)(2,1)S(1)}, u32[]{:S(2)}, u32[]{:S(2)}) collective-permute-start(bf16[128,1024]{1,0:T(8,128)(2,1)} %get-tuple-element.119), channel_id=1, source_target_pairs={{1,0},{2,1},{3,2},{0,3},{5,4},{6,5},{7,6},{4,7},{9,8},{10,9},{11,1... | collective-permute-start | bytes 786440 | tf_op jit(solution)/shard_map/ppermute | solution.py:806
  148.3 19.9 %collective-permute-start.16 = (bf16[128,1024]{1,0:T(8,128)(2,1)}, bf16[128,1024]{1,0:T(8,128)(2,1)S(1)}, u32[]{:S(2)}, u32[]{:S(2)}) collective-permute-start(bf16[128,1024]{1,0:T(8,128)(2,1)} %get-tuple-element.119), channel_id=1, source_target_pairs={{3,0},{0,1},{1,2},{2,3},{7,4},{4,5},{5,6},{6,7},{11,8},{8,9},{9,10... | collective-permute-start | bytes 786440 | tf_op jit(solution)/shard_map/ppermute | solution.py:806
  148.3 3.2 copy-start.11
  148.3 19.8 %collective-permute-start.15 = (bf16[128,1024]{1,0:T(8,128)(2,1)}, bf16[128,1024]{1,0:T(8,128)(2,1)S(1)}, u32[]{:S(2)}, u32[]{:S(2)}) collective-permute-start(bf16[128,1024]{1,0:T(8,128)(2,1)} %get-tuple-element.120), channel_id=1, source_target_pairs={{1,0},{2,1},{3,2},{0,3},{5,4},{6,5},{7,6},{4,7},{9,8},{10,9},{11,1... | collective-permute-start | bytes 786440 | tf_op jit(solution)/shard_map/ppermute | solution.py:806
  151.0 17.2 %collective-permute-start.17 = (bf16[128,1024]{1,0:T(8,128)(2,1)}, bf16[128,1024]{1,0:T(8,128)(2,1)S(1)}, u32[]{:S(2)}, u32[]{:S(2)}) collective-permute-start(bf16[128,1024]{1,0:T(8,128)(2,1)} %get-tuple-element.120), channel_id=1, source_target_pairs={{3,0},{0,1},{1,2},{2,3},{7,4},{4,5},{5,6},{6,7},{11,8},{8,9},{9,10... | collective-permute-start | bytes 786440 | tf_op jit(solution)/shard_map/ppermute | solution.py:806
  168.2 7.6 %copy-start.16 = (bf16[256,1024]{1,0:T(8,128)(2,1)}, bf16[256,1024]{1,0:T(8,128)(2,1)S(1)}, u32[]{:S(2)}) copy-start(bf16[256,1024]{1,0:T(8,128)(2,1)S(1)} %collective-permute-done.18.refs_7_) | copy-start | bytes 1572868
  168.2 7.6 %copy-start.20 = (bf16[128,1024]{1,0:T(8,128)(2,1)}, bf16[128,1024]{1,0:T(8,128)(2,1)S(1)}, u32[]{:S(2)}) copy-start(bf16[128,1024]{1,0:T(8,128)(2,1)S(1)} %collective-permute-done.14.refs_0_) | copy-start | bytes 786436
  168.2 7.6 %copy-start.23 = (bf16[128,1024]{1,0:T(8,128)(2,1)}, bf16[128,1024]{1,0:T(8,128)(2,1)S(1)}, u32[]{:S(2)}) copy-start(bf16[128,1024]{1,0:T(8,128)(2,1)S(1)} %collective-permute-done.15.refs_1_) | copy-start | bytes 786436
  168.2 7.6 %copy-start.22 = (bf16[128,1024]{1,0:T(8,128)(2,1)}, bf16[128,1024]{1,0:T(8,128)(2,1)S(1)}, u32[]{:S(2)}) copy-start(bf16[128,1024]{1,0:T(8,128)(2,1)S(1)} %collective-permute-done.16.refs_4_) | copy-start | bytes 786436
  168.2 7.6 %copy-start.24 = (bf16[128,1024]{1,0:T(8,128)(2,1)}, bf16[128,1024]{1,0:T(8,128)(2,1)S(1)}, u32[]{:S(2)}) copy-start(bf16[128,1024]{1,0:T(8,128)(2,1)S(1)} %collective-permute-done.17.refs_5_) | copy-start | bytes 786436
  175.8 8.4 %copy-start.17 = (bf16[256,1024]{1,0:T(8,128)(2,1)S(1)}, bf16[256,1024]{1,0:T(8,128)(2,1)}, u32[]{:S(2)}) copy-start(bf16[256,1024]{1,0:T(8,128)(2,1)} %get-tuple-element.136.right) | copy-start | bytes 1572868
  175.8 8.7 %copy-start.21 = (bf16[128,1024]{1,0:T(8,128)(2,1)S(1)}, bf16[128,1024]{1,0:T(8,128)(2,1)}, u32[]{:S(2)}) copy-start(bf16[128,1024]{1,0:T(8,128)(2,1)} %copy-done.20) | copy-start | bytes 786436
  175.8 11.6 %copy-start.25 = (bf16[128,1024]{1,0:T(8,128)(2,1)S(1)}, bf16[128,1024]{1,0:T(8,128)(2,1)}, u32[]{:S(2)}) copy-start(bf16[128,1024]{1,0:T(8,128)(2,1)} %copy-done.24) | copy-start | bytes 786436
  175.8 46.5 %all-to-all-start.2 = ((bf16[32,272,128]{2,1,0:T(8,128)(2,1)}), bf16[32,272,128]{2,1,0:T(8,128)(2,1)S(1)}, u32[]{:S(2)}, u32[]{:S(2)}) async-start(bf16[32,272,128]{2,1,0:T(8,128)(2,1)} %get-tuple-element.125), calls=%async_computation.2 | async-start | bytes 4456448 | tf_op jit(solution)/shard_map/all_to_all | solution.py:774
  184.2 34.2 %collective-permute-start.22 = (bf16[256,1024]{1,0:T(8,128)(2,1)S(1)}, bf16[256,1024]{1,0:T(8,128)(2,1)S(1)}, u32[]{:S(2)}, u32[]{:S(2)}) collective-permute-start(bf16[256,1024]{1,0:T(8,128)(2,1)S(1)} %copy-done.17), channel_id=1, source_target_pairs={{0,4},{4,0},{8,12},{12,8},{16,20},{20,16},{24,28},{28,24},{32,36},... | collective-permute-start | bytes 1572872 | tf_op jit(solution)/shard_map/ppermute | solution.py:797
  184.5 8.3 %collective-permute-start.19 = (bf16[128,1024]{1,0:T(8,128)(2,1)S(1)}, bf16[128,1024]{1,0:T(8,128)(2,1)S(1)}, u32[]{:S(2)}, u32[]{:S(2)}) collective-permute-start(bf16[128,1024]{1,0:T(8,128)(2,1)S(1)} %copy-done.21), channel_id=1, source_target_pairs={{1,0},{2,1},{3,2},{0,3},{5,4},{6,5},{7,6},{4,7},{9,8},{10,9},{11,1... | collective-permute-start | bytes 786440 | tf_op jit(solution)/shard_map/ppermute | solution.py:806
  187.4 8.5 %collective-permute-start.20 = (bf16[128,1024]{1,0:T(8,128)(2,1)S(1)}, bf16[128,1024]{1,0:T(8,128)(2,1)S(1)}, u32[]{:S(2)}, u32[]{:S(2)}) collective-permute-start(bf16[128,1024]{1,0:T(8,128)(2,1)S(1)} %copy-done.25), channel_id=1, source_target_pairs={{3,0},{0,1},{1,2},{2,3},{7,4},{4,5},{5,6},{6,7},{11,8},{8,9},{9,10... | collective-permute-start | bytes 786440 | tf_op jit(solution)/shard_map/ppermute | solution.py:806
  187.4 30.9 %collective-permute-start.21 = (bf16[16,32,256]{2,1,0:T(8,128)(2,1)}, bf16[16,32,256]{2,1,0:T(8,128)(2,1)S(1)}, u32[]{:S(2)}, u32[]{:S(2)}) collective-permute-start(bf16[16,32,256]{2,1,0:T(8,128)(2,1)} %get-tuple-element.135), channel_id=1, source_target_pairs={{0,4},{4,0},{8,12},{12,8},{16,20},{20,16},{24,28},{28,24},{32,36},... | collective-permute-start | bytes 786440 | tf_op jit(solution)/shard_map/ppermute | solution.py:797
  192.9 3.1 copy-start.28
  222.4 58.8 %collective-permute-start.29 = (bf16[16,32,2048]{2,1,0:T(8,128)(2,1)}, bf16[16,32,2048]{2,1,0:T(8,128)(2,1)}, u32[]{:S(2)}, u32[]{:S(2)}) collective-permute-start(bf16[16,32,2048]{2,1,0:T(8,128)(2,1)} %get-tuple-element.162), channel_id=1, source_target_pairs={{0,4},{4,0},{8,12},{12,8},{16,20},{20,16},{24,28},{28,24},{32,36},... | collective-permute-start | bytes 6291464 | tf_op jit(solution)/shard_map/ppermute | solution.py:797
  249.4 18.3 %copy-start.32 = (bf16[16,256,128]{2,1,0:T(8,128)(2,1)S(1)}, bf16[16,256,128]{2,1,0:T(8,128)(2,1)}, u32[]{:S(2)}) copy-start(bf16[16,256,128]{2,1,0:T(8,128)(2,1)} %get-tuple-element.148) | copy-start | bytes 3145732
  266.4 6.0 %copy-start.14 = (bf16[16,256,128]{2,1,0:T(8,128)(2,1)S(1)}, bf16[16,256,128]{2,1,0:T(8,128)(2,1)}, u32[]{:S(2)}) copy-start(bf16[16,256,128]{2,1,0:T(8,128)(2,1)} %get-tuple-element.147) | copy-start | bytes 3145732
  266.4 4.5 %collective-permute-start.23 = (bf16[16,256,128]{2,1,0:T(8,128)(2,1)}, bf16[16,256,128]{2,1,0:T(8,128)(2,1)S(1)}, u32[]{:S(2)}, u32[]{:S(2)}) collective-permute-start(bf16[16,256,128]{2,1,0:T(8,128)(2,1)} %get-tuple-element.146), channel_id=1, source_target_pairs={{0,4},{4,0},{8,12},{12,8},{16,20},{20,16},{24,28},{28,24},{32,36},... | collective-permute-start | bytes 3145736 | tf_op jit(solution)/shard_map/ppermute | solution.py:797
  267.7 4.6 %collective-permute-start.24 = (bf16[16,256,128]{2,1,0:T(8,128)(2,1)S(1)}, bf16[16,256,128]{2,1,0:T(8,128)(2,1)S(1)}, u32[]{:S(2)}, u32[]{:S(2)}) collective-permute-start(bf16[16,256,128]{2,1,0:T(8,128)(2,1)S(1)} %copy-done.32), channel_id=1, source_target_pairs={{0,4},{4,0},{8,12},{12,8},{16,20},{20,16},{24,28},{28,24},{32,36},... | collective-permute-start | bytes 3145736 | tf_op jit(solution)/shard_map/ppermute | solution.py:797
  274.3 43.8 %all-to-all-start.3 = ((bf16[16,256,256]{2,1,0:T(8,128)(2,1)}), bf16[16,256,256]{2,1,0:T(8,128)(2,1)S(1)}, u32[]{:S(2)}, u32[]{:S(2)}) async-start(bf16[16,256,256]{2,1,0:T(8,128)(2,1)} %pad_maximum_fusion), calls=%async_computation.3 | async-start | bytes 4194304 | tf_op jit(solution)/shard_map/all_to_all | solution.py:791
  281.1 62.9 %reduce-scatter.3.cloned.1.call-start = ((), (), s32[]{:S(2)}) async-start(), calls=%async_computation.7 | async-start | bytes 2621440 | tf_op jit(solution)/shard_map/reduce_scatter | solution.py:886
  286.9 7.3 %collective-permute-start.25 = (bf16[16,8,1024]{2,1,0:T(8,128)(2,1)S(1)}, bf16[16,8,1024]{2,1,0:T(8,128)(2,1)S(1)}, u32[]{:S(2)}, u32[]{:S(2)}) collective-permute-start(bf16[16,8,1024]{2,1,0:T(8,128)(2,1)S(1)} %get-tuple-element.173), channel_id=1, source_target_pairs={{1,0},{2,1},{3,2},{0,3},{5,4},{6,5},{7,6},{4,7},{9,8},{10,9},{11,1... | collective-permute-start | bytes 786440 | tf_op jit(solution)/shard_map/ppermute | solution.py:806
  287.7 8.4 %collective-permute-start.26 = (bf16[16,8,1024]{2,1,0:T(8,128)(2,1)S(1)}, bf16[16,8,1024]{2,1,0:T(8,128)(2,1)S(1)}, u32[]{:S(2)}, u32[]{:S(2)}) collective-permute-start(bf16[16,8,1024]{2,1,0:T(8,128)(2,1)S(1)} %get-tuple-element.172), channel_id=1, source_target_pairs={{2,0},{3,1},{0,2},{1,3},{6,4},{7,5},{4,6},{5,7},{10,8},{11,9},{8,1... | collective-permute-start | bytes 786440 | tf_op jit(solution)/shard_map/ppermute | solution.py:806
  287.7 15.5 %collective-permute-start.27 = (bf16[16,8,1024]{2,1,0:T(8,128)(2,1)S(1)}, bf16[16,8,1024]{2,1,0:T(8,128)(2,1)}, u32[]{:S(2)}, u32[]{:S(2)}) collective-permute-start(bf16[16,8,1024]{2,1,0:T(8,128)(2,1)S(1)} %get-tuple-element.171), channel_id=1, source_target_pairs={{3,0},{0,1},{1,2},{2,3},{7,4},{4,5},{5,6},{6,7},{11,8},{8,9},{9,10... | collective-permute-start | bytes 786440 | tf_op jit(solution)/shard_map/ppermute | solution.py:806
  322.4 11.7 %collective-permute-start.28 = (bf16[256,2048]{1,0:T(8,128)(2,1)}, bf16[256,2048]{1,0:T(8,128)(2,1)S(1)}, u32[]{:S(2)}, u32[]{:S(2)}) collective-permute-start(bf16[256,2048]{1,0:T(8,128)(2,1)} %sum_rounds.1.grads.right), channel_id=1, source_target_pairs={{0,4},{4,0},{8,12},{12,8},{16,20},{20,16},{24,28},{28,24},{32,36},... | collective-permute-start | bytes 3145736 | tf_op jit(solution)/shard_map/ppermute | solution.py:797
  339.5 43.1 %all-to-all-start.4 = ((bf16[16,32,2432]{2,1,0:T(8,128)(2,1)}), bf16[16,32,2432]{2,1,0:T(8,128)(2,1)S(1)}, u32[]{:S(2)}, u32[]{:S(2)}) async-start(bf16[16,32,2432]{2,1,0:T(8,128)(2,1)} %pair.3), calls=%async_computation.4 | async-start | bytes 4980736 | tf_op jit(solution)/shard_map/all_to_all | solution.py:791
  343.9 40.5 %reduce-scatter.5.cloned.1.call-start = ((), (), s32[]{:S(2)}) async-start(), calls=%async_computation.8 | async-start | bytes 655360 | tf_op jit(solution)/shard_map/reduce_scatter | solution.py:886
  384.8 3.2 collective-permute-start.30
  384.9 4.7 %collective-permute-start.31 = (f32[8,2176]{1,0:T(8,128)S(1)}, f32[8,2176]{1,0:T(8,128)S(1)}, u32[]{:S(2)}, u32[]{:S(2)}) collective-permute-start(f32[8,2176]{1,0:T(8,128)S(1)} %get-tuple-element.178), channel_id=1, source_target_pairs={{2,0},{3,1},{0,2},{1,3},{6,4},{7,5},{4,6},{5,7},{10,8},{11,9},{8,1... | collective-permute-start | bytes 208904 | tf_op jit(solution)/shard_map/ppermute | solution.py:806
  385.0 5.4 %collective-permute-start.32 = (f32[8,2176]{1,0:T(8,128)S(1)}, f32[8,2176]{1,0:T(8,128)S(1)}, u32[]{:S(2)}, u32[]{:S(2)}) collective-permute-start(f32[8,2176]{1,0:T(8,128)S(1)} %get-tuple-element.177), channel_id=1, source_target_pairs={{3,0},{0,1},{1,2},{2,3},{7,4},{4,5},{5,6},{6,7},{11,8},{8,9},{9,10... | collective-permute-start | bytes 208904 | tf_op jit(solution)/shard_map/ppermute | solution.py:806
  390.5 3.7 collective-permute-start.33
  (12 other events, 12.9 us)
Sparse Core Ops, SparseCore 0:
  285.8 40.2 reduce-scatter.2
  347.3 37.1 reduce-scatter.4
